TPU v7x, 256 devices: a whole 4x4x8 slice. The times are simulated.
256 devices in a mesh: gx: 16 (over z, core), gy: 16 (over y, x).
Axes of the slice: x: 4, y: 4, z: 8, core: 2. Of those that a mesh axis runs over, the one named last changes fastest.
Arguments:
- leaf_map: float32 [16, 16, 512, 512], P('gx', 'gy'), may hold values from -0.97 to 0.97, as said below
- source_trace: float32 [16, 16, 512], P('gx', 'gy'), may hold values from -6 to 6
- tile_class: int32 [16, 16, 16], P('gx', 'gy'), may hold values from 0 to 7
- absorb_table: float32 [8], replicated, may hold values from 0.2 to 2
Outputs:
- top_map: float32 [16, 16, 192, 1536], P('gx', 'gy')
- top_out: float32 [16, 16, 192], P('gx', 'gy')
Inputs may be any that keep to these rules, and one draw needn't show every extreme that they name: `leaf_map`: each leaf map is a dense matrix whose largest singular value is at most 0.97.
All inputs are finite; a program needn't handle non-finite values.
Results may differ from a plain program's by a relative error of at most 0.000086.
Values sent between devices are 32-bit elements; how exact they have to be, the bound alone decides.
No kernel may reach another device: no remote copies, remote signals or barrier semaphores. Data moves between devices by JAX's collectives and lax.ppermute only.
A program may use at most 128 MiB of HBM per device.

v0:
```python
import math

import jax
import jax.numpy as jnp
from jax import lax
from jax.experimental import pallas as pl
from jax.experimental.pallas import tpu as pltpu
from jax.sharding import PartitionSpec as P

S = 128
f32 = jnp.float32
bf16 = jnp.bfloat16
HIGHEST = lax.Precision.HIGHEST


def roles():
    gx = lax.axis_index("gx")
    gy = lax.axis_index("gy")
    return gx % 2, gy % 2, (gx // 2) % 2


def at(offset, size, unit=S):
    return pl.ds(pl.multiple_of(offset * unit, unit), size)


def split(x):
    high = x.astype(bf16)
    return high, (x - high.astype(f32)).astype(bf16)


def mm(a, b):
    return jnp.dot(a, b, preferred_element_type=f32)


def dot3s(a, b):
    return mm(a[0], b[0]) + (mm(a[0], b[1]) + mm(a[1], b[0]))


def dot3(a, b):
    return dot3s(split(a), split(b))


def dot_full(a, b):
    return jnp.dot(a, b, precision=HIGHEST, preferred_element_type=f32)


def inverse(K):
    n = K.shape[0]
    rows = lax.broadcasted_iota(jnp.int32, (n, n), 0)
    cols = lax.broadcasted_iota(jnp.int32, (n, n), 1)
    eye = (rows == cols).astype(f32)
    ks = split(K)
    X = eye + K
    power = mm(ks[0], ks[0])
    steps = 6
    for j in range(1, steps + 1):
        pb = power.astype(bf16)
        if j < steps:
            both = mm(jnp.concatenate([X.astype(bf16), pb], 0), pb)
            X = X + both[:n]
            power = both[n:]
        else:
            X = X + mm(X.astype(bf16), pb)
    for _ in range(2):
        xs = split(X)
        residual = eye - X + dot3s(ks, xs)
        X = X + mm(xs[0], residual.astype(bf16))
    residual = eye - X + dot_full(K, X)
    return X + dot3(X, residual)


def as_columns(row):
    return jnp.broadcast_to(row, (S, S)).T


def as_rows(block):
    return block.T[:8]


def level1(own, oth, hown, hoth, m1, pii, xi, xe, r1, r2):
    c, s, r = roles()
    d = 1 - c
    P_ii = own[at(d, S), at(d, S)]
    Q_ii = oth[at(c, S), at(c, S)]
    P_ie = jnp.concatenate([own[at(d, S), at(c, S)], own[at(d, S), 2 * S :]], 1)
    Q_ie = jnp.concatenate([oth[at(c, S), at(d, S)], oth[at(c, S), 2 * S :]], 1)
    p_i = as_columns(hown[:, at(d, S)])
    q_i = as_columns(hoth[:, at(c, S)])
    Minv = inverse(dot_full(Q_ii, P_ii))
    U = dot3(Q_ii, jnp.concatenate([P_ie, p_i], 1))
    Z = jnp.concatenate([-U[:, : 3 * S], Q_ie, q_i - U[:, 3 * S :]], 1)
    T = dot3(Minv, Z)
    Tp = jnp.concatenate([P_ie, jnp.zeros((S, 3 * S), f32), p_i], 1) - dot3(P_ii, T)
    P_ei = jnp.concatenate([own[at(c, S), at(d, S)], own[2 * S :, at(d, S)]], 0)
    Q_ei = jnp.concatenate([oth[at(d, S), at(c, S)], oth[2 * S :, at(c, S)]], 0)
    DP = dot3(P_ei, T)
    DQ = dot3(Q_ei, Tp)
    for k in range(3):
        mine = slice(k * S, (k + 1) * S)
        row_own = at(c, S) if k == 0 else slice((k + 1) * S, (k + 2) * S)
        row_oth = at(d, S) if k == 0 else slice((k + 1) * S, (k + 2) * S)
        to_own = at(c + 2 * k, S)
        to_oth = at(d + 2 * k, S)
        for n in range(3):
            col_own = at(c, S) if n == 0 else slice((n + 1) * S, (n + 2) * S)
            col_oth = at(d, S) if n == 0 else slice((n + 1) * S, (n + 2) * S)
            n_own = slice(n * S, (n + 1) * S)
            n_oth = slice((n + 3) * S, (n + 4) * S)
            m1[to_own, at(c + 2 * n, S)] = own[row_own, col_own] - DP[mine, n_own]
            m1[to_own, at(d + 2 * n, S)] = -DP[mine, n_oth]
            m1[to_oth, at(d + 2 * n, S)] = oth[row_oth, col_oth] - DQ[mine, n_oth]
            m1[to_oth, at(c + 2 * n, S)] = -DQ[mine, n_own]
        h_own = hown[:, at(c, S)] if k == 0 else hown[:, (k + 1) * S : (k + 2) * S]
        h_oth = hoth[:, at(d, S)] if k == 0 else hoth[:, (k + 1) * S : (k + 2) * S]
        m1[to_own, 6 * S :] = as_columns(h_own) - DP[mine, 6 * S :]
        m1[to_oth, 6 * S :] = as_columns(h_oth) - DQ[mine, 6 * S :]
    row = at(2 * (2 - s) + c, S)
    pii[...] = m1[at(2 * (2 - s), 2 * S), at(2 * (2 - s), 2 * S)]
    xi[:S] = m1[row, at(2 * (2 - s), 2 * S)]
    xi[S:, :S] = as_rows(m1[row, 6 * S :])
    xi[S:, S:] = jnp.zeros((8, S), f32)
    xe[:, : 2 * S] = m1[row, : 2 * S]
    xe[:, 2 * S :] = m1[row, at(2 * (1 + s), 2 * S)]
    first = jnp.where(c == 0, jnp.where(s == 0, 4, 2 * r), 8)
    r1[...] = m1[at(first, S // 2, S // 2), :]
    r2[...] = m1[5 * S // 2 : 3 * S, :]


def level2_inverse(pii, xin, xic, minv, gii, qii):
    c, s, r = roles()
    qii[at(c, S), :] = xin[:S]
    qii[at(1 - c, S), :] = xic[:S]
    X = inverse(dot_full(qii[...], pii[...]))
    minv[...] = X
    gii[...] = dot3(X, qii[...])


def level2_interface(minv, gii, m1, xin, xic, xen, xec, t, y, yi, ye, qe):
    c, s, r = roles()
    o = 1 - s
    inner = at(2 * (2 - s), 2 * S)
    outer = at(2 * (1 + s), 2 * S)
    P_e = jnp.concatenate([m1[inner, : 2 * S], m1[inner, outer], m1[inner, 6 * S :]], 1)
    A = dot3(gii[...], P_e)
    qe[at(c, S), : 4 * S] = xen[...]
    qe[at(1 - c, S), : 4 * S] = xec[...]
    qe[at(c, S), 4 * S :] = as_columns(xin[S : S + 1, :S])
    qe[at(1 - c, S), 4 * S :] = as_columns(xic[S : S + 1, :S])
    B = dot3(minv[...], qe[...])
    t[:, at(s, S)] = -A[:, :S]
    t[:, at(2 + s, S)] = -A[:, S : 2 * S]
    t[:, at(4 + 2 * s, 2 * S)] = -A[:, 2 * S : 4 * S]
    t[:, at(o, S)] = B[:, :S]
    t[:, at(2 + o, S)] = B[:, S : 2 * S]
    t[:, at(4 + 2 * o, 2 * S)] = B[:, 2 * S : 4 * S]
    t[:, 8 * S :] = B[:, 4 * S :] - A[:, 4 * S :]
    row = at(1 - r, S)
    y[...] = -dot3(m1[row, inner], t[...])
    y[:, at(s, S)] += m1[row, :S]
    y[:, at(2 + s, S)] += m1[row, S : 2 * S]
    y[:, at(4 + 2 * s, 2 * S)] += m1[row, outer]
    y[:, 8 * S :] += m1[row, 6 * S :]
    half = at(c, S // 2, S // 2)
    yi[: S // 2] = y[half, at(2 * (1 - r), 2 * S)]
    yi[S // 2 :, :S] = as_rows(y[:, 8 * S :])
    yi[S // 2 :, S:] = jnp.zeros((8, S), f32)
    ye[:, : 2 * S] = y[half, at(2 * r, 2 * S)]
    ye[:, 2 * S :] = y[half, 4 * S : 8 * S]


def level2_rows(t, m1, r1n, r2n, rows, chip, work):
    c, s, r = roles()
    o = 1 - s
    H = S // 2
    inner = at(2 * (2 - s), 2 * S)
    outer = at(2 * (1 + s), 2 * S)
    m = 2 * c + s

    @pl.when(m == 0)
    def _():
        work[: 2 * H] = m1[at(2 * r, 2 * H, H), :]
        work[2 * H :] = r1n[...]

    @pl.when(m == 1)
    def _():
        work[:H] = m1[at(2 * r + 1, H, H), :]
        work[H : 2 * H] = r1n[...]
        work[2 * H :] = r2n[...]

    @pl.when(m == 2)
    def _():
        work[: 2 * H] = m1[6 * H : 8 * H, :]
        work[2 * H :] = r1n[...]

    @pl.when(m == 3)
    def _():
        work[...] = m1[9 * H : 12 * H, :]

    start = jnp.where(m == 1, H, jnp.where(m == 3, 3 * H, 2 * H))
    index = lax.broadcasted_iota(jnp.int32, (3 * H, 1), 0)
    got = index >= start
    V = dot3(work[:, outer], m1[inner, :])
    rows[:, : 7 * S] = V
    V_ii = rows[:, inner]
    V_pair = rows[:, outer]
    C = jnp.where(got, V_ii, -work[:, inner])
    D = dot3(C, t[...])
    own_side = jnp.where(got, -V[:, : 2 * S], work[:, : 2 * S])
    own_pair = jnp.where(got, -V_pair, work[:, outer])
    oth_side = jnp.where(got, work[:, : 2 * S], 0.0)
    oth_pair = jnp.where(got, work[:, inner], 0.0)
    data = work[:, 6 * S :] - jnp.where(got, V[:, 6 * S :], 0.0)
    rows[...] = D
    rows[:, at(s, S)] += own_side[:, :S]
    rows[:, at(2 + s, S)] += own_side[:, S:]
    rows[:, at(4 + 2 * s, 2 * S)] += own_pair
    rows[:, at(o, S)] += oth_side[:, :S]
    rows[:, at(2 + o, S)] += oth_side[:, S:]
    rows[:, at(4 + 2 * o, 2 * S)] += oth_pair
    rows[:, 8 * S :] += data
    P_ei = jnp.concatenate([m1[at(r, S), inner], m1[outer, inner]], 0)
    T_i = jnp.concatenate([t[:, at(2 * (1 - r), 2 * S)], t[:, 8 * S :]], 1)
    chip[...] = -dot3(P_ei, T_i)
    chip[:S, at(s, S)] += m1[at(r, S), at(1 - r, S)]
    chip[S:, at(s, S)] += m1[outer, at(1 - r, S)]
    chip[:S, 2 * S :] += m1[at(r, S), 6 * S :]
    chip[S:, 2 * S :] += m1[outer, 6 * S :]


def level3_inverse(y, yx, yz, yd, yxc, yzc, ydc, chip, minv, gii, th, hs, pii, qii, pq):
    c, s, r = roles()
    o = 1 - s
    d = 1 - c
    H = S // 2
    pii[at(s, S), :] = y[:, at(2 * (1 - r), 2 * S)]
    pii[at(2 * o + c, H, H), :] = yx[:H]
    pii[at(2 * o + d, H, H), :] = yxc[:H]
    qii[at(2 * s + c, H, H), :] = yz[:H]
    qii[at(2 * s + d, H, H), :] = yzc[:H]
    qii[at(2 * o + c, H, H), :] = yd[:H]
    qii[at(2 * o + d, H, H), :] = ydc[:H]
    pq[at(s, S), :S] = y[:, 8 * S :]
    pq[at(o, S), :S] = as_columns(yx[H : H + 1, :S])
    pq[at(s, S), S:] = as_columns(yz[H : H + 1, :S])
    pq[at(o, S), S:] = as_columns(yd[H : H + 1, :S])
    X = inverse(dot_full(qii[...], pii[...]))
    xs = split(X)
    minv[...] = X
    G = dot3s(xs, split(qii[...]))
    gii[...] = G
    tv = dot3s(xs, split(pq[:, S:])) - dot3(G, pq[:, :S])
    th[...] = tv
    h3 = chip[:, 2 * S :] - dot3(chip[:, : 2 * S], tv)
    hs[:, :S] = jnp.where(c == 0, as_rows(h3[:S]), as_rows(h3[S : 2 * S]))
    hs[:, S:] = as_rows(h3[2 * S :])


def level3_rows(minv, gii, th, y, yx, yz, yd, yxc, yzc, ydc, rows, top, h3, pe, qe):
    c, s, r = roles()
    o = 1 - s
    d = 1 - c
    H = S // 2
    pe[at(s, S), : 2 * S] = y[:, at(2 * r, 2 * S)]
    pe[at(s, S), 2 * S :] = y[:, 4 * S : 8 * S]
    pe[at(2 * o + c, H, H), :] = yx[...]
    pe[at(2 * o + d, H, H), :] = yxc[...]
    qe[at(2 * s + c, H, H), :] = yz[...]
    qe[at(2 * s + d, H, H), :] = yzc[...]
    qe[at(2 * o + c, H, H), :] = yd[...]
    qe[at(2 * o + d, H, H), :] = ydc[...]
    A = dot3(gii[...], pe[...])
    B = dot3(minv[...], qe[...])
    R_ei = split(rows[:, at(2 * (1 - r), 2 * S)])
    scale = math.sqrt(12 * S)
    R_ee = jnp.concatenate([rows[:, at(2 * r, 2 * S)], rows[:, 4 * S : 8 * S]], 1)
    top[:, at(6 * r, 6 * S)] = (R_ee + dot3s(R_ei, split(A))) * scale
    top[:, at(6 * (1 - r), 6 * S)] = dot3s(R_ei, split(B)) * (-scale)
    h3[...] = rows[:, 8 * S :] - dot3s(R_ei, split(th[...]))


def couple(top, h3, g0, gx, gz, gd, k0, kx, kz, kd, out, inc):
    c, s, r = roles()
    for mine, core, ss, rr in ((g0, k0, s, r), (gx, kx, 1 - s, r), (gz, kz, s, 1 - r), (gd, kd, 1 - s, 1 - r)):
        side = jnp.where(c == 0, mine[:, :S], core[:, :S])
        pair = jnp.where(c == 0, core[...], mine[...])
        inc[:, at(6 * rr + ss, S)] = side
        inc[:, at(6 * rr + 2 + 2 * ss, 2 * S)] = pair
    lane = lax.broadcasted_iota(jnp.int32, (h3.shape[0], S), 1)
    total = jnp.where(lane == 0, h3[...], 0.0)
    back = 1.0 / math.sqrt(12 * S)
    for k in range(12):
        total = total - top[:, k * S : (k + 1) * S] * (inc[0:1, k * S : (k + 1) * S] * back)
    lines = jnp.concatenate([total, jnp.zeros((2 * S - h3.shape[0], S), f32)], 0)
    flat = jnp.concatenate([lines[:S].T, lines[S:].T], 1)
    out[...] = jnp.sum(flat, 0, keepdims=True)[:, : h3.shape[0]]


def call(body, outs, scratch, args, flops):
    total = sum(a.size for a in args) + sum(math.prod(o) for o in outs)
    return pl.pallas_call(
        body,
        out_shape=[jax.ShapeDtypeStruct(o, f32) for o in outs],
        scratch_shapes=[pltpu.VMEM(x, f32) for x in scratch],
        compiler_params=pltpu.CompilerParams(vmem_limit_bytes=24 * 1024 * 1024),
        cost_estimate=pl.CostEstimate(flops=flops, bytes_accessed=4 * total, transcendentals=0),
        name=body.__name__,
    )(*args)


def send(value, to):
    nx, ny = lax.axis_size("gx"), lax.axis_size("gy")
    pairs = []
    for i in range(nx):
        for j in range(ny):
            goal = to(i, j)
            if goal is not None and 0 <= goal[0] < nx and 0 <= goal[1] < ny:
                pairs.append((i * ny + j, goal[0] * ny + goal[1]))
    return lax.ppermute(value, ("gx", "gy"), pairs)


def over_core(value):
    return send(value, lambda i, j: (i ^ 1, j))


def over_x(value):
    return send(value, lambda i, j: (i, j ^ 1))


def over_z(value):
    return send(value, lambda i, j: (i ^ 2, j))


def over_xz(value):
    return send(value, lambda i, j: (i ^ 2, j ^ 1))


def edge_target(i, j):
    if i % 2 == 0:
        return (i + 2, j) if (i // 2) % 2 else (i - 2, j)
    return (i, j + 1) if j % 2 else (i, j - 1)


def local(leaf_map, source_trace, tile_class, absorb_table):
    leaf = leaf_map[0, 0]
    classes = tile_class[0, 0]
    chosen = (classes[:, None] == jnp.arange(absorb_table.shape[0], dtype=jnp.int32)[None, :]).astype(f32)
    levels = jnp.sum(chosen * absorb_table[None, :], axis=1)
    seg = leaf.shape[0] // classes.shape[0]
    spread = jnp.broadcast_to(levels[:, None], (classes.shape[0], seg)).reshape(-1)
    hown = (spread * source_trace[0, 0])[None]

    oth = over_core(leaf)
    hoth = over_core(hown)
    m1, pii, xi, xe, r1, r2 = call(
        level1,
        [(6 * S, 7 * S), (2 * S, 2 * S), (S + 8, 2 * S), (S, 4 * S), (S // 2, 7 * S), (S // 2, 7 * S)],
        [],
        [leaf, oth, hown, hoth],
        3 * 2 * 768 * 128 * 896 * 2,
    )
    xin = over_x(xi)
    xic = over_core(xin)
    xen = over_x(xe)
    r1n = send(r1, lambda i, j: (i, j ^ 1) if (i % 2 == 0 or j % 2 == 1) else None)
    r2n = send(r2, lambda i, j: (i, j ^ 1) if (i % 2 == 0 and j % 2 == 0) else None)
    minv, gii = call(
        level2_inverse, [(2 * S, 2 * S)] * 2, [(2 * S, 2 * S)], [pii, xin, xic], 3 * 2 * 256**3 * 16
    )
    xec = over_core(xen)
    t, y, yi, ye = call(
        level2_interface,
        [(2 * S, 9 * S), (S, 9 * S), (S // 2 + 8, 2 * S), (S // 2, 6 * S)],
        [(2 * S, 5 * S)],
        [minv, gii, m1, xin, xic, xen, xec],
        3 * 2 * 256 * 256 * 1152 * 2,
    )
    yx, yz, yd = over_x(yi), over_z(yi), over_xz(yi)
    yxc, yzc, ydc = over_core(yx), over_core(yz), over_core(yd)
    ex, ez, ed = over_x(ye), over_z(ye), over_xz(ye)
    rows, chip = call(
        level2_rows,
        [(3 * S // 2, 9 * S), (3 * S, 3 * S)],
        [(3 * S // 2, 7 * S)],
        [t, m1, r1n, r2n],
        3 * 2 * 256 * 256 * 1152 * 2,
    )
    minv3, gii3, th, hs = call(
        level3_inverse,
        [(2 * S, 2 * S), (2 * S, 2 * S), (2 * S, S), (8, 2 * S)],
        [(2 * S, 2 * S)] * 3,
        [y, yx, yz, yd, yxc, yzc, ydc, chip],
        3 * 2 * 256**3 * 16,
    )
    exc, ezc, edc = over_core(ex), over_core(ez), over_core(ed)
    g0 = send(hs, edge_target)
    top, h3 = call(
        level3_rows,
        [(3 * S // 2, 12 * S), (3 * S // 2, S)],
        [(2 * S, 6 * S)] * 2,
        [minv3, gii3, th, y, ex, ez, ed, exc, ezc, edc, rows],
        3 * 2 * 256 * 256 * 1536 * 3,
    )
    gx, gz, gd = over_x(g0), over_z(g0), over_xz(g0)
    k0, kx, kz, kd = over_core(g0), over_core(gx), over_core(gz), over_core(gd)
    (out,) = call(
        couple, [(1, 3 * S // 2)], [(8, 12 * S)], [top, h3, g0, gx, gz, gd, k0, kx, kz, kd], 2 * 192 * 1536
    )
    return top[None, None], out[None]


def solution(mesh):
    return jax.shard_map(
        local,
        mesh=mesh,
        in_specs=(P("gx", "gy", None, None), P("gx", "gy", None), P("gx", "gy", None), P()),
        out_specs=(P("gx", "gy", None, None), P("gx", "gy", None)),
        check_vma=False,
    )
```

profile of v0, /device:TPU:1, one launch (start us, length us, event | category | flops | bytes accessed | tf_op | source)
XLA Modules:
  0.0 77.5 jit_solution(5101600219045629359)
XLA Ops:
  0.6 3.3 %collective-permute-start = (f32[512,512]{1,0:T(8,128)}, f32[512,512]{1,0:T(8,128)S(1)}, u32[]{:S(2)}, u32[]{:S(2)}) collective-permute-start(f32[512,512]{1,0:T(8,128)} %bitcast.7), channel_id=1, source_target_pairs={{0,16},{1,17},{2,18},{3,19},{4,20},{5,21},{6,22},{7,23},{8,24},{9,... | collective-permute-start | bytes 3145736 | tf_op jit(solution)/shard_map/ppermute | solution.py:318
  4.0 0.8 select_reduce_fusion
  4.7 0.1 broadcast_in_dim.6
  4.8 0.1 reshape.27
  4.9 0.7 bitcast_multiply_fusion.hown
  5.6 0.0 collective-permute-start.1
  5.6 1.1 %collective-permute-done.1.hoth = f32[1,512]{1,0:T(1,128)S(1)} collective-permute-done((f32[1,512]{1,0:T(1,128)S(1)}, f32[1,512]{1,0:T(1,128)S(1)}, u32[]{:S(2)}, u32[]{:S(2)}) %collective-permute-start.1) | collective-permute-done | bytes 2080 | tf_op jit(solution)/shard_map/ppermute | solution.py:318
  6.7 0.0 collective-permute-done.oth
  6.7 1.2 %copy-done.1 = f32[1,1,512,512]{3,2,1,0:T(8,128)S(1)} copy-done((f32[1,1,512,512]{3,2,1,0:T(8,128)S(1)}, f32[1,1,512,512]{3,2,1,0:T(8,128)}, u32[]{:S(2)}) %copy-start.1) | copy-done | bytes 1048600
  7.9 4.6 %level1.1 = (f32[768,896]{1,0:T(8,128)S(1)}, f32[256,256]{1,0:T(8,128)S(1)}, f32[136,256]{1,0:T(8,128)S(1)}, f32[128,512]{1,0:T(8,128)S(1)}, f32[64,896]{1,0:T(8,128)S(1)}, /*index=5*/f32[64,896]{1,0:T(8,128)S(1)}) custom-call(f32[512,512]{1,0:T(8,128)S(1)} %bitcast.8, f32[512,512]{1,0:T(8,128)S(1)} %collective-permute-done.oth, ...), custom_call_target="tpu_custom_call" | custom-call | flops 1056964608 | bytes 5976064 | tf_op jit(solution)/shard_map/level1/pallas_call | solution.py:300
  12.5 0.1 collective-permute-start.4
  12.6 1.5 %collective-permute-start.2 = (f32[136,256]{1,0:T(8,128)S(1)}, f32[136,256]{1,0:T(8,128)S(1)}, u32[]{:S(2)}, u32[]{:S(2)}) collective-permute-start(f32[136,256]{1,0:T(8,128)S(1)} %get-tuple-element.23), channel_id=1, source_target_pairs={{0,1},{1,0},{2,3},{3,2},{4,5},{5,4},{6,7},{7,6},{8,9},{9,8},{10,11... | collective-permute-start | bytes 417800 | tf_op jit(solution)/shard_map/ppermute | solution.py:318
  14.0 9.3 %collective-permute-done.2.xin = f32[136,256]{1,0:T(8,128)S(1)} collective-permute-done((f32[136,256]{1,0:T(8,128)S(1)}, f32[136,256]{1,0:T(8,128)S(1)}, u32[]{:S(2)}, u32[]{:S(2)}) %collective-permute-start.2) | collective-permute-done | bytes 139296 | tf_op jit(solution)/shard_map/ppermute | solution.py:318
  23.3 1.0 %collective-permute-start.3 = (f32[136,256]{1,0:T(8,128)S(1)}, f32[136,256]{1,0:T(8,128)S(1)}, u32[]{:S(2)}, u32[]{:S(2)}) collective-permute-start(f32[136,256]{1,0:T(8,128)S(1)} %collective-permute-done.2.xin), channel_id=1, source_target_pairs={{0,16},{1,17},{2,18},{3,19},{4,20},{5,21},{6,22},{7,23},{8,24},{9,... | collective-permute-start | bytes 417800 | tf_op jit(solution)/shard_map/ppermute | solution.py:318
  24.3 0.0 collective-permute-done.4.xen
  24.3 0.0 collective-permute-start.5
  24.3 1.3 %collective-permute-start.12 = (f32[64,896]{1,0:T(8,128)S(1)}, f32[64,896]{1,0:T(8,128)S(1)}, u32[]{:S(2)}, u32[]{:S(2)}) collective-permute-start(f32[64,896]{1,0:T(8,128)S(1)} %get-tuple-element.31), channel_id=1, source_target_pairs={{0,1},{1,0},{2,3},{3,2},{4,5},{5,4},{6,7},{7,6},{8,9},{9,8},{10,11... | collective-permute-start | bytes 688136 | tf_op jit(solution)/shard_map/ppermute | solution.py:318
  25.6 0.7 collective-permute-start.13
  26.3 0.0 collective-permute-done.3.xic
  26.3 4.3 %level2_inverse.1 = (f32[256,256]{1,0:T(8,128)S(1)}, f32[256,256]{1,0:T(8,128)S(1)}) custom-call(f32[256,256]{1,0:T(8,128)S(1)} %get-tuple-element.22.pii, f32[136,256]{1,0:T(8,128)S(1)} %collective-permute-done.2.xin, f32[136,256]{1,0:T(8,128)S(1)} %collective-permute-done.3.xic), custom_call_target="tpu_custom_call" | custom-call | flops 1610612736 | bytes 1064960 | tf_op jit(solution)/shard_map/level2_inverse/pallas_call | solution.py:300
  30.6 1.5 %level2_interface.1 = (f32[256,1152]{1,0:T(8,128)S(1)}, f32[128,1152]{1,0:T(8,128)S(1)}, f32[72,256]{1,0:T(8,128)S(1)}, f32[64,768]{1,0:T(8,128)S(1)}) custom-call(f32[256,256]{1,0:T(8,128)S(1)} %get-tuple-element.24.minv, f32[256,256]{1,0:T(8,128)S(1)} %get-tuple-element.25.gii, f32[768,896]{1,0:T(8,128)S(1)} %get-tuple-element.26.m1, ...), custom_call_target="tpu_custom_call" | custom-call | flops 905969664 | bytes 6119424 | tf_op jit(solution)/shard_map/level2_interface/pallas_call | solution.py:300
  32.1 1.8 %collective-permute-start.16 = (f32[64,768]{1,0:T(8,128)S(1)}, f32[64,768]{1,0:T(8,128)S(1)}, u32[]{:S(2)}, u32[]{:S(2)}) collective-permute-start(f32[64,768]{1,0:T(8,128)S(1)} %get-tuple-element.37), channel_id=1, source_target_pairs={{0,33},{1,32},{2,35},{3,34},{4,37},{5,36},{6,39},{7,38},{8,41},{9,... | collective-permute-start | bytes 589832 | tf_op jit(solution)/shard_map/ppermute | solution.py:318
  33.9 1.6 %collective-permute-start.15 = (f32[64,768]{1,0:T(8,128)S(1)}, f32[64,768]{1,0:T(8,128)S(1)}, u32[]{:S(2)}, u32[]{:S(2)}) collective-permute-start(f32[64,768]{1,0:T(8,128)S(1)} %get-tuple-element.37), channel_id=1, source_target_pairs={{0,32},{1,33},{2,34},{3,35},{4,36},{5,37},{6,38},{7,39},{8,40},{9,... | collective-permute-start | bytes 589832 | tf_op jit(solution)/shard_map/ppermute | solution.py:318
  35.5 1.2 %collective-permute-start.8 = (f32[72,256]{1,0:T(8,128)S(1)}, f32[72,256]{1,0:T(8,128)S(1)}, u32[]{:S(2)}, u32[]{:S(2)}) collective-permute-start(f32[72,256]{1,0:T(8,128)S(1)} %get-tuple-element.29), channel_id=1, source_target_pairs={{0,33},{1,32},{2,35},{3,34},{4,37},{5,36},{6,39},{7,38},{8,41},{9,... | collective-permute-start | bytes 221192 | tf_op jit(solution)/shard_map/ppermute | solution.py:318
  36.7 1.5 %collective-permute-start.7 = (f32[72,256]{1,0:T(8,128)S(1)}, f32[72,256]{1,0:T(8,128)S(1)}, u32[]{:S(2)}, u32[]{:S(2)}) collective-permute-start(f32[72,256]{1,0:T(8,128)S(1)} %get-tuple-element.29), channel_id=1, source_target_pairs={{0,32},{1,33},{2,34},{3,35},{4,36},{5,37},{6,38},{7,39},{8,40},{9,... | collective-permute-start | bytes 221192 | tf_op jit(solution)/shard_map/ppermute | solution.py:318
  38.1 3.4 %collective-permute-done.8.yd = f32[72,256]{1,0:T(8,128)S(1)} collective-permute-done((f32[72,256]{1,0:T(8,128)S(1)}, f32[72,256]{1,0:T(8,128)S(1)}, u32[]{:S(2)}, u32[]{:S(2)}) %collective-permute-start.8) | collective-permute-done | bytes 73760 | tf_op jit(solution)/shard_map/ppermute | solution.py:318
  41.5 4.2 %collective-permute-start.6 = (f32[72,256]{1,0:T(8,128)S(1)}, f32[72,256]{1,0:T(8,128)S(1)}, u32[]{:S(2)}, u32[]{:S(2)}) collective-permute-start(f32[72,256]{1,0:T(8,128)S(1)} %get-tuple-element.29), channel_id=1, source_target_pairs={{0,1},{1,0},{2,3},{3,2},{4,5},{5,4},{6,7},{7,6},{8,9},{9,8},{10,11... | collective-permute-start | bytes 221192 | tf_op jit(solution)/shard_map/ppermute | solution.py:318
  45.8 0.7 collective-permute-done.7.yz
  46.4 3.0 %collective-permute-start.11 = (f32[72,256]{1,0:T(8,128)S(1)}, f32[72,256]{1,0:T(8,128)S(1)}, u32[]{:S(2)}, u32[]{:S(2)}) collective-permute-start(f32[72,256]{1,0:T(8,128)S(1)} %collective-permute-done.8.yd), channel_id=1, source_target_pairs={{0,16},{1,17},{2,18},{3,19},{4,20},{5,21},{6,22},{7,23},{8,24},{9,... | collective-permute-start | bytes 221192 | tf_op jit(solution)/shard_map/ppermute | solution.py:318
  49.5 2.3 %collective-permute-start.10 = (f32[72,256]{1,0:T(8,128)S(1)}, f32[72,256]{1,0:T(8,128)S(1)}, u32[]{:S(2)}, u32[]{:S(2)}) collective-permute-start(f32[72,256]{1,0:T(8,128)S(1)} %collective-permute-done.7.yz), channel_id=1, source_target_pairs={{0,16},{1,17},{2,18},{3,19},{4,20},{5,21},{6,22},{7,23},{8,24},{9,... | collective-permute-start | bytes 221192 | tf_op jit(solution)/shard_map/ppermute | solution.py:318
  51.8 0.0 collective-permute-start.9
  51.8 0.5 collective-permute-start.19
  52.3 0.1 collective-permute-start.18
  52.4 0.4 collective-permute-start.17
  52.8 1.8 %level2_rows.1 = (f32[192,1152]{1,0:T(8,128)S(1)}, f32[384,384]{1,0:T(8,128)S(1)}) custom-call(f32[256,1152]{1,0:T(8,128)S(1)} %get-tuple-element.30.t, f32[768,896]{1,0:T(8,128)S(1)} %get-tuple-element.26.m1, f32[64,896]{1,0:T(8,128)S(1)} %collective-permute-done.12.r1n, f32[64,896]{1,0:T(8,128)S(1)} %collective-permute-done.13.r2n), custom_call_target="tpu_custom_call" | custom-call | flops 905969664 | bytes 5865472 | tf_op jit(solution)/shard_map/level2_rows/pallas_call | solution.py:300
  54.7 5.1 %level3_inverse.1 = (f32[256,256]{1,0:T(8,128)S(1)}, f32[256,256]{1,0:T(8,128)S(1)}, f32[256,128]{1,0:T(8,128)S(1)}, f32[8,256]{1,0:T(8,128)S(1)}) custom-call(f32[128,1152]{1,0:T(8,128)S(1)} %get-tuple-element.28.y, f32[72,256]{1,0:T(8,128)S(1)} %collective-permute-done.6.yx, f32[72,256]{1,0:T(8,128)S(1)} %collective-permute-done.7.yz, ...), custom_call_target="tpu_custom_call" | custom-call | flops 1610612736 | bytes 2285568 | tf_op jit(solution)/shard_map/level3_inverse/pallas_call | solution.py:300
  59.8 0.7 collective-permute-start.20
  60.4 5.2 %collective-permute-start.23 = (f32[8,256]{1,0:T(8,128)S(1)}, f32[8,256]{1,0:T(8,128)S(1)}, u32[]{:S(2)}, u32[]{:S(2)}) collective-permute-start(f32[8,256]{1,0:T(8,128)S(1)} %collective-permute-done.20.g0), channel_id=1, source_target_pairs={{0,33},{1,32},{2,35},{3,34},{4,37},{5,36},{6,39},{7,38},{8,41},{9,... | collective-permute-start | bytes 24584 | tf_op jit(solution)/shard_map/ppermute | solution.py:318
  65.6 1.5 %collective-permute-start.22 = (f32[8,256]{1,0:T(8,128)S(1)}, f32[8,256]{1,0:T(8,128)S(1)}, u32[]{:S(2)}, u32[]{:S(2)}) collective-permute-start(f32[8,256]{1,0:T(8,128)S(1)} %collective-permute-done.20.g0), channel_id=1, source_target_pairs={{0,32},{1,33},{2,34},{3,35},{4,36},{5,37},{6,38},{7,39},{8,40},{9,... | collective-permute-start | bytes 24584 | tf_op jit(solution)/shard_map/ppermute | solution.py:318
  67.1 2.2 %collective-permute-start.21 = (f32[8,256]{1,0:T(8,128)S(1)}, f32[8,256]{1,0:T(8,128)S(1)}, u32[]{:S(2)}, u32[]{:S(2)}) collective-permute-start(f32[8,256]{1,0:T(8,128)S(1)} %collective-permute-done.20.g0), channel_id=1, source_target_pairs={{0,1},{1,0},{2,3},{3,2},{4,5},{5,4},{6,7},{7,6},{8,9},{9,8},{10,11... | collective-permute-start | bytes 24584 | tf_op jit(solution)/shard_map/ppermute | solution.py:318
  69.3 1.4 %collective-permute-start.24 = (f32[8,256]{1,0:T(8,128)S(1)}, f32[8,256]{1,0:T(8,128)S(1)}, u32[]{:S(2)}, u32[]{:S(2)}) collective-permute-start(f32[8,256]{1,0:T(8,128)S(1)} %collective-permute-done.20.g0), channel_id=1, source_target_pairs={{0,16},{1,17},{2,18},{3,19},{4,20},{5,21},{6,22},{7,23},{8,24},{9,... | collective-permute-start | bytes 24584 | tf_op jit(solution)/shard_map/ppermute | solution.py:318
  70.8 1.6 %collective-permute-start.27 = (f32[8,256]{1,0:T(8,128)S(1)}, f32[8,256]{1,0:T(8,128)S(1)}, u32[]{:S(2)}, u32[]{:S(2)}) collective-permute-start(f32[8,256]{1,0:T(8,128)S(1)} %collective-permute-done.23.gd), channel_id=1, source_target_pairs={{0,16},{1,17},{2,18},{3,19},{4,20},{5,21},{6,22},{7,23},{8,24},{9,... | collective-permute-start | bytes 24584 | tf_op jit(solution)/shard_map/ppermute | solution.py:318
  72.4 0.0 collective-permute-start.26
  72.4 0.5 collective-permute-start.25
  72.9 2.5 %level3_rows.1 = (f32[192,1536]{1,0:T(8,128)}, f32[192,128]{1,0:T(8,128)S(1)}) custom-call(f32[256,256]{1,0:T(8,128)S(1)} %get-tuple-element.34.minv, f32[256,256]{1,0:T(8,128)S(1)} %get-tuple-element.35.gii, f32[256,128]{1,0:T(8,128)S(1)} %get-tuple-element.36.th, f32[128,1152]{1,0:T(8,128)S(1)} %get-tuple-element.28.y, ...), custom_call_target="tpu_custom_call" | custom-call | flops 1811939328 | bytes 4587520 | tf_op jit(solution)/shard_map/level3_rows/pallas_call | solution.py:300
  75.4 0.0 copy-start
  75.5 1.3 %copy-done = f32[192,1536]{1,0:T(8,128)S(1)} copy-done((f32[192,1536]{1,0:T(8,128)S(1)}, f32[192,1536]{1,0:T(8,128)}, u32[]{:S(2)}) %copy-start) | copy-done | bytes 1179672
  76.7 0.8 couple.1
  (23 shorter events, 0.1 us)
Async XLA Ops:
  0.6 6.1 %collective-permute-start = (f32[512,512]{1,0:T(8,128)}, f32[512,512]{1,0:T(8,128)S(1)}, u32[]{:S(2)}, u32[]{:S(2)}) collective-permute-start(f32[512,512]{1,0:T(8,128)} %bitcast.7), channel_id=1, source_target_pairs={{0,16},{1,17},{2,18},{3,19},{4,20},{5,21},{6,22},{7,23},{8,24},{9,... | collective-permute-start | bytes 3145736 | tf_op jit(solution)/shard_map/ppermute | solution.py:318
  5.6 1.2 %collective-permute-start.1 = (f32[1,512]{1,0:T(1,128)S(1)}, f32[1,512]{1,0:T(1,128)S(1)}, u32[]{:S(2)}, u32[]{:S(2)}) collective-permute-start(f32[1,512]{1,0:T(1,128)S(1)} %bitcast_multiply_fusion.hown), channel_id=1, source_target_pairs={{0,16},{1,17},{2,18},{3,19},{4,20},{5,21},{6,22},{7,23},{8,24},{9,... | collective-permute-start | bytes 6152 | tf_op jit(solution)/shard_map/ppermute | solution.py:318
  6.7 1.2 %copy-start.1 = (f32[1,1,512,512]{3,2,1,0:T(8,128)S(1)}, f32[1,1,512,512]{3,2,1,0:T(8,128)}, u32[]{:S(2)}) copy-start(f32[1,1,512,512]{3,2,1,0:T(8,128)} %param.4) | copy-start | bytes 3145732
  12.5 11.8 %collective-permute-start.4 = (f32[128,512]{1,0:T(8,128)S(1)}, f32[128,512]{1,0:T(8,128)S(1)}, u32[]{:S(2)}, u32[]{:S(2)}) collective-permute-start(f32[128,512]{1,0:T(8,128)S(1)} %get-tuple-element.27), channel_id=1, source_target_pairs={{0,1},{1,0},{2,3},{3,2},{4,5},{5,4},{6,7},{7,6},{8,9},{9,8},{10,11... | collective-permute-start | bytes 786440 | tf_op jit(solution)/shard_map/ppermute | solution.py:318
  12.6 10.7 %collective-permute-start.2 = (f32[136,256]{1,0:T(8,128)S(1)}, f32[136,256]{1,0:T(8,128)S(1)}, u32[]{:S(2)}, u32[]{:S(2)}) collective-permute-start(f32[136,256]{1,0:T(8,128)S(1)} %get-tuple-element.23), channel_id=1, source_target_pairs={{0,1},{1,0},{2,3},{3,2},{4,5},{5,4},{6,7},{7,6},{8,9},{9,8},{10,11... | collective-permute-start | bytes 417800 | tf_op jit(solution)/shard_map/ppermute | solution.py:318
  23.3 3.0 %collective-permute-start.3 = (f32[136,256]{1,0:T(8,128)S(1)}, f32[136,256]{1,0:T(8,128)S(1)}, u32[]{:S(2)}, u32[]{:S(2)}) collective-permute-start(f32[136,256]{1,0:T(8,128)S(1)} %collective-permute-done.2.xin), channel_id=1, source_target_pairs={{0,16},{1,17},{2,18},{3,19},{4,20},{5,21},{6,22},{7,23},{8,24},{9,... | collective-permute-start | bytes 417800 | tf_op jit(solution)/shard_map/ppermute | solution.py:318
  24.3 6.3 %collective-permute-start.5 = (f32[128,512]{1,0:T(8,128)S(1)}, f32[128,512]{1,0:T(8,128)S(1)}, u32[]{:S(2)}, u32[]{:S(2)}) collective-permute-start(f32[128,512]{1,0:T(8,128)S(1)} %collective-permute-done.4.xen), channel_id=1, source_target_pairs={{0,16},{1,17},{2,18},{3,19},{4,20},{5,21},{6,22},{7,23},{8,24},{9,... | collective-permute-start | bytes 786440 | tf_op jit(solution)/shard_map/ppermute | solution.py:318
  24.3 11.2 %collective-permute-start.12 = (f32[64,896]{1,0:T(8,128)S(1)}, f32[64,896]{1,0:T(8,128)S(1)}, u32[]{:S(2)}, u32[]{:S(2)}) collective-permute-start(f32[64,896]{1,0:T(8,128)S(1)} %get-tuple-element.31), channel_id=1, source_target_pairs={{0,1},{1,0},{2,3},{3,2},{4,5},{5,4},{6,7},{7,6},{8,9},{9,8},{10,11... | collective-permute-start | bytes 688136 | tf_op jit(solution)/shard_map/ppermute | solution.py:318
  25.6 11.1 %collective-permute-start.13 = (f32[64,896]{1,0:T(8,128)S(1)}, f32[64,896]{1,0:T(8,128)S(1)}, u32[]{:S(2)}, u32[]{:S(2)}) collective-permute-start(f32[64,896]{1,0:T(8,128)S(1)} %get-tuple-element.32), channel_id=1, source_target_pairs={{0,1},{2,3},{4,5},{6,7},{8,9},{10,11},{12,13},{14,15},{32,33},{34,... | collective-permute-start | bytes 688136 | tf_op jit(solution)/shard_map/ppermute | solution.py:318
  32.1 19.6 %collective-permute-start.16 = (f32[64,768]{1,0:T(8,128)S(1)}, f32[64,768]{1,0:T(8,128)S(1)}, u32[]{:S(2)}, u32[]{:S(2)}) collective-permute-start(f32[64,768]{1,0:T(8,128)S(1)} %get-tuple-element.37), channel_id=1, source_target_pairs={{0,33},{1,32},{2,35},{3,34},{4,37},{5,36},{6,39},{7,38},{8,41},{9,... | collective-permute-start | bytes 589832 | tf_op jit(solution)/shard_map/ppermute | solution.py:318
  33.9 18.4 %collective-permute-start.15 = (f32[64,768]{1,0:T(8,128)S(1)}, f32[64,768]{1,0:T(8,128)S(1)}, u32[]{:S(2)}, u32[]{:S(2)}) collective-permute-start(f32[64,768]{1,0:T(8,128)S(1)} %get-tuple-element.37), channel_id=1, source_target_pairs={{0,32},{1,33},{2,34},{3,35},{4,36},{5,37},{6,38},{7,39},{8,40},{9,... | collective-permute-start | bytes 589832 | tf_op jit(solution)/shard_map/ppermute | solution.py:318
  35.5 16.9 %collective-permute-start.14 = (f32[64,768]{1,0:T(8,128)S(1)}, f32[64,768]{1,0:T(8,128)S(1)}, u32[]{:S(2)}, u32[]{:S(2)}) collective-permute-start(f32[64,768]{1,0:T(8,128)S(1)} %get-tuple-element.37), channel_id=1, source_target_pairs={{0,1},{1,0},{2,3},{3,2},{4,5},{5,4},{6,7},{7,6},{8,9},{9,8},{10,11... | collective-permute-start | bytes 589832 | tf_op jit(solution)/shard_map/ppermute | solution.py:318
  35.5 6.0 %collective-permute-start.8 = (f32[72,256]{1,0:T(8,128)S(1)}, f32[72,256]{1,0:T(8,128)S(1)}, u32[]{:S(2)}, u32[]{:S(2)}) collective-permute-start(f32[72,256]{1,0:T(8,128)S(1)} %get-tuple-element.29), channel_id=1, source_target_pairs={{0,33},{1,32},{2,35},{3,34},{4,37},{5,36},{6,39},{7,38},{8,41},{9,... | collective-permute-start | bytes 221192 | tf_op jit(solution)/shard_map/ppermute | solution.py:318
  36.7 9.8 %collective-permute-start.7 = (f32[72,256]{1,0:T(8,128)S(1)}, f32[72,256]{1,0:T(8,128)S(1)}, u32[]{:S(2)}, u32[]{:S(2)}) collective-permute-start(f32[72,256]{1,0:T(8,128)S(1)} %get-tuple-element.29), channel_id=1, source_target_pairs={{0,32},{1,33},{2,34},{3,35},{4,36},{5,37},{6,38},{7,39},{8,40},{9,... | collective-permute-start | bytes 221192 | tf_op jit(solution)/shard_map/ppermute | solution.py:318
  41.5 7.9 %collective-permute-start.6 = (f32[72,256]{1,0:T(8,128)S(1)}, f32[72,256]{1,0:T(8,128)S(1)}, u32[]{:S(2)}, u32[]{:S(2)}) collective-permute-start(f32[72,256]{1,0:T(8,128)S(1)} %get-tuple-element.29), channel_id=1, source_target_pairs={{0,1},{1,0},{2,3},{3,2},{4,5},{5,4},{6,7},{7,6},{8,9},{9,8},{10,11... | collective-permute-start | bytes 221192 | tf_op jit(solution)/shard_map/ppermute | solution.py:318
  46.4 5.3 %collective-permute-start.11 = (f32[72,256]{1,0:T(8,128)S(1)}, f32[72,256]{1,0:T(8,128)S(1)}, u32[]{:S(2)}, u32[]{:S(2)}) collective-permute-start(f32[72,256]{1,0:T(8,128)S(1)} %collective-permute-done.8.yd), channel_id=1, source_target_pairs={{0,16},{1,17},{2,18},{3,19},{4,20},{5,21},{6,22},{7,23},{8,24},{9,... | collective-permute-start | bytes 221192 | tf_op jit(solution)/shard_map/ppermute | solution.py:318
  49.5 5.2 %collective-permute-start.10 = (f32[72,256]{1,0:T(8,128)S(1)}, f32[72,256]{1,0:T(8,128)S(1)}, u32[]{:S(2)}, u32[]{:S(2)}) collective-permute-start(f32[72,256]{1,0:T(8,128)S(1)} %collective-permute-done.7.yz), channel_id=1, source_target_pairs={{0,16},{1,17},{2,18},{3,19},{4,20},{5,21},{6,22},{7,23},{8,24},{9,... | collective-permute-start | bytes 221192 | tf_op jit(solution)/shard_map/ppermute | solution.py:318
  51.8 2.9 %collective-permute-start.9 = (f32[72,256]{1,0:T(8,128)S(1)}, f32[72,256]{1,0:T(8,128)S(1)}, u32[]{:S(2)}, u32[]{:S(2)}) collective-permute-start(f32[72,256]{1,0:T(8,128)S(1)} %collective-permute-done.6.yx), channel_id=1, source_target_pairs={{0,16},{1,17},{2,18},{3,19},{4,20},{5,21},{6,22},{7,23},{8,24},{9,... | collective-permute-start | bytes 221192 | tf_op jit(solution)/shard_map/ppermute | solution.py:318
  51.8 20.6 %collective-permute-start.19 = (f32[64,768]{1,0:T(8,128)S(1)}, f32[64,768]{1,0:T(8,128)S(1)}, u32[]{:S(2)}, u32[]{:S(2)}) collective-permute-start(f32[64,768]{1,0:T(8,128)S(1)} %collective-permute-done.16.yd), channel_id=1, source_target_pairs={{0,16},{1,17},{2,18},{3,19},{4,20},{5,21},{6,22},{7,23},{8,24},{9,... | collective-permute-start | bytes 589832 | tf_op jit(solution)/shard_map/ppermute | solution.py:318
  52.3 20.1 %collective-permute-start.18 = (f32[64,768]{1,0:T(8,128)S(1)}, f32[64,768]{1,0:T(8,128)S(1)}, u32[]{:S(2)}, u32[]{:S(2)}) collective-permute-start(f32[64,768]{1,0:T(8,128)S(1)} %collective-permute-done.15.yz), channel_id=1, source_target_pairs={{0,16},{1,17},{2,18},{3,19},{4,20},{5,21},{6,22},{7,23},{8,24},{9,... | collective-permute-start | bytes 589832 | tf_op jit(solution)/shard_map/ppermute | solution.py:318
  52.4 20.5 %collective-permute-start.17 = (f32[64,768]{1,0:T(8,128)S(1)}, f32[64,768]{1,0:T(8,128)S(1)}, u32[]{:S(2)}, u32[]{:S(2)}) collective-permute-start(f32[64,768]{1,0:T(8,128)S(1)} %collective-permute-done.14.yx), channel_id=1, source_target_pairs={{0,16},{1,17},{2,18},{3,19},{4,20},{5,21},{6,22},{7,23},{8,24},{9,... | collective-permute-start | bytes 589832 | tf_op jit(solution)/shard_map/ppermute | solution.py:318
  59.8 0.7 collective-permute-start.20
  60.4 6.7 %collective-permute-start.23 = (f32[8,256]{1,0:T(8,128)S(1)}, f32[8,256]{1,0:T(8,128)S(1)}, u32[]{:S(2)}, u32[]{:S(2)}) collective-permute-start(f32[8,256]{1,0:T(8,128)S(1)} %collective-permute-done.20.g0), channel_id=1, source_target_pairs={{0,33},{1,32},{2,35},{3,34},{4,37},{5,36},{6,39},{7,38},{8,41},{9,... | collective-permute-start | bytes 24584 | tf_op jit(solution)/shard_map/ppermute | solution.py:318
  65.6 3.7 %collective-permute-start.22 = (f32[8,256]{1,0:T(8,128)S(1)}, f32[8,256]{1,0:T(8,128)S(1)}, u32[]{:S(2)}, u32[]{:S(2)}) collective-permute-start(f32[8,256]{1,0:T(8,128)S(1)} %collective-permute-done.20.g0), channel_id=1, source_target_pairs={{0,32},{1,33},{2,34},{3,35},{4,36},{5,37},{6,38},{7,39},{8,40},{9,... | collective-permute-start | bytes 24584 | tf_op jit(solution)/shard_map/ppermute | solution.py:318
  67.1 3.7 %collective-permute-start.21 = (f32[8,256]{1,0:T(8,128)S(1)}, f32[8,256]{1,0:T(8,128)S(1)}, u32[]{:S(2)}, u32[]{:S(2)}) collective-permute-start(f32[8,256]{1,0:T(8,128)S(1)} %collective-permute-done.20.g0), channel_id=1, source_target_pairs={{0,1},{1,0},{2,3},{3,2},{4,5},{5,4},{6,7},{7,6},{8,9},{9,8},{10,11... | collective-permute-start | bytes 24584 | tf_op jit(solution)/shard_map/ppermute | solution.py:318
  69.3 6.1 %collective-permute-start.24 = (f32[8,256]{1,0:T(8,128)S(1)}, f32[8,256]{1,0:T(8,128)S(1)}, u32[]{:S(2)}, u32[]{:S(2)}) collective-permute-start(f32[8,256]{1,0:T(8,128)S(1)} %collective-permute-done.20.g0), channel_id=1, source_target_pairs={{0,16},{1,17},{2,18},{3,19},{4,20},{5,21},{6,22},{7,23},{8,24},{9,... | collective-permute-start | bytes 24584 | tf_op jit(solution)/shard_map/ppermute | solution.py:318
  70.8 4.7 %collective-permute-start.27 = (f32[8,256]{1,0:T(8,128)S(1)}, f32[8,256]{1,0:T(8,128)S(1)}, u32[]{:S(2)}, u32[]{:S(2)}) collective-permute-start(f32[8,256]{1,0:T(8,128)S(1)} %collective-permute-done.23.gd), channel_id=1, source_target_pairs={{0,16},{1,17},{2,18},{3,19},{4,20},{5,21},{6,22},{7,23},{8,24},{9,... | collective-permute-start | bytes 24584 | tf_op jit(solution)/shard_map/ppermute | solution.py:318
  72.4 3.0 %collective-permute-start.26 = (f32[8,256]{1,0:T(8,128)S(1)}, f32[8,256]{1,0:T(8,128)S(1)}, u32[]{:S(2)}, u32[]{:S(2)}) collective-permute-start(f32[8,256]{1,0:T(8,128)S(1)} %collective-permute-done.22.gz), channel_id=1, source_target_pairs={{0,16},{1,17},{2,18},{3,19},{4,20},{5,21},{6,22},{7,23},{8,24},{9,... | collective-permute-start | bytes 24584 | tf_op jit(solution)/shard_map/ppermute | solution.py:318
  72.4 3.0 %collective-permute-start.25 = (f32[8,256]{1,0:T(8,128)S(1)}, f32[8,256]{1,0:T(8,128)S(1)}, u32[]{:S(2)}, u32[]{:S(2)}) collective-permute-start(f32[8,256]{1,0:T(8,128)S(1)} %collective-permute-done.21.gx), channel_id=1, source_target_pairs={{0,16},{1,17},{2,18},{3,19},{4,20},{5,21},{6,22},{7,23},{8,24},{9,... | collective-permute-start | bytes 24584 | tf_op jit(solution)/shard_map/ppermute | solution.py:318
  75.4 1.3 %copy-start = (f32[192,1536]{1,0:T(8,128)S(1)}, f32[192,1536]{1,0:T(8,128)}, u32[]{:S(2)}) copy-start(f32[192,1536]{1,0:T(8,128)} %get-tuple-element.39.top) | copy-start | bytes 3538948
where the time goes:
time: 78.5 us; the launch traced here: 77.5 us
  starting transfers between devices  37.5 us (48%)
  Pallas kernels  20.6 us (26%)
  waiting for transfers between devices  14.5 us (18%)
  local copies, waits for them, and re-layouts  2.65 us (3%)
  other arithmetic  1.44 us (2%)
    ppermute x28, starting transfers between devices, send(): return lax.ppermute(value, ('gx', 'gy'), pairs)  37.5 us
    pallas_call x7, Pallas kernels, call(): pl.pallas_call(body, out_shape=[jax.ShapeDtypeStruct(o, f32) for o in out...  20.6 us
    ppermute x28, waiting for transfers between devices, send(): return lax.ppermute(value, ('gx', 'gy'), pairs)  14.5 us
    unnamed x4, local copies, waits for them, and re-layouts  2.49 us
  transfers between devices with their start and end apart: 28, of which 4 were waited for; matrix products, arithmetic and copies ran while one was open for 2% of the time, Pallas kernels for 20%

commit v1 on v0

v1 whole, which is shorter than its diff:
```python
import math

import jax
import jax.numpy as jnp
from jax import lax
from jax.experimental import pallas as pl
from jax.experimental.pallas import tpu as pltpu
from jax.sharding import PartitionSpec as P

S = 128
f32 = jnp.float32
bf16 = jnp.bfloat16
HIGHEST = lax.Precision.HIGHEST


def roles():
    gx = lax.axis_index("gx")
    gy = lax.axis_index("gy")
    return gx % 2, gy % 2, (gx // 2) % 2


def at(offset, size, unit=S):
    return pl.ds(pl.multiple_of(offset * unit, unit), size)


def split(x):
    high = x.astype(bf16)
    return high, (x - high.astype(f32)).astype(bf16)


def mm(a, b):
    return jnp.dot(a, b, preferred_element_type=f32)


def dot3s(a, b):
    return mm(a[0], b[0]) + (mm(a[0], b[1]) + mm(a[1], b[0]))


def dot3(a, b):
    return dot3s(split(a), split(b))


def dot_full(a, b):
    return jnp.dot(a, b, precision=HIGHEST, preferred_element_type=f32)


def inverse(K):
    n = K.shape[0]
    rows = lax.broadcasted_iota(jnp.int32, (n, n), 0)
    cols = lax.broadcasted_iota(jnp.int32, (n, n), 1)
    eye = (rows == cols).astype(f32)
    ks = split(K)
    X = eye + K
    power = mm(ks[0], ks[0])
    steps = 5
    for j in range(1, steps + 1):
        pb = power.astype(bf16)
        if j < steps:
            both = mm(jnp.concatenate([X.astype(bf16), pb], 0), pb)
            X = X + both[:n]
            power = both[n:]
        else:
            X = X + mm(X.astype(bf16), pb)
    for _ in range(2):
        xs = split(X)
        residual = eye - X + dot3s(ks, xs)
        X = X + mm(xs[0], residual.astype(bf16))
    residual = eye - X + dot_full(K, X)
    return X + dot3(X, residual)


def as_columns(row):
    return jnp.broadcast_to(row, (S, S)).T


def as_rows(block):
    return block.T[:8]


def bring(leaf, mark):
    mark[...] = leaf[:8, :S]


def level1_interface(own, oth, hown, hoth, mark, minv, pii, xi):
    c, s, r = roles()
    d = 1 - c
    e = 3 - s
    P_ii = own[at(d, S), at(d, S)]
    Q_ii = split(oth[at(c, S), at(c, S)])
    P_ie = own[at(d, S), at(e, S)]
    Q_ie = oth[at(c, S), at(e, S)]
    p_i = as_columns(hown[:, at(d, S)])
    q_i = as_columns(hoth[:, at(c, S)])
    X = inverse(dot_full(oth[at(c, S), at(c, S)], P_ii))
    minv[...] = X
    U = dot3s(Q_ii, split(jnp.concatenate([P_ie, p_i], 1)))
    T = split(dot3(X, jnp.concatenate([-U[:, :S], Q_ie, q_i - U[:, S:]], 1)))
    D = dot3s(split(own[at(e, S), at(d, S)]), T)
    Tp = jnp.concatenate([P_ie, jnp.zeros((S, S), f32)], 1) - dot3s(split(P_ii), (T[0][:, : 2 * S], T[1][:, : 2 * S]))
    DQ = dot3(oth[at(e, S), at(c, S)], Tp)
    pii[at(c, S), at(c, S)] = own[at(e, S), at(e, S)] - D[:, :S]
    pii[at(c, S), at(d, S)] = -D[:, S : 2 * S]
    pii[at(d, S), at(c, S)] = -DQ[:, :S]
    pii[at(d, S), at(d, S)] = oth[at(e, S), at(e, S)] - DQ[:, S:]
    xi[:S] = pii[at(c, S), :]
    xi[S:, :S] = as_rows(as_columns(hown[:, at(e, S)]) - D[:, 2 * S :])
    xi[S:, S:] = jnp.zeros((8, S), f32)


def level1_map(own, oth, hown, hoth, minv, m1, xe, xl):
    c, s, r = roles()
    d = 1 - c
    P_ii = own[at(d, S), at(d, S)]
    Q_ii = oth[at(c, S), at(c, S)]
    P_ie = jnp.concatenate([own[at(d, S), at(c, S)], own[at(d, S), 2 * S :]], 1)
    Q_ie = jnp.concatenate([oth[at(c, S), at(d, S)], oth[at(c, S), 2 * S :]], 1)
    p_i = as_columns(hown[:, at(d, S)])
    q_i = as_columns(hoth[:, at(c, S)])
    U = dot3(Q_ii, jnp.concatenate([P_ie, p_i], 1))
    Z = jnp.concatenate([-U[:, : 3 * S], Q_ie, q_i - U[:, 3 * S :]], 1)
    T = dot3(minv[...], Z)
    ts = split(T)
    Tp = jnp.concatenate([P_ie, jnp.zeros((S, 3 * S), f32), p_i], 1) - dot3s(split(P_ii), ts)
    P_ei = jnp.concatenate([own[at(c, S), at(d, S)], own[2 * S :, at(d, S)]], 0)
    Q_ei = jnp.concatenate([oth[at(d, S), at(c, S)], oth[2 * S :, at(c, S)]], 0)
    DP = dot3s(split(P_ei), ts)
    DQ = dot3(Q_ei, Tp)
    for k in range(3):
        mine = slice(k * S, (k + 1) * S)
        row_own = at(c, S) if k == 0 else slice((k + 1) * S, (k + 2) * S)
        row_oth = at(d, S) if k == 0 else slice((k + 1) * S, (k + 2) * S)
        to_own = at(c + 2 * k, S)
        to_oth = at(d + 2 * k, S)
        for n in range(3):
            col_own = at(c, S) if n == 0 else slice((n + 1) * S, (n + 2) * S)
            col_oth = at(d, S) if n == 0 else slice((n + 1) * S, (n + 2) * S)
            n_own = slice(n * S, (n + 1) * S)
            n_oth = slice((n + 3) * S, (n + 4) * S)
            m1[to_own, at(c + 2 * n, S)] = own[row_own, col_own] - DP[mine, n_own]
            m1[to_own, at(d + 2 * n, S)] = -DP[mine, n_oth]
            m1[to_oth, at(d + 2 * n, S)] = oth[row_oth, col_oth] - DQ[mine, n_oth]
            m1[to_oth, at(c + 2 * n, S)] = -DQ[mine, n_own]
        h_own = hown[:, at(c, S)] if k == 0 else hown[:, (k + 1) * S : (k + 2) * S]
        h_oth = hoth[:, at(d, S)] if k == 0 else hoth[:, (k + 1) * S : (k + 2) * S]
        m1[to_own, 6 * S :] = as_columns(h_own) - DP[mine, 6 * S :]
        m1[to_oth, 6 * S :] = as_columns(h_oth) - DQ[mine, 6 * S :]
    row = at(2 * (2 - s) + c, S)
    xe[:, : 2 * S] = m1[row, : 2 * S]
    xe[:, 2 * S :] = m1[row, at(2 * (1 + s), 2 * S)]
    xl[...] = m1[at(2 * (1 - r) + c, S // 2, S // 2), : 6 * S]


def pick(x, s, low, high):
    return jnp.where(s == 0, x[:, 2 * S * low : 2 * S * (low + 1)], x[:, 2 * S * high : 2 * S * (high + 1)])


def level2_inverse(pii, xin, xic, minv, gii, qii):
    c, s, r = roles()
    qii[at(c, S), :] = xin[:S]
    qii[at(1 - c, S), :] = xic[:S]
    X = inverse(dot_full(qii[...], pii[...]))
    minv[...] = X
    gii[...] = dot3(X, qii[...])


def level2_interface(minv, gii, m1, xin, xic, xen, xec, t, y, yi, yh, qe):
    c, s, r = roles()
    o = 1 - s
    inner = at(2 * (2 - s), 2 * S)
    outer = at(2 * (1 + s), 2 * S)
    P_e = jnp.concatenate([m1[inner, : 2 * S], m1[inner, outer], m1[inner, 6 * S :]], 1)
    A = dot3(gii[...], P_e)
    qe[at(c, S), : 4 * S] = xen[...]
    qe[at(1 - c, S), : 4 * S] = xec[...]
    qe[at(c, S), 4 * S :] = as_columns(xin[S : S + 1, :S])
    qe[at(1 - c, S), 4 * S :] = as_columns(xic[S : S + 1, :S])
    B = dot3(minv[...], qe[...])
    t[:, at(s, S)] = -A[:, :S]
    t[:, at(2 + s, S)] = -A[:, S : 2 * S]
    t[:, at(4 + 2 * s, 2 * S)] = -A[:, 2 * S : 4 * S]
    t[:, at(o, S)] = B[:, :S]
    t[:, at(2 + o, S)] = B[:, S : 2 * S]
    t[:, at(4 + 2 * o, 2 * S)] = B[:, 2 * S : 4 * S]
    t[:, 8 * S :] = B[:, 4 * S :] - A[:, 4 * S :]
    row = at(1 - r, S)
    y[...] = -dot3(m1[row, inner], t[...])
    y[:, at(s, S)] += m1[row, :S]
    y[:, at(2 + s, S)] += m1[row, S : 2 * S]
    y[:, at(4 + 2 * s, 2 * S)] += m1[row, outer]
    y[:, 8 * S :] += m1[row, 6 * S :]
    H = S // 2
    yi[:S] = y[:, at(2 * (1 - r), 2 * S)]
    yi[S:, :S] = as_rows(y[:, 8 * S :])
    yi[S:, S:] = jnp.zeros((8, S), f32)
    yh[:H] = yi[at(c, H, H), :]
    yh[H:] = yi[S:]


def level2_chip(t, m1, chip, rr):
    c, s, r = roles()
    inner = at(2 * (2 - s), 2 * S)
    outer = at(2 * (1 + s), 2 * S)
    P_ei = jnp.concatenate([m1[at(r, S), inner], m1[outer, inner]], 0)
    T_i = jnp.concatenate([t[:, at(2 * (1 - r), 2 * S)], t[:, 8 * S :]], 1)
    chip[...] = -dot3(P_ei, T_i)
    chip[:S, at(s, S)] += m1[at(r, S), at(1 - r, S)]
    chip[S:, at(s, S)] += m1[outer, at(1 - r, S)]
    chip[:S, 2 * S :] += m1[at(r, S), 6 * S :]
    chip[S:, 2 * S :] += m1[outer, 6 * S :]
    H = S // 2
    first = jnp.where(c == 0, jnp.where(s == 0, 4, 2 * r), jnp.where(s == 0, 5, 8))
    lines = at(first, H, H)
    rr[:H] = m1[lines, : 6 * S]
    rr[H:, :S] = as_rows(jnp.concatenate([m1[lines, 6 * S :]] * 2, 0))
    rr[H:, S:] = jnp.zeros((8, 5 * S), f32)


def level2_edge(t, m1, y, xln, xlc, be, yx, row):
    c, s, r = roles()
    o = 1 - s
    H = S // 2
    inner = at(2 * (2 - s), 2 * S)
    outer = at(2 * (1 + s), 2 * S)
    row[at(c, H, H), : 6 * S] = xln[...]
    row[at(1 - c, H, H), : 6 * S] = xlc[...]
    V = dot3(row[:, outer], m1[inner, : 6 * S])
    D = dot3(pick(V, s, 2, 1), jnp.concatenate([t[:, at(2 * r, 2 * S)], t[:, 4 * S : 8 * S]], 1))
    yx[...] = D
    yx[:, at(s, S)] -= jnp.where(r == 0, V[:, :S], V[:, S : 2 * S])
    yx[:, at(2 + 2 * s, 2 * S)] -= pick(V, s, 1, 2)
    yx[:, at(o, S)] += row[:, at(r, S)]
    yx[:, at(2 + 2 * o, 2 * S)] += row[:, inner]

    @pl.when(c == 0)
    def _():
        be[:, : 2 * S] = y[:, at(2 * r, 2 * S)]
        be[:, 2 * S :] = y[:, 4 * S : 8 * S]

    @pl.when(c == 1)
    def _():
        be[...] = yx[...]


def level2_rows(t, m1, rn, rc, rows, work):
    c, s, r = roles()
    o = 1 - s
    H = S // 2
    inner = at(2 * (2 - s), 2 * S)
    outer = at(2 * (1 + s), 2 * S)
    m = 2 * c + s

    @pl.when(m == 0)
    def _():
        work[: 2 * H] = m1[at(2 * r, 2 * H, H), :]

    @pl.when(m == 1)
    def _():
        work[:H] = m1[at(2 * r + 1, H, H), :]
        work[H : 2 * H, : 6 * S] = rn[:H]
        work[H : 2 * H, 6 * S :] = as_columns(rn[H : H + 1, :S])[:H]
        work[2 * H :, : 6 * S] = rc[:H]
        work[2 * H :, 6 * S :] = as_columns(rc[H : H + 1, :S])[:H]

    @pl.when(m == 2)
    def _():
        work[: 2 * H] = m1[6 * H : 8 * H, :]

    @pl.when((m == 0) | (m == 2))
    def _():
        work[2 * H :, : 6 * S] = rn[:H]
        work[2 * H :, 6 * S :] = as_columns(rn[H : H + 1, :S])[:H]

    @pl.when(m == 3)
    def _():
        work[...] = m1[9 * H : 12 * H, :]

    start = jnp.where(m == 1, H, jnp.where(m == 3, 3 * H, 2 * H))
    index = lax.broadcasted_iota(jnp.int32, (3 * H, 1), 0)
    got = index >= start
    V = dot3(work[:, outer], m1[inner, :])
    rows[:, : 7 * S] = V
    V_ii = rows[:, inner]
    V_pair = rows[:, outer]
    C = jnp.where(got, V_ii, -work[:, inner])
    D = dot3(C, t[...])
    own_side = jnp.where(got, -V[:, : 2 * S], work[:, : 2 * S])
    own_pair = jnp.where(got, -V_pair, work[:, outer])
    oth_side = jnp.where(got, work[:, : 2 * S], 0.0)
    oth_pair = jnp.where(got, work[:, inner], 0.0)
    data = work[:, 6 * S :] - jnp.where(got, V[:, 6 * S :], 0.0)
    rows[...] = D
    rows[:, at(s, S)] += own_side[:, :S]
    rows[:, at(2 + s, S)] += own_side[:, S:]
    rows[:, at(4 + 2 * s, 2 * S)] += own_pair
    rows[:, at(o, S)] += oth_side[:, :S]
    rows[:, at(2 + o, S)] += oth_side[:, S:]
    rows[:, at(4 + 2 * o, 2 * S)] += oth_pair
    rows[:, 8 * S :] += data


def level3_inverse(y, a1, k1, a2, k2, chip, minv, gii, th, hs, pii, qii, pq):
    c, s, r = roles()
    o = 1 - s
    d = 1 - c
    H = S // 2
    x = jnp.where(c == 0, a1[...], k1[...])
    z = jnp.where(c == 0, k1[...], a1[...])
    pii[at(s, S), :] = y[:, at(2 * (1 - r), 2 * S)]
    pii[at(o, S), :] = x[:S]
    qii[at(s, S), :] = z[:S]
    qii[at(2 * o + c, H, H), :] = a2[:H]
    qii[at(2 * o + d, H, H), :] = k2[:H]
    pq[at(s, S), :S] = y[:, 8 * S :]
    pq[at(o, S), :S] = as_columns(x[S : S + 1, :S])
    pq[at(s, S), S:] = as_columns(z[S : S + 1, :S])
    pq[at(o, S), S:] = as_columns(a2[H : H + 1, :S])
    X = inverse(dot_full(qii[...], pii[...]))
    xs = split(X)
    minv[...] = X
    G = dot3s(xs, split(qii[...]))
    gii[...] = G
    tv = dot3s(xs, split(pq[:, S:])) - dot3(G, pq[:, :S])
    th[...] = tv
    h3 = chip[:, 2 * S :] - dot3(chip[:, : 2 * S], tv)
    hs[:, :S] = jnp.where(c == 0, as_rows(h3[:S]), as_rows(h3[S : 2 * S]))
    hs[:, S:] = as_rows(h3[2 * S :])


def level3_rows(minv, gii, th, y, yx, be, kb, rows, top, raw, h3, pe, qe):
    c, s, r = roles()
    o = 1 - s
    pe[at(s, S), : 2 * S] = y[:, at(2 * r, 2 * S)]
    pe[at(s, S), 2 * S :] = y[:, 4 * S : 8 * S]
    pe[at(o, S), :] = yx[...]
    qe[at(s, S), :] = jnp.where(c == 0, be[...], kb[...])
    qe[at(o, S), :] = jnp.where(c == 0, kb[...], be[...])
    A = dot3(gii[...], pe[...])
    B = dot3(minv[...], qe[...])
    R_ei = split(rows[:, at(2 * (1 - r), 2 * S)])
    scale = math.sqrt(12 * S)
    R_ee = jnp.concatenate([rows[:, at(2 * r, 2 * S)], rows[:, 4 * S : 8 * S]], 1)
    own = R_ee + dot3s(R_ei, split(A))
    oth = -dot3s(R_ei, split(B))
    raw[:, at(6 * r, 6 * S)] = own
    raw[:, at(6 * (1 - r), 6 * S)] = oth
    top[...] = raw[...] * scale
    h3[...] = rows[:, 8 * S :] - dot3s(R_ei, split(th[...]))


def couple(raw, h3, g0, gx, gz, gd, k0, kx, kz, kd, out, inc):
    c, s, r = roles()
    box_x = lax.axis_index("gx") // 4
    box_y = lax.axis_index("gy") // 2
    last_x = lax.axis_size("gx") // 4 - 1
    last_y = lax.axis_size("gy") // 2 - 1
    edge_x = (box_x == 0) | (box_x == last_x)
    edge_y = (box_y == 0) | (box_y == last_y)
    at_x = jnp.where(box_x == 0, 0, 1)
    at_y = jnp.where(box_y == 0, 0, 1)
    for mine, core, ss, rr in ((g0, k0, s, r), (gx, kx, 1 - s, r), (gz, kz, s, 1 - r), (gd, kd, 1 - s, 1 - r)):
        side = jnp.where(c == 0, mine[:, :S], core[:, :S])
        pair = jnp.where(c == 0, core[...], mine[...])
        inc[:, at(6 * rr + ss, S)] = jnp.where(edge_x & (at_x == rr), 0.0, side)
        inc[:, at(6 * rr + 2 + 2 * ss, 2 * S)] = jnp.where(edge_y & (at_y == ss), 0.0, pair)
    lane = lax.broadcasted_iota(jnp.int32, (h3.shape[0], S), 1)
    total = jnp.where(lane == 0, h3[...], 0.0)
    for k in range(12):
        total = total - raw[:, k * S : (k + 1) * S] * inc[0:1, k * S : (k + 1) * S]
    lines = jnp.concatenate([total, jnp.zeros((2 * S - h3.shape[0], S), f32)], 0)
    flat = jnp.concatenate([lines[:S].T, lines[S:].T], 1)
    out[...] = jnp.sum(flat, 0, keepdims=True)[:, : h3.shape[0]]


def call(body, outs, scratch, args, us):
    whole = pl.BlockSpec(memory_space=pltpu.VMEM)
    return pl.pallas_call(
        body,
        out_shape=[jax.ShapeDtypeStruct(o, f32) for o in outs],
        in_specs=[whole] * len(args),
        out_specs=[whole] * len(outs),
        scratch_shapes=[pltpu.VMEM(x, f32) for x in scratch],
        compiler_params=pltpu.CompilerParams(vmem_limit_bytes=24 * 1024 * 1024),
        cost_estimate=pl.CostEstimate(flops=int(us * 1.15e9), bytes_accessed=0, transcendentals=0),
        name=body.__name__,
    )(*args)


def send(value, to):
    nx, ny = lax.axis_size("gx"), lax.axis_size("gy")
    pairs = []
    for i in range(nx):
        for j in range(ny):
            goal = to(i, j)
            if goal is not None and 0 <= goal[0] < nx and 0 <= goal[1] < ny:
                pairs.append((i * ny + j, goal[0] * ny + goal[1]))
    return lax.ppermute(value, ("gx", "gy"), pairs)


def after(value, *others):
    return lax.optimization_barrier((value, *others))[0]


def over_core(value):
    return send(value, lambda i, j: (i ^ 1, j))


def over_x(value):
    return send(value, lambda i, j: (i, j ^ 1))


def over_z(value):
    return send(value, lambda i, j: (i ^ 2, j))


def over_xz(value):
    return send(value, lambda i, j: (i ^ 2, j ^ 1))


def over_x_or_z(value):
    return send(value, lambda i, j: (i ^ 2, j) if i % 2 else (i, j ^ 1))


def over_edge(value):
    nx, ny = lax.axis_size("gx"), lax.axis_size("gy")

    def to(i, j):
        if i % 2 == 0:
            return ((i + 2) % nx if (i // 2) % 2 else (i - 2) % nx, j)
        return (i, (j + 1) % ny if j % 2 else (j - 1) % ny)

    return send(value, to)


def local(leaf_map, source_trace, tile_class, absorb_table):
    H = S // 2
    leaf = leaf_map[0, 0]
    oth = over_core(leaf)
    classes = tile_class[0, 0]
    chosen = (classes[:, None] == jnp.arange(absorb_table.shape[0], dtype=jnp.int32)[None, :]).astype(f32)
    levels = jnp.sum(chosen * absorb_table[None, :], axis=1)
    seg = leaf.shape[0] // classes.shape[0]
    spread = jnp.broadcast_to(levels[:, None], (classes.shape[0], seg)).reshape(-1)
    hown = (spread * source_trace[0, 0])[None]
    hoth = over_core(hown)
    (mark,) = call(bring, [(8, S)], [], [leaf], 1.0)
    minv1, pii, xi = call(
        level1_interface, [(S, S), (2 * S, 2 * S), (S + 8, 2 * S)], [], [leaf, oth, hown, hoth, mark], 2.5
    )
    xin = over_x(xi)
    m1, xe, xl = call(
        level1_map, [(6 * S, 7 * S), (S, 4 * S), (H, 6 * S)], [], [leaf, oth, hown, hoth, minv1], 2.0
    )
    xen = over_x(xe)
    xic = over_core(after(xin, xe))
    minv, gii = call(level2_inverse, [(2 * S, 2 * S)] * 2, [(2 * S, 2 * S)], [pii, xin, xic], 0.5)
    xec = over_core(after(xen, minv))
    xln = over_x(after(xl, xen, minv))
    t, y, yi, yh = call(
        level2_interface,
        [(2 * S, 9 * S), (S, 9 * S), (S + 8, 2 * S), (H + 8, 2 * S)],
        [(2 * S, 5 * S)],
        [minv, gii, m1, xin, xic, xen, xec],
        1.5,
    )
    a1, a2 = over_x_or_z(yi), over_xz(yh)
    chip, rr = call(level2_chip, [(3 * S, 3 * S), (H + 8, 6 * S)], [], [t, m1], 0.01)
    a1, a2, chip = lax.optimization_barrier((a1, a2, chip))
    k1, k2 = over_core(a1), over_core(a2)
    xlc = over_core(after(xln, chip))
    be, yx = call(level2_edge, [(S, 6 * S)] * 2, [(S, 6 * S)], [t, m1, y, xln, xlc], 0.01)
    bn = over_z(be)
    rn = over_x(after(rr, be))
    minv3, gii3, th, hs = call(
        level3_inverse,
        [(2 * S, 2 * S), (2 * S, 2 * S), (2 * S, S), (8, 2 * S)],
        [(2 * S, 2 * S)] * 3,
        [y, a1, k1, a2, k2, chip],
        20.0,
    )
    g0 = over_edge(hs)
    rc = over_core(after(rn, g0))
    kb = over_core(after(bn, g0))
    (rows,) = call(level2_rows, [(3 * H, 9 * S)], [(3 * H, 7 * S)], [t, m1, rn, rc], 1.5)
    gx, gz, gd = over_x(g0), over_z(g0), over_xz(g0)
    top, raw, h3 = call(
        level3_rows,
        [(3 * H, 12 * S), (3 * H, 12 * S), (3 * H, S)],
        [(2 * S, 6 * S)] * 2,
        [minv3, gii3, th, y, yx, bn, kb, rows],
        2.5,
    )
    g0, gx, gz, gd, h3 = lax.optimization_barrier((g0, gx, gz, gd, h3))
    k0, kx, kz, kd = over_core(g0), over_core(gx), over_core(gz), over_core(gd)
    (out,) = call(couple, [(1, 3 * H)], [(8, 12 * S)], [raw, h3, g0, gx, gz, gd, k0, kx, kz, kd], 0.7)
    return top[None, None], out[None]


def solution(mesh):
    return jax.shard_map(
        local,
        mesh=mesh,
        in_specs=(P("gx", "gy", None, None), P("gx", "gy", None), P("gx", "gy", None), P()),
        out_specs=(P("gx", "gy", None, None), P("gx", "gy", None)),
        check_vma=False,
    )
```

time: 78.5 us -> 59 us (0.75); the launches traced: 77.5 us -> 58.8 us
  starting transfers between devices: 37.5 us -> 24.1 us
  waiting for transfers between devices: 14.5 us -> 8.95 us
  Pallas kernels: 20.6 us -> 22.2 us
  local copies, waits for them, and re-layouts: 2.65 us -> 1.38 us
    ppermute x28 -> x24, starting transfers between devices: 37.5 us -> 24.1 us  [send(): return lax.ppermute(value, ('gx', 'gy'), pairs)]
    ppermute x28 -> x24, waiting for transfers between devices: 14.5 us -> 8.95 us  [send(): return lax.ppermute(value, ('gx', 'gy'), pairs)]
    pallas_call x7 -> x11, Pallas kernels: 20.6 us -> 22.2 us  [call(): pl.pallas_call(body, out_shape=[jax.ShapeDtypeStruct(o, f32) for o in out...]
    unnamed x4 -> x2, local copies, waits for them, and re-layouts: 2.49 us -> 1.22 us
  transfers between devices with their start and end apart: 28 -> 24, of which waited for: 4 -> 10; matrix products, arithmetic and copies ran while one was open for 2% -> 3% of each run, Pallas kernels for 20% -> 32%
where the time goes in v1:
time: 59 us; the launch traced here: 58.8 us
  starting transfers between devices  24.1 us (41%)
  Pallas kernels  22.2 us (38%)
  waiting for transfers between devices  8.95 us (15%)
  other arithmetic  1.44 us (2%)
  local copies, waits for them, and re-layouts  1.38 us (2%)
  between operations  0.75 us (1%)
    ppermute x24, starting transfers between devices, send(): return lax.ppermute(value, ('gx', 'gy'), pairs)  24.1 us
    pallas_call x11, Pallas kernels, call(): pl.pallas_call(body, out_shape=[jax.ShapeDtypeStruct(o, f32) for o in out...  22.2 us
    ppermute x24, waiting for transfers between devices, send(): return lax.ppermute(value, ('gx', 'gy'), pairs)  8.95 us
    unnamed x2, local copies, waits for them, and re-layouts  1.22 us
  transfers between devices with their start and end apart: 24, of which 10 were waited for; matrix products, arithmetic and copies ran while one was open for 3% of the time, Pallas kernels for 32%

profile of v1, /device:TPU:1, one launch (start us, length us, event | category | flops | bytes accessed | tf_op | source)
XLA Modules:
  0.0 58.8 jit_solution(1946728594030971567)
XLA Ops:
  0.6 3.3 %collective-permute-start = (f32[512,512]{1,0:T(8,128)}, f32[512,512]{1,0:T(8,128)S(1)}, u32[]{:S(2)}, u32[]{:S(2)}) collective-permute-start(f32[512,512]{1,0:T(8,128)} %bitcast.6), channel_id=1, source_target_pairs={{0,16},{1,17},{2,18},{3,19},{4,20},{5,21},{6,22},{7,23},{8,24},{9,... | collective-permute-start | bytes 3145736 | tf_op jit(solution)/shard_map/ppermute | solution.py:396
  4.0 0.8 %select_reduce_fusion = f32[16]{0:T(128)S(1)} fusion(f32[8]{0:T(128)} %param.7, s32[16]{0:T(128)} %bitcast.10), kind=kLoop, calls=%fused_computation | loop fusion | flops 368 | bytes 160 | tf_op jit(solution)/shard_map/reduce_sum | solution.py:440
  4.7 0.1 broadcast_in_dim.6
  4.8 0.1 reshape.27
  4.9 0.7 %bitcast_multiply_fusion.hown = f32[1,512]{1,0:T(1,128)S(1)} fusion(f32[1,512]{1,0:T(1,128)S(1)} %reshape.27, f32[1,1,512]{2,1,0:T(1,128)} %param.5), kind=kLoop, calls=%fused_computation.2 | loop fusion | flops 512 | bytes 6144 | tf_op jit(solution)/shard_map/mul | solution.py:443
  5.6 0.0 collective-permute-start.1
  5.6 1.2 %copy-done = f32[1,1,512,512]{3,2,1,0:T(8,128)S(1)} copy-done((f32[1,1,512,512]{3,2,1,0:T(8,128)S(1)}, f32[1,1,512,512]{3,2,1,0:T(8,128)}, u32[]{:S(2)}) %copy-start) | copy-done | bytes 1048600
  6.8 2.9 %level1_interface.1 = (f32[128,128]{1,0:T(8,128)S(1)}, f32[256,256]{1,0:T(8,128)S(1)}, f32[136,256]{1,0:T(8,128)S(1)}) custom-call(f32[512,512]{1,0:T(8,128)S(1)} %bitcast.8, f32[512,512]{1,0:T(8,128)S(1)} %collective-permute-done.oth, f32[1,512]{1,0:T(1,128)S(1)} %bitcast_multiply_fusion.hown, f32[1,512]{1,0:T(1,128)S(1)} %collective-permute-done.1.hoth, ...), custom_call_target="tpu_custom_call" | custom-call | flops 2875000064 | tf_op jit(solution)/shard_map/level1_interface/pallas_call | solution.py:376
  9.8 0.1 collective-permute-start.2
  9.9 2.2 %level1_map.1 = (f32[768,896]{1,0:T(8,128)S(1)}, f32[128,512]{1,0:T(8,128)S(1)}, f32[64,768]{1,0:T(8,128)S(1)}) custom-call(f32[512,512]{1,0:T(8,128)S(1)} %bitcast.9, f32[512,512]{1,0:T(8,128)S(1)} %collective-permute-done.oth, f32[1,512]{1,0:T(1,128)S(1)} %bitcast_multiply_fusion.hown, f32[1,512]{1,0:T(1,128)S(1)} %collective-permute-done.1.hoth, ...), custom_call_target="tpu_custom_call" | custom-call | flops 2300000000 | tf_op jit(solution)/shard_map/level1_map/pallas_call | solution.py:376
  12.1 1.5 %collective-permute-start.4 = (f32[128,512]{1,0:T(8,128)S(1)}, f32[128,512]{1,0:T(8,128)S(1)}, u32[]{:S(2)}, u32[]{:S(2)}) collective-permute-start(f32[128,512]{1,0:T(8,128)S(1)} %get-tuple-element.43), channel_id=1, source_target_pairs={{0,1},{1,0},{2,3},{3,2},{4,5},{5,4},{6,7},{7,6},{8,9},{9,8},{10,11... | collective-permute-start | bytes 786440 | tf_op jit(solution)/shard_map/ppermute | solution.py:396
  13.6 1.0 %collective-permute-done.2.xin = f32[136,256]{1,0:T(8,128)S(1)} collective-permute-done((f32[136,256]{1,0:T(8,128)S(1)}, f32[136,256]{1,0:T(8,128)S(1)}, u32[]{:S(2)}, u32[]{:S(2)}) %collective-permute-start.2) | collective-permute-done | bytes 139296 | tf_op jit(solution)/shard_map/ppermute | solution.py:396
  14.6 2.0 %collective-permute-start.3 = (f32[136,256]{1,0:T(8,128)S(1)}, f32[136,256]{1,0:T(8,128)S(1)}, u32[]{:S(2)}, u32[]{:S(2)}) collective-permute-start(f32[136,256]{1,0:T(8,128)S(1)} %collective-permute-done.2.xin), channel_id=1, source_target_pairs={{0,16},{1,17},{2,18},{3,19},{4,20},{5,21},{6,22},{7,23},{8,24},{9,... | collective-permute-start | bytes 417800 | tf_op jit(solution)/shard_map/ppermute | solution.py:396
  16.5 1.0 %collective-permute-done.3.xic = f32[136,256]{1,0:T(8,128)S(1)} collective-permute-done((f32[136,256]{1,0:T(8,128)S(1)}, f32[136,256]{1,0:T(8,128)S(1)}, u32[]{:S(2)}, u32[]{:S(2)}) %collective-permute-start.3) | collective-permute-done | bytes 139296 | tf_op jit(solution)/shard_map/ppermute | solution.py:396
  17.5 4.1 %level2_inverse.1 = (f32[256,256]{1,0:T(8,128)S(1)}, f32[256,256]{1,0:T(8,128)S(1)}) custom-call(f32[256,256]{1,0:T(8,128)S(1)} %get-tuple-element.40.pii, f32[136,256]{1,0:T(8,128)S(1)} %collective-permute-done.2.xin, f32[136,256]{1,0:T(8,128)S(1)} %collective-permute-done.3.xic), custom_call_target="tpu_custom_call" | custom-call | flops 575000000 | tf_op jit(solution)/shard_map/level2_inverse/pallas_call | solution.py:376
  21.6 0.5 collective-permute-start.5
  22.1 0.2 collective-permute-start.10
  22.3 0.9 %collective-permute-done.5.xec = f32[128,512]{1,0:T(8,128)S(1)} collective-permute-done((f32[128,512]{1,0:T(8,128)S(1)}, f32[128,512]{1,0:T(8,128)S(1)}, u32[]{:S(2)}, u32[]{:S(2)}) %collective-permute-start.5) | collective-permute-done | bytes 262176 | tf_op jit(solution)/shard_map/ppermute | solution.py:396
  23.3 1.5 %level2_interface.1 = (f32[256,1152]{1,0:T(8,128)S(1)}, f32[128,1152]{1,0:T(8,128)S(1)}, f32[136,256]{1,0:T(8,128)S(1)}, f32[72,256]{1,0:T(8,128)S(1)}) custom-call(f32[256,256]{1,0:T(8,128)S(1)} %get-tuple-element.45.minv, f32[256,256]{1,0:T(8,128)S(1)} %get-tuple-element.46.gii, f32[768,896]{1,0:T(8,128)S(1)} %get-tuple-element.47.m1, ...), custom_call_target="tpu_custom_call" | custom-call | flops 1724999936 | tf_op jit(solution)/shard_map/level2_interface/pallas_call | solution.py:376
  24.8 0.1 collective-permute-start.6
  24.9 1.5 %collective-permute-start.7 = (f32[72,256]{1,0:T(8,128)S(1)}, f32[72,256]{1,0:T(8,128)S(1)}, u32[]{:S(2)}, u32[]{:S(2)}) collective-permute-start(f32[72,256]{1,0:T(8,128)S(1)} %get-tuple-element.51), channel_id=1, source_target_pairs={{0,33},{1,32},{2,35},{3,34},{4,37},{5,36},{6,39},{7,38},{8,41},{9,... | collective-permute-start | bytes 221192 | tf_op jit(solution)/shard_map/ppermute | solution.py:396
  26.3 0.6 level2_chip.1
  26.9 2.8 %collective-permute-done.7.a2 = f32[72,256]{1,0:T(8,128)S(1)} collective-permute-done((f32[72,256]{1,0:T(8,128)S(1)}, f32[72,256]{1,0:T(8,128)S(1)}, u32[]{:S(2)}, u32[]{:S(2)}) %collective-permute-start.7) | collective-permute-done | bytes 73760 | tf_op jit(solution)/shard_map/ppermute | solution.py:396
  29.7 2.8 %collective-permute-start.11 = (f32[64,768]{1,0:T(8,128)S(1)}, f32[64,768]{1,0:T(8,128)S(1)}, u32[]{:S(2)}, u32[]{:S(2)}) collective-permute-start(f32[64,768]{1,0:T(8,128)S(1)} %collective-permute-done.10.xln), channel_id=1, source_target_pairs={{0,16},{1,17},{2,18},{3,19},{4,20},{5,21},{6,22},{7,23},{8,24},{9,... | collective-permute-start | bytes 589832 | tf_op jit(solution)/shard_map/ppermute | solution.py:396
  32.5 0.0 collective-permute-start.8
  32.5 0.5 collective-permute-start.9
  33.0 0.6 collective-permute-done.11.xlc
  33.5 1.0 %level2_edge.1 = (f32[128,768]{1,0:T(8,128)S(1)}, f32[128,768]{1,0:T(8,128)S(1)}) custom-call(f32[256,1152]{1,0:T(8,128)S(1)} %get-tuple-element.52.t, f32[768,896]{1,0:T(8,128)S(1)} %get-tuple-element.47.m1, f32[128,1152]{1,0:T(8,128)S(1)} %get-tuple-element.49.y, f32[64,768]{1,0:T(8,128)S(1)} %collective-permute-done.10.xln, ...), custom_call_target="tpu_custom_call" | custom-call | flops 11500000 | tf_op jit(solution)/shard_map/level2_edge/pallas_call | solution.py:376
  34.5 0.1 collective-permute-start.12
  34.6 0.8 %collective-permute-start.15 = (f32[72,768]{1,0:T(8,128)S(1)}, f32[72,768]{1,0:T(8,128)S(1)}, u32[]{:S(2)}, u32[]{:S(2)}) collective-permute-start(f32[72,768]{1,0:T(8,128)S(1)} %get-tuple-element.68), channel_id=1, source_target_pairs={{0,1},{1,0},{2,3},{3,2},{4,5},{5,4},{6,7},{7,6},{8,9},{9,8},{10,11... | collective-permute-start | bytes 663560 | tf_op jit(solution)/shard_map/ppermute | solution.py:396
  35.5 4.8 %level3_inverse.1 = (f32[256,256]{1,0:T(8,128)S(1)}, f32[256,256]{1,0:T(8,128)S(1)}, f32[256,128]{1,0:T(8,128)S(1)}, f32[8,256]{1,0:T(8,128)S(1)}) custom-call(f32[128,1152]{1,0:T(8,128)S(1)} %get-tuple-element.49.y, f32[136,256]{1,0:T(8,128)S(1)} %collective-permute-done.6.a1, f32[136,256]{1,0:T(8,128)S(1)} %collective-permute-done.8.k1, ...), custom_call_target="tpu_custom_call" | custom-call | flops 23000000512 | tf_op jit(solution)/shard_map/level3_inverse/pallas_call | solution.py:376
  40.3 4.3 %collective-permute-start.13 = (f32[8,256]{1,0:T(8,128)S(1)}, f32[8,256]{1,0:T(8,128)S(1)}, u32[]{:S(2)}, u32[]{:S(2)}) collective-permute-start(f32[8,256]{1,0:T(8,128)S(1)} %get-tuple-element.65), channel_id=1, source_target_pairs={{0,224},{1,225},{2,226},{3,227},{4,228},{5,229},{6,230},{7,231},{8... | collective-permute-start | bytes 24584 | tf_op jit(solution)/shard_map/ppermute | solution.py:396
  44.6 1.6 %collective-permute-done.13.g0 = f32[8,256]{1,0:T(8,128)S(1)} collective-permute-done((f32[8,256]{1,0:T(8,128)S(1)}, f32[8,256]{1,0:T(8,128)S(1)}, u32[]{:S(2)}, u32[]{:S(2)}) %collective-permute-start.13) | collective-permute-done | bytes 8224 | tf_op jit(solution)/shard_map/ppermute | solution.py:396
  46.2 1.7 %collective-permute-start.14 = (f32[128,768]{1,0:T(8,128)S(1)}, f32[128,768]{1,0:T(8,128)S(1)}, u32[]{:S(2)}, u32[]{:S(2)}) collective-permute-start(f32[128,768]{1,0:T(8,128)S(1)} %collective-permute-done.12.be), channel_id=1, source_target_pairs={{0,16},{1,17},{2,18},{3,19},{4,20},{5,21},{6,22},{7,23},{8,24},{9,... | collective-permute-start | bytes 1179656 | tf_op jit(solution)/shard_map/ppermute | solution.py:396
  47.9 0.1 collective-permute-start.16
  48.0 0.5 collective-permute-start.17
  48.5 2.2 %collective-permute-start.19 = (f32[8,256]{1,0:T(8,128)S(1)}, f32[8,256]{1,0:T(8,128)S(1)}, u32[]{:S(2)}, u32[]{:S(2)}) collective-permute-start(f32[8,256]{1,0:T(8,128)S(1)} %collective-permute-done.13.g0), channel_id=1, source_target_pairs={{0,33},{1,32},{2,35},{3,34},{4,37},{5,36},{6,39},{7,38},{8,41},{9,... | collective-permute-start | bytes 24584 | tf_op jit(solution)/shard_map/ppermute | solution.py:396
  50.7 1.6 %level2_rows.1.rows = f32[192,1152]{1,0:T(8,128)S(1)} custom-call(f32[256,1152]{1,0:T(8,128)S(1)} %get-tuple-element.52.t, f32[768,896]{1,0:T(8,128)S(1)} %get-tuple-element.47.m1, f32[72,768]{1,0:T(8,128)S(1)} %collective-permute-done.15.rn, f32[72,768]{1,0:T(8,128)S(1)} %collective-permute-done.16.rc), custom_call_target="tpu_custom_call" | custom-call | flops 1724999936 | tf_op jit(solution)/shard_map/level2_rows/pallas_call | solution.py:376
  52.3 2.7 %level3_rows.1 = (f32[192,1536]{1,0:T(8,128)}, f32[192,1536]{1,0:T(8,128)S(1)}, f32[192,128]{1,0:T(8,128)S(1)}) custom-call(f32[256,256]{1,0:T(8,128)S(1)} %get-tuple-element.57.minv, f32[256,256]{1,0:T(8,128)S(1)} %get-tuple-element.58.gii, f32[256,128]{1,0:T(8,128)S(1)} %get-tuple-element.59.th, f32[128,1152]{1,0:T(8,128)S(1)} %get-tuple-element.49.y, ...), custom_call_target="tpu_custom_call" | custom-call | flops 2875000064 | tf_op jit(solution)/shard_map/level3_rows/pallas_call | solution.py:376
  55.0 1.4 %collective-permute-start.20 = (f32[8,256]{1,0:T(8,128)S(1)}, f32[8,256]{1,0:T(8,128)S(1)}, u32[]{:S(2)}, u32[]{:S(2)}) collective-permute-start(f32[8,256]{1,0:T(8,128)S(1)} %collective-permute-done.13.g0), channel_id=1, source_target_pairs={{0,16},{1,17},{2,18},{3,19},{4,20},{5,21},{6,22},{7,23},{8,24},{9,... | collective-permute-start | bytes 24584 | tf_op jit(solution)/shard_map/ppermute | solution.py:396
  56.4 0.1 collective-permute-start.21
  56.5 0.4 collective-permute-start.22
  56.9 0.1 collective-permute-start.23
  57.0 0.2 collective-permute-done.20.k0
  57.2 0.3 collective-permute-done.21.kx
  57.6 0.2 collective-permute-done.22.kz
  57.7 0.3 collective-permute-done.23.kd
  58.1 0.7 %couple.1 = f32[1,192]{1,0:T(1,128)} custom-call(f32[192,1536]{1,0:T(8,128)S(1)} %get-tuple-element.71.raw, f32[192,128]{1,0:T(8,128)S(1)} %get-tuple-element.73.h3, f32[8,256]{1,0:T(8,128)S(1)} %collective-permute-done.13.g0, f32[8,256]{1,0:T(8,128)S(1)} %collective-permute-done.17.gx, f32[8,256]{1,0:T(8,128)S(1)} %collective-permute-done.18.gz, ...), custom_call_target="tpu_custom_call" | custom-call | flops 805000000 | tf_op jit(solution)/shard_map/couple/pallas_call | solution.py:376
  (17 shorter events, 0.0 us)
Async XLA Ops:
  0.6 6.2 %collective-permute-start = (f32[512,512]{1,0:T(8,128)}, f32[512,512]{1,0:T(8,128)S(1)}, u32[]{:S(2)}, u32[]{:S(2)}) collective-permute-start(f32[512,512]{1,0:T(8,128)} %bitcast.6), channel_id=1, source_target_pairs={{0,16},{1,17},{2,18},{3,19},{4,20},{5,21},{6,22},{7,23},{8,24},{9,... | collective-permute-start | bytes 3145736 | tf_op jit(solution)/shard_map/ppermute | solution.py:396
  5.6 1.2 %collective-permute-start.1 = (f32[1,512]{1,0:T(1,128)S(1)}, f32[1,512]{1,0:T(1,128)S(1)}, u32[]{:S(2)}, u32[]{:S(2)}) collective-permute-start(f32[1,512]{1,0:T(1,128)S(1)} %bitcast_multiply_fusion.hown), channel_id=1, source_target_pairs={{0,16},{1,17},{2,18},{3,19},{4,20},{5,21},{6,22},{7,23},{8,24},{9,... | collective-permute-start | bytes 6152 | tf_op jit(solution)/shard_map/ppermute | solution.py:396
  5.6 1.2 %copy-start = (f32[1,1,512,512]{3,2,1,0:T(8,128)S(1)}, f32[1,1,512,512]{3,2,1,0:T(8,128)}, u32[]{:S(2)}) copy-start(f32[1,1,512,512]{3,2,1,0:T(8,128)} %param.4) | copy-start | bytes 3145732
  9.8 4.8 %collective-permute-start.2 = (f32[136,256]{1,0:T(8,128)S(1)}, f32[136,256]{1,0:T(8,128)S(1)}, u32[]{:S(2)}, u32[]{:S(2)}) collective-permute-start(f32[136,256]{1,0:T(8,128)S(1)} %get-tuple-element.41), channel_id=1, source_target_pairs={{0,1},{1,0},{2,3},{3,2},{4,5},{5,4},{6,7},{7,6},{8,9},{9,8},{10,11... | collective-permute-start | bytes 417800 | tf_op jit(solution)/shard_map/ppermute | solution.py:396
  12.1 9.5 %collective-permute-start.4 = (f32[128,512]{1,0:T(8,128)S(1)}, f32[128,512]{1,0:T(8,128)S(1)}, u32[]{:S(2)}, u32[]{:S(2)}) collective-permute-start(f32[128,512]{1,0:T(8,128)S(1)} %get-tuple-element.43), channel_id=1, source_target_pairs={{0,1},{1,0},{2,3},{3,2},{4,5},{5,4},{6,7},{7,6},{8,9},{9,8},{10,11... | collective-permute-start | bytes 786440 | tf_op jit(solution)/shard_map/ppermute | solution.py:396
  14.6 3.0 %collective-permute-start.3 = (f32[136,256]{1,0:T(8,128)S(1)}, f32[136,256]{1,0:T(8,128)S(1)}, u32[]{:S(2)}, u32[]{:S(2)}) collective-permute-start(f32[136,256]{1,0:T(8,128)S(1)} %collective-permute-done.2.xin), channel_id=1, source_target_pairs={{0,16},{1,17},{2,18},{3,19},{4,20},{5,21},{6,22},{7,23},{8,24},{9,... | collective-permute-start | bytes 417800 | tf_op jit(solution)/shard_map/ppermute | solution.py:396
  21.6 1.6 %collective-permute-start.5 = (f32[128,512]{1,0:T(8,128)S(1)}, f32[128,512]{1,0:T(8,128)S(1)}, u32[]{:S(2)}, u32[]{:S(2)}) collective-permute-start(f32[128,512]{1,0:T(8,128)S(1)} %collective-permute-done.4.xen), channel_id=1, source_target_pairs={{0,16},{1,17},{2,18},{3,19},{4,20},{5,21},{6,22},{7,23},{8,24},{9,... | collective-permute-start | bytes 786440 | tf_op jit(solution)/shard_map/ppermute | solution.py:396
  22.1 7.6 %collective-permute-start.10 = (f32[64,768]{1,0:T(8,128)S(1)}, f32[64,768]{1,0:T(8,128)S(1)}, u32[]{:S(2)}, u32[]{:S(2)}) collective-permute-start(f32[64,768]{1,0:T(8,128)S(1)} %get-tuple-element.61), channel_id=1, source_target_pairs={{0,1},{1,0},{2,3},{3,2},{4,5},{5,4},{6,7},{7,6},{8,9},{9,8},{10,11... | collective-permute-start | bytes 589832 | tf_op jit(solution)/shard_map/ppermute | solution.py:396
  24.8 4.9 %collective-permute-start.6 = (f32[136,256]{1,0:T(8,128)S(1)}, f32[136,256]{1,0:T(8,128)S(1)}, u32[]{:S(2)}, u32[]{:S(2)}) collective-permute-start(f32[136,256]{1,0:T(8,128)S(1)} %get-tuple-element.50), channel_id=1, source_target_pairs={{0,1},{1,0},{2,3},{3,2},{4,5},{5,4},{6,7},{7,6},{8,9},{9,8},{10,11... | collective-permute-start | bytes 417800 | tf_op jit(solution)/shard_map/ppermute | solution.py:396
  24.9 4.8 %collective-permute-start.7 = (f32[72,256]{1,0:T(8,128)S(1)}, f32[72,256]{1,0:T(8,128)S(1)}, u32[]{:S(2)}, u32[]{:S(2)}) collective-permute-start(f32[72,256]{1,0:T(8,128)S(1)} %get-tuple-element.51), channel_id=1, source_target_pairs={{0,33},{1,32},{2,35},{3,34},{4,37},{5,36},{6,39},{7,38},{8,41},{9,... | collective-permute-start | bytes 221192 | tf_op jit(solution)/shard_map/ppermute | solution.py:396
  29.7 3.9 %collective-permute-start.11 = (f32[64,768]{1,0:T(8,128)S(1)}, f32[64,768]{1,0:T(8,128)S(1)}, u32[]{:S(2)}, u32[]{:S(2)}) collective-permute-start(f32[64,768]{1,0:T(8,128)S(1)} %collective-permute-done.10.xln), channel_id=1, source_target_pairs={{0,16},{1,17},{2,18},{3,19},{4,20},{5,21},{6,22},{7,23},{8,24},{9,... | collective-permute-start | bytes 589832 | tf_op jit(solution)/shard_map/ppermute | solution.py:396
  32.5 3.0 %collective-permute-start.8 = (f32[136,256]{1,0:T(8,128)S(1)}, f32[136,256]{1,0:T(8,128)S(1)}, u32[]{:S(2)}, u32[]{:S(2)}) collective-permute-start(f32[136,256]{1,0:T(8,128)S(1)} %collective-permute-done.6.a1), channel_id=1, source_target_pairs={{0,16},{1,17},{2,18},{3,19},{4,20},{5,21},{6,22},{7,23},{8,24},{9,... | collective-permute-start | bytes 417800 | tf_op jit(solution)/shard_map/ppermute | solution.py:396
  32.5 3.0 %collective-permute-start.9 = (f32[72,256]{1,0:T(8,128)S(1)}, f32[72,256]{1,0:T(8,128)S(1)}, u32[]{:S(2)}, u32[]{:S(2)}) collective-permute-start(f32[72,256]{1,0:T(8,128)S(1)} %collective-permute-done.7.a2), channel_id=1, source_target_pairs={{0,16},{1,17},{2,18},{3,19},{4,20},{5,21},{6,22},{7,23},{8,24},{9,... | collective-permute-start | bytes 221192 | tf_op jit(solution)/shard_map/ppermute | solution.py:396
  34.5 11.7 %collective-permute-start.12 = (f32[128,768]{1,0:T(8,128)S(1)}, f32[128,768]{1,0:T(8,128)S(1)}, u32[]{:S(2)}, u32[]{:S(2)}) collective-permute-start(f32[128,768]{1,0:T(8,128)S(1)} %get-tuple-element.64), channel_id=1, source_target_pairs={{0,32},{1,33},{2,34},{3,35},{4,36},{5,37},{6,38},{7,39},{8,40},{9,... | collective-permute-start | bytes 1179656 | tf_op jit(solution)/shard_map/ppermute | solution.py:396
  34.6 13.3 %collective-permute-start.15 = (f32[72,768]{1,0:T(8,128)S(1)}, f32[72,768]{1,0:T(8,128)S(1)}, u32[]{:S(2)}, u32[]{:S(2)}) collective-permute-start(f32[72,768]{1,0:T(8,128)S(1)} %get-tuple-element.68), channel_id=1, source_target_pairs={{0,1},{1,0},{2,3},{3,2},{4,5},{5,4},{6,7},{7,6},{8,9},{9,8},{10,11... | collective-permute-start | bytes 663560 | tf_op jit(solution)/shard_map/ppermute | solution.py:396
  40.3 5.9 %collective-permute-start.13 = (f32[8,256]{1,0:T(8,128)S(1)}, f32[8,256]{1,0:T(8,128)S(1)}, u32[]{:S(2)}, u32[]{:S(2)}) collective-permute-start(f32[8,256]{1,0:T(8,128)S(1)} %get-tuple-element.65), channel_id=1, source_target_pairs={{0,224},{1,225},{2,226},{3,227},{4,228},{5,229},{6,230},{7,231},{8... | collective-permute-start | bytes 24584 | tf_op jit(solution)/shard_map/ppermute | solution.py:396
  46.2 6.1 %collective-permute-start.14 = (f32[128,768]{1,0:T(8,128)S(1)}, f32[128,768]{1,0:T(8,128)S(1)}, u32[]{:S(2)}, u32[]{:S(2)}) collective-permute-start(f32[128,768]{1,0:T(8,128)S(1)} %collective-permute-done.12.be), channel_id=1, source_target_pairs={{0,16},{1,17},{2,18},{3,19},{4,20},{5,21},{6,22},{7,23},{8,24},{9,... | collective-permute-start | bytes 1179656 | tf_op jit(solution)/shard_map/ppermute | solution.py:396
  47.9 2.7 %collective-permute-start.16 = (f32[72,768]{1,0:T(8,128)S(1)}, f32[72,768]{1,0:T(8,128)S(1)}, u32[]{:S(2)}, u32[]{:S(2)}) collective-permute-start(f32[72,768]{1,0:T(8,128)S(1)} %collective-permute-done.15.rn), channel_id=1, source_target_pairs={{0,16},{1,17},{2,18},{3,19},{4,20},{5,21},{6,22},{7,23},{8,24},{9,... | collective-permute-start | bytes 663560 | tf_op jit(solution)/shard_map/ppermute | solution.py:396
  48.0 7.0 %collective-permute-start.17 = (f32[8,256]{1,0:T(8,128)S(1)}, f32[8,256]{1,0:T(8,128)S(1)}, u32[]{:S(2)}, u32[]{:S(2)}) collective-permute-start(f32[8,256]{1,0:T(8,128)S(1)} %collective-permute-done.13.g0), channel_id=1, source_target_pairs={{0,1},{1,0},{2,3},{3,2},{4,5},{5,4},{6,7},{7,6},{8,9},{9,8},{10,11... | collective-permute-start | bytes 24584 | tf_op jit(solution)/shard_map/ppermute | solution.py:396
  48.5 6.6 %collective-permute-start.18 = (f32[8,256]{1,0:T(8,128)S(1)}, f32[8,256]{1,0:T(8,128)S(1)}, u32[]{:S(2)}, u32[]{:S(2)}) collective-permute-start(f32[8,256]{1,0:T(8,128)S(1)} %collective-permute-done.13.g0), channel_id=1, source_target_pairs={{0,32},{1,33},{2,34},{3,35},{4,36},{5,37},{6,38},{7,39},{8,40},{9,... | collective-permute-start | bytes 24584 | tf_op jit(solution)/shard_map/ppermute | solution.py:396
  48.5 6.6 %collective-permute-start.19 = (f32[8,256]{1,0:T(8,128)S(1)}, f32[8,256]{1,0:T(8,128)S(1)}, u32[]{:S(2)}, u32[]{:S(2)}) collective-permute-start(f32[8,256]{1,0:T(8,128)S(1)} %collective-permute-done.13.g0), channel_id=1, source_target_pairs={{0,33},{1,32},{2,35},{3,34},{4,37},{5,36},{6,39},{7,38},{8,41},{9,... | collective-permute-start | bytes 24584 | tf_op jit(solution)/shard_map/ppermute | solution.py:396
  55.0 2.2 %collective-permute-start.20 = (f32[8,256]{1,0:T(8,128)S(1)}, f32[8,256]{1,0:T(8,128)S(1)}, u32[]{:S(2)}, u32[]{:S(2)}) collective-permute-start(f32[8,256]{1,0:T(8,128)S(1)} %collective-permute-done.13.g0), channel_id=1, source_target_pairs={{0,16},{1,17},{2,18},{3,19},{4,20},{5,21},{6,22},{7,23},{8,24},{9,... | collective-permute-start | bytes 24584 | tf_op jit(solution)/shard_map/ppermute | solution.py:396
  56.4 1.2 %collective-permute-start.21 = (f32[8,256]{1,0:T(8,128)S(1)}, f32[8,256]{1,0:T(8,128)S(1)}, u32[]{:S(2)}, u32[]{:S(2)}) collective-permute-start(f32[8,256]{1,0:T(8,128)S(1)} %collective-permute-done.17.gx), channel_id=1, source_target_pairs={{0,16},{1,17},{2,18},{3,19},{4,20},{5,21},{6,22},{7,23},{8,24},{9,... | collective-permute-start | bytes 24584 | tf_op jit(solution)/shard_map/ppermute | solution.py:396
  56.5 1.2 %collective-permute-start.22 = (f32[8,256]{1,0:T(8,128)S(1)}, f32[8,256]{1,0:T(8,128)S(1)}, u32[]{:S(2)}, u32[]{:S(2)}) collective-permute-start(f32[8,256]{1,0:T(8,128)S(1)} %collective-permute-done.18.gz), channel_id=1, source_target_pairs={{0,16},{1,17},{2,18},{3,19},{4,20},{5,21},{6,22},{7,23},{8,24},{9,... | collective-permute-start | bytes 24584 | tf_op jit(solution)/shard_map/ppermute | solution.py:396
  56.9 1.2 %collective-permute-start.23 = (f32[8,256]{1,0:T(8,128)S(1)}, f32[8,256]{1,0:T(8,128)S(1)}, u32[]{:S(2)}, u32[]{:S(2)}) collective-permute-start(f32[8,256]{1,0:T(8,128)S(1)} %collective-permute-done.19.gd), channel_id=1, source_target_pairs={{0,16},{1,17},{2,18},{3,19},{4,20},{5,21},{6,22},{7,23},{8,24},{9,... | collective-permute-start | bytes 24584 | tf_op jit(solution)/shard_map/ppermute | solution.py:396

commit v2 on v1

--- a/solution.py
+++ b/solution.py
@@ -52,7 +52,7 @@
     ks = split(K)
     X = eye + K
     power = mm(ks[0], ks[0])
-    steps = 5
+    steps = 6
     for j in range(1, steps + 1):
         pb = power.astype(bf16)
         if j < steps:
@@ -61,10 +61,9 @@
             power = both[n:]
         else:
             X = X + mm(X.astype(bf16), pb)
-    for _ in range(2):
-        xs = split(X)
-        residual = eye - X + dot3s(ks, xs)
-        X = X + mm(xs[0], residual.astype(bf16))
+    xs = split(X)
+    residual = eye - X + dot3s(ks, xs)
+    X = X + mm(xs[0], residual.astype(bf16))
     residual = eye - X + dot_full(K, X)
     return X + dot3(X, residual)
 
@@ -163,9 +162,33 @@
     gii[...] = dot3(X, qii[...])
 
 
-def level2_interface(minv, gii, m1, xin, xic, xen, xec, t, y, yi, yh, qe):
+def level2_interface(minv, gii, m1, xin, xic, xen, xec, yi, yh, yd, qe):
+    c, s, r = roles()
+    d = 1 - c
+    H = S // 2
+    inner = at(2 * (2 - s), 2 * S)
+    side = at(1 - r, S)
+    A = dot3(gii[...], jnp.concatenate([m1[inner, side], m1[inner, 6 * S :]], 1))
+    qe[at(c, S), :S] = xen[:, side]
+    qe[at(d, S), :S] = xec[:, side]
+    qe[at(c, S), S:] = as_columns(xin[S : S + 1, :S])
+    qe[at(d, S), S:] = as_columns(xic[S : S + 1, :S])
+    B = dot3(minv[...], qe[...])
+    D = dot3(m1[side, inner], jnp.concatenate([A[:, :S], B[:, :S], B[:, S:] - A[:, S:]], 1))
+    data = m1[side, 6 * S :] - D[:, 2 * S :]
+    yd[...] = data
+    yi[:S, at(s, S)] = m1[side, side] + D[:, :S]
+    yi[:S, at(1 - s, S)] = -D[:, S : 2 * S]
+    yi[S:, :S] = as_rows(data)
+    yi[S:, S:] = jnp.zeros((8, S), f32)
+    yh[:H] = yi[at(c, H, H), :]
+    yh[H:] = yi[S:]
+
+
+def level2_rest(minv, gii, m1, xin, xic, xen, xec, t, ye, chip, rr, qe):
     c, s, r = roles()
     o = 1 - s
+    H = S // 2
     inner = at(2 * (2 - s), 2 * S)
     outer = at(2 * (1 + s), 2 * S)
     P_e = jnp.concatenate([m1[inner, : 2 * S], m1[inner, outer], m1[inner, 6 * S :]], 1)
@@ -183,23 +206,9 @@
     t[:, at(4 + 2 * o, 2 * S)] = B[:, 2 * S : 4 * S]
     t[:, 8 * S :] = B[:, 4 * S :] - A[:, 4 * S :]
     row = at(1 - r, S)
-    y[...] = -dot3(m1[row, inner], t[...])
-    y[:, at(s, S)] += m1[row, :S]
-    y[:, at(2 + s, S)] += m1[row, S : 2 * S]
-    y[:, at(4 + 2 * s, 2 * S)] += m1[row, outer]
-    y[:, 8 * S :] += m1[row, 6 * S :]
-    H = S // 2
-    yi[:S] = y[:, at(2 * (1 - r), 2 * S)]
-    yi[S:, :S] = as_rows(y[:, 8 * S :])
-    yi[S:, S:] = jnp.zeros((8, S), f32)
-    yh[:H] = yi[at(c, H, H), :]
-    yh[H:] = yi[S:]
-
-
-def level2_chip(t, m1, chip, rr):
-    c, s, r = roles()
-    inner = at(2 * (2 - s), 2 * S)
-    outer = at(2 * (1 + s), 2 * S)
+    ye[...] = -dot3(m1[row, inner], jnp.concatenate([t[:, at(2 * r, 2 * S)], t[:, 4 * S : 8 * S]], 1))
+    ye[:, at(s, S)] += m1[row, at(r, S)]
+    ye[:, at(2 + 2 * s, 2 * S)] += m1[row, outer]
     P_ei = jnp.concatenate([m1[at(r, S), inner], m1[outer, inner]], 0)
     T_i = jnp.concatenate([t[:, at(2 * (1 - r), 2 * S)], t[:, 8 * S :]], 1)
     chip[...] = -dot3(P_ei, T_i)
@@ -207,7 +216,6 @@
     chip[S:, at(s, S)] += m1[outer, at(1 - r, S)]
     chip[:S, 2 * S :] += m1[at(r, S), 6 * S :]
     chip[S:, 2 * S :] += m1[outer, 6 * S :]
-    H = S // 2
     first = jnp.where(c == 0, jnp.where(s == 0, 4, 2 * r), jnp.where(s == 0, 5, 8))
     lines = at(first, H, H)
     rr[:H] = m1[lines, : 6 * S]
@@ -215,7 +223,7 @@
     rr[H:, S:] = jnp.zeros((8, 5 * S), f32)
 
 
-def level2_edge(t, m1, y, xln, xlc, be, yx, row):
+def level2_edge(t, m1, ye, xln, xlc, be, yx, row):
     c, s, r = roles()
     o = 1 - s
     H = S // 2
@@ -233,8 +241,7 @@
 
     @pl.when(c == 0)
     def _():
-        be[:, : 2 * S] = y[:, at(2 * r, 2 * S)]
-        be[:, 2 * S :] = y[:, 4 * S : 8 * S]
+        be[...] = ye[...]
 
     @pl.when(c == 1)
     def _():
@@ -298,19 +305,19 @@
     rows[:, 8 * S :] += data
 
 
-def level3_inverse(y, a1, k1, a2, k2, chip, minv, gii, th, hs, pii, qii, pq):
+def level3_inverse(yi, yd, a1, k1, a2, k2, chip, minv, gii, th, hs, pii, qii, pq):
     c, s, r = roles()
     o = 1 - s
     d = 1 - c
     H = S // 2
     x = jnp.where(c == 0, a1[...], k1[...])
     z = jnp.where(c == 0, k1[...], a1[...])
-    pii[at(s, S), :] = y[:, at(2 * (1 - r), 2 * S)]
+    pii[at(s, S), :] = yi[:S]
     pii[at(o, S), :] = x[:S]
     qii[at(s, S), :] = z[:S]
     qii[at(2 * o + c, H, H), :] = a2[:H]
     qii[at(2 * o + d, H, H), :] = k2[:H]
-    pq[at(s, S), :S] = y[:, 8 * S :]
+    pq[at(s, S), :S] = yd[...]
     pq[at(o, S), :S] = as_columns(x[S : S + 1, :S])
     pq[at(s, S), S:] = as_columns(z[S : S + 1, :S])
     pq[at(o, S), S:] = as_columns(a2[H : H + 1, :S])
@@ -326,11 +333,10 @@
     hs[:, S:] = as_rows(h3[2 * S :])
 
 
-def level3_rows(minv, gii, th, y, yx, be, kb, rows, top, raw, h3, pe, qe):
+def level3_rows(minv, gii, th, ye, yx, be, kb, rows, top, raw, h3, pe, qe):
     c, s, r = roles()
     o = 1 - s
-    pe[at(s, S), : 2 * S] = y[:, at(2 * r, 2 * S)]
-    pe[at(s, S), 2 * S :] = y[:, 4 * S : 8 * S]
+    pe[at(s, S), :] = ye[...]
     pe[at(o, S), :] = yx[...]
     qe[at(s, S), :] = jnp.where(c == 0, be[...], kb[...])
     qe[at(o, S), :] = jnp.where(c == 0, kb[...], be[...])
@@ -347,7 +353,7 @@
     h3[...] = rows[:, 8 * S :] - dot3s(R_ei, split(th[...]))
 
 
-def couple(raw, h3, g0, gx, gz, gd, k0, kx, kz, kd, out, inc):
+def couple(raw, h3, mine, core, out, inc):
     c, s, r = roles()
     box_x = lax.axis_index("gx") // 4
     box_y = lax.axis_index("gy") // 2
@@ -357,9 +363,10 @@
     edge_y = (box_y == 0) | (box_y == last_y)
     at_x = jnp.where(box_x == 0, 0, 1)
     at_y = jnp.where(box_y == 0, 0, 1)
-    for mine, core, ss, rr in ((g0, k0, s, r), (gx, kx, 1 - s, r), (gz, kz, s, 1 - r), (gd, kd, 1 - s, 1 - r)):
-        side = jnp.where(c == 0, mine[:, :S], core[:, :S])
-        pair = jnp.where(c == 0, core[...], mine[...])
+    for n, (ss, rr) in enumerate(((s, r), (1 - s, r), (s, 1 - r), (1 - s, 1 - r))):
+        lines = slice(8 * n, 8 * n + 8)
+        side = jnp.where(c == 0, mine[lines, :S], core[lines, :S])
+        pair = jnp.where(c == 0, core[lines, :], mine[lines, :])
         inc[:, at(6 * rr + ss, S)] = jnp.where(edge_x & (at_x == rr), 0.0, side)
         inc[:, at(6 * rr + 2 + 2 * ss, 2 * S)] = jnp.where(edge_y & (at_y == ss), 0.0, pair)
     lane = lax.broadcasted_iota(jnp.int32, (h3.shape[0], S), 1)
@@ -455,43 +462,50 @@
     minv, gii = call(level2_inverse, [(2 * S, 2 * S)] * 2, [(2 * S, 2 * S)], [pii, xin, xic], 0.5)
     xec = over_core(after(xen, minv))
     xln = over_x(after(xl, xen, minv))
-    t, y, yi, yh = call(
+    yi, yh, yd = call(
         level2_interface,
-        [(2 * S, 9 * S), (S, 9 * S), (S + 8, 2 * S), (H + 8, 2 * S)],
+        [(S + 8, 2 * S), (H + 8, 2 * S), (S, S)],
+        [(2 * S, 2 * S)],
+        [minv, gii, m1, xin, xic, xen, xec],
+        1.0,
+    )
+    a1, a2 = over_x_or_z(yi), over_xz(yh)
+    t, ye, chip, rr = call(
+        level2_rest,
+        [(2 * S, 9 * S), (S, 6 * S), (3 * S, 3 * S), (H + 8, 6 * S)],
         [(2 * S, 5 * S)],
-        [minv, gii, m1, xin, xic, xen, xec],
-        1.5,
-    )
-    a1, a2 = over_x_or_z(yi), over_xz(yh)
-    chip, rr = call(level2_chip, [(3 * S, 3 * S), (H + 8, 6 * S)], [], [t, m1], 0.01)
+        [after(minv, yd), gii, m1, xin, xic, xen, xec],
+        0.01,
+    )
     a1, a2, chip = lax.optimization_barrier((a1, a2, chip))
     k1, k2 = over_core(a1), over_core(a2)
     xlc = over_core(after(xln, chip))
-    be, yx = call(level2_edge, [(S, 6 * S)] * 2, [(S, 6 * S)], [t, m1, y, xln, xlc], 0.01)
+    be, yx = call(level2_edge, [(S, 6 * S)] * 2, [(S, 6 * S)], [t, m1, ye, xln, xlc], 0.01)
     bn = over_z(be)
     rn = over_x(after(rr, be))
     minv3, gii3, th, hs = call(
         level3_inverse,
         [(2 * S, 2 * S), (2 * S, 2 * S), (2 * S, S), (8, 2 * S)],
         [(2 * S, 2 * S)] * 3,
-        [y, a1, k1, a2, k2, chip],
+        [yi, yd, a1, k1, a2, k2, chip],
         20.0,
     )
     g0 = over_edge(hs)
-    rc = over_core(after(rn, g0))
-    kb = over_core(after(bn, g0))
+    rc = over_core(after(rn, minv3))
     (rows,) = call(level2_rows, [(3 * H, 9 * S)], [(3 * H, 7 * S)], [t, m1, rn, rc], 1.5)
+    bn, g0, rows = lax.optimization_barrier((bn, g0, rows))
+    kb = over_core(bn)
     gx, gz, gd = over_x(g0), over_z(g0), over_xz(g0)
     top, raw, h3 = call(
         level3_rows,
         [(3 * H, 12 * S), (3 * H, 12 * S), (3 * H, S)],
         [(2 * S, 6 * S)] * 2,
-        [minv3, gii3, th, y, yx, bn, kb, rows],
+        [minv3, gii3, th, ye, yx, bn, kb, rows],
         2.5,
     )
     g0, gx, gz, gd, h3 = lax.optimization_barrier((g0, gx, gz, gd, h3))
-    k0, kx, kz, kd = over_core(g0), over_core(gx), over_core(gz), over_core(gd)
-    (out,) = call(couple, [(1, 3 * H)], [(8, 12 * S)], [raw, h3, g0, gx, gz, gd, k0, kx, kz, kd], 0.7)
+    edges = jnp.concatenate([g0, gx, gz, gd], 0)
+    (out,) = call(couple, [(1, 3 * H)], [(8, 12 * S)], [raw, h3, edges, over_core(edges)], 0.7)
     return top[None, None], out[None]
 
 

time: 59 us -> 57 us (0.966)
  waiting for transfers between devices: 8.95 us -> 6.72 us
  starting transfers between devices: 24.1 us -> 24.8 us
    ppermute x24 -> x21, waiting for transfers between devices: 8.95 us -> 6.72 us  [send(): return lax.ppermute(value, ('gx', 'gy'), pairs)]
    ppermute x24 -> x21, starting transfers between devices: 24.1 us -> 24.8 us  [send(): return lax.ppermute(value, ('gx', 'gy'), pairs)]
    unnamed x2 -> x5, local copies, waits for them, and re-layouts: 1.22 us -> 1.23 us
  transfers between devices with their start and end apart: 24 -> 21, of which waited for: 10 -> 7; matrix products, arithmetic and copies ran while one was open for 3% -> 3% of each run, Pallas kernels for 32% -> 32%
where the time goes in v2:
time: 57 us; the launch traced here: 56.9 us
  starting transfers between devices  24.8 us (44%)
  Pallas kernels  21.7 us (38%)
  waiting for transfers between devices  6.72 us (12%)
  other arithmetic  1.44 us (3%)
  local copies, waits for them, and re-layouts  1.39 us (2%)
  between operations  0.77 us (1%)
    ppermute x21, starting transfers between devices, send(): return lax.ppermute(value, ('gx', 'gy'), pairs)  24.8 us
    pallas_call x11, Pallas kernels, call(): pl.pallas_call(body, out_shape=[jax.ShapeDtypeStruct(o, f32) for o in out...  21.7 us
    ppermute x21, waiting for transfers between devices, send(): return lax.ppermute(value, ('gx', 'gy'), pairs)  6.72 us
    unnamed x5, local copies, waits for them, and re-layouts  1.23 us
  transfers between devices with their start and end apart: 21, of which 7 were waited for; matrix products, arithmetic and copies ran while one was open for 3% of the time, Pallas kernels for 32%

profile of v2, /device:TPU:1, one launch (start us, length us, event | category | flops | bytes accessed | tf_op | source)
XLA Modules:
  0.0 56.9 jit_solution(14661780972330512403)
XLA Ops:
  0.6 3.3 %collective-permute-start = (f32[512,512]{1,0:T(8,128)}, f32[512,512]{1,0:T(8,128)S(1)}, u32[]{:S(2)}, u32[]{:S(2)}) collective-permute-start(f32[512,512]{1,0:T(8,128)} %bitcast.6), channel_id=1, source_target_pairs={{0,16},{1,17},{2,18},{3,19},{4,20},{5,21},{6,22},{7,23},{8,24},{9,... | collective-permute-start | bytes 3145736 | tf_op jit(solution)/shard_map/ppermute | solution.py:403
  4.0 0.8 %select_reduce_fusion = f32[16]{0:T(128)S(1)} fusion(f32[8]{0:T(128)} %param.7, s32[16]{0:T(128)} %bitcast.10), kind=kLoop, calls=%fused_computation.4 | loop fusion | flops 368 | bytes 160 | tf_op jit(solution)/shard_map/reduce_sum | solution.py:447
  4.7 0.1 broadcast_in_dim.6
  4.8 0.1 reshape.27
  4.9 0.7 %bitcast_multiply_fusion.hown = f32[1,512]{1,0:T(1,128)S(1)} fusion(f32[1,512]{1,0:T(1,128)S(1)} %reshape.27, f32[1,1,512]{2,1,0:T(1,128)} %param.5), kind=kLoop, calls=%fused_computation.6 | loop fusion | flops 512 | bytes 6144 | tf_op jit(solution)/shard_map/mul | solution.py:450
  5.6 0.0 collective-permute-start.1
  5.6 1.2 %copy-done = f32[1,1,512,512]{3,2,1,0:T(8,128)S(1)} copy-done((f32[1,1,512,512]{3,2,1,0:T(8,128)S(1)}, f32[1,1,512,512]{3,2,1,0:T(8,128)}, u32[]{:S(2)}) %copy-start) | copy-done | bytes 1048600
  6.8 2.8 %level1_interface.1 = (f32[128,128]{1,0:T(8,128)S(1)}, f32[256,256]{1,0:T(8,128)S(1)}, f32[136,256]{1,0:T(8,128)S(1)}) custom-call(f32[512,512]{1,0:T(8,128)S(1)} %bitcast.8, f32[512,512]{1,0:T(8,128)S(1)} %collective-permute-done.oth, f32[1,512]{1,0:T(1,128)S(1)} %bitcast_multiply_fusion.hown, f32[1,512]{1,0:T(1,128)S(1)} %collective-permute-done.1.hoth, ...), custom_call_target="tpu_custom_call" | custom-call | flops 2875000064 | tf_op jit(solution)/shard_map/level1_interface/pallas_call | solution.py:383
  9.6 0.1 collective-permute-start.2
  9.7 2.2 %level1_map.1 = (f32[768,896]{1,0:T(8,128)S(1)}, f32[128,512]{1,0:T(8,128)S(1)}, f32[64,768]{1,0:T(8,128)S(1)}) custom-call(f32[512,512]{1,0:T(8,128)S(1)} %bitcast.9, f32[512,512]{1,0:T(8,128)S(1)} %collective-permute-done.oth, f32[1,512]{1,0:T(1,128)S(1)} %bitcast_multiply_fusion.hown, f32[1,512]{1,0:T(1,128)S(1)} %collective-permute-done.1.hoth, ...), custom_call_target="tpu_custom_call" | custom-call | flops 2300000000 | tf_op jit(solution)/shard_map/level1_map/pallas_call | solution.py:383
  11.9 1.5 %collective-permute-start.4 = (f32[128,512]{1,0:T(8,128)S(1)}, f32[128,512]{1,0:T(8,128)S(1)}, u32[]{:S(2)}, u32[]{:S(2)}) collective-permute-start(f32[128,512]{1,0:T(8,128)S(1)} %get-tuple-element.47), channel_id=1, source_target_pairs={{0,1},{1,0},{2,3},{3,2},{4,5},{5,4},{6,7},{7,6},{8,9},{9,8},{10,11... | collective-permute-start | bytes 786440 | tf_op jit(solution)/shard_map/ppermute | solution.py:403
  13.4 1.0 %collective-permute-done.2.xin = f32[136,256]{1,0:T(8,128)S(1)} collective-permute-done((f32[136,256]{1,0:T(8,128)S(1)}, f32[136,256]{1,0:T(8,128)S(1)}, u32[]{:S(2)}, u32[]{:S(2)}) %collective-permute-start.2) | collective-permute-done | bytes 139296 | tf_op jit(solution)/shard_map/ppermute | solution.py:403
  14.4 2.0 %collective-permute-start.3 = (f32[136,256]{1,0:T(8,128)S(1)}, f32[136,256]{1,0:T(8,128)S(1)}, u32[]{:S(2)}, u32[]{:S(2)}) collective-permute-start(f32[136,256]{1,0:T(8,128)S(1)} %collective-permute-done.2.xin), channel_id=1, source_target_pairs={{0,16},{1,17},{2,18},{3,19},{4,20},{5,21},{6,22},{7,23},{8,24},{9,... | collective-permute-start | bytes 417800 | tf_op jit(solution)/shard_map/ppermute | solution.py:403
  16.4 1.0 %collective-permute-done.3.xic = f32[136,256]{1,0:T(8,128)S(1)} collective-permute-done((f32[136,256]{1,0:T(8,128)S(1)}, f32[136,256]{1,0:T(8,128)S(1)}, u32[]{:S(2)}, u32[]{:S(2)}) %collective-permute-start.3) | collective-permute-done | bytes 139296 | tf_op jit(solution)/shard_map/ppermute | solution.py:403
  17.4 3.7 %level2_inverse.1 = (f32[256,256]{1,0:T(8,128)S(1)}, f32[256,256]{1,0:T(8,128)S(1)}) custom-call(f32[256,256]{1,0:T(8,128)S(1)} %get-tuple-element.44.pii, f32[136,256]{1,0:T(8,128)S(1)} %collective-permute-done.2.xin, f32[136,256]{1,0:T(8,128)S(1)} %collective-permute-done.3.xic), custom_call_target="tpu_custom_call" | custom-call | flops 575000000 | tf_op jit(solution)/shard_map/level2_inverse/pallas_call | solution.py:383
  21.1 0.0 collective-permute-done.4.xen
  21.2 0.5 collective-permute-start.5
  21.6 0.6 collective-permute-start.10
  22.2 0.6 %collective-permute-done.5.xec = f32[128,512]{1,0:T(8,128)S(1)} collective-permute-done((f32[128,512]{1,0:T(8,128)S(1)}, f32[128,512]{1,0:T(8,128)S(1)}, u32[]{:S(2)}, u32[]{:S(2)}) %collective-permute-start.5) | collective-permute-done | bytes 262176 | tf_op jit(solution)/shard_map/ppermute | solution.py:403
  22.8 0.8 %level2_interface.1 = (f32[136,256]{1,0:T(8,128)S(1)}, f32[72,256]{1,0:T(8,128)S(1)}, f32[128,128]{1,0:T(8,128)S(1)}) custom-call(f32[256,256]{1,0:T(8,128)S(1)} %get-tuple-element.56.minv, f32[256,256]{1,0:T(8,128)S(1)} %get-tuple-element.50.gii, f32[768,896]{1,0:T(8,128)S(1)} %get-tuple-element.51.m1, f32[136,256]{1,0:T(8,128)S(1)} %collective-permute-done.2.xin, ...), custom_call_target="tpu_custom_call" | custom-call | flops 1150000000 | tf_op jit(solution)/shard_map/level2_interface/pallas_call | solution.py:383
  23.5 0.3 collective-permute-start.6
  23.8 1.5 %collective-permute-start.7 = (f32[72,256]{1,0:T(8,128)S(1)}, f32[72,256]{1,0:T(8,128)S(1)}, u32[]{:S(2)}, u32[]{:S(2)}) collective-permute-start(f32[72,256]{1,0:T(8,128)S(1)} %get-tuple-element.55), channel_id=1, source_target_pairs={{0,33},{1,32},{2,35},{3,34},{4,37},{5,36},{6,39},{7,38},{8,41},{9,... | collective-permute-start | bytes 221192 | tf_op jit(solution)/shard_map/ppermute | solution.py:403
  25.3 1.8 %level2_rest.1 = (f32[256,1152]{1,0:T(8,128)S(1)}, f32[128,768]{1,0:T(8,128)S(1)}, f32[384,384]{1,0:T(8,128)S(1)}, f32[72,768]{1,0:T(8,128)S(1)}) custom-call(f32[256,256]{1,0:T(8,128)S(1)} %get-tuple-element.56.minv, f32[256,256]{1,0:T(8,128)S(1)} %get-tuple-element.50.gii, f32[768,896]{1,0:T(8,128)S(1)} %get-tuple-element.51.m1, ...), custom_call_target="tpu_custom_call" | custom-call | flops 11500000 | tf_op jit(solution)/shard_map/level2_rest/pallas_call | solution.py:383
  27.1 1.6 %collective-permute-done.7.a2 = f32[72,256]{1,0:T(8,128)S(1)} collective-permute-done((f32[72,256]{1,0:T(8,128)S(1)}, f32[72,256]{1,0:T(8,128)S(1)}, u32[]{:S(2)}, u32[]{:S(2)}) %collective-permute-start.7) | collective-permute-done | bytes 73760 | tf_op jit(solution)/shard_map/ppermute | solution.py:403
  28.7 0.0 collective-permute-done.6.a1
  28.7 0.0 collective-permute-done.10.xln
  28.7 3.3 %collective-permute-start.11 = (f32[64,768]{1,0:T(8,128)S(1)}, f32[64,768]{1,0:T(8,128)S(1)}, u32[]{:S(2)}, u32[]{:S(2)}) collective-permute-start(f32[64,768]{1,0:T(8,128)S(1)} %collective-permute-done.10.xln), channel_id=1, source_target_pairs={{0,16},{1,17},{2,18},{3,19},{4,20},{5,21},{6,22},{7,23},{8,24},{9,... | collective-permute-start | bytes 589832 | tf_op jit(solution)/shard_map/ppermute | solution.py:403
  32.0 0.0 collective-permute-start.8
  32.0 0.5 collective-permute-start.9
  32.5 0.6 collective-permute-done.11.xlc
  33.1 1.0 %level2_edge.1 = (f32[128,768]{1,0:T(8,128)S(1)}, f32[128,768]{1,0:T(8,128)S(1)}) custom-call(f32[256,1152]{1,0:T(8,128)S(1)} %get-tuple-element.65.t, f32[768,896]{1,0:T(8,128)S(1)} %get-tuple-element.51.m1, f32[128,768]{1,0:T(8,128)S(1)} %get-tuple-element.64.ye, f32[64,768]{1,0:T(8,128)S(1)} %collective-permute-done.10.xln, ...), custom_call_target="tpu_custom_call" | custom-call | flops 11500000 | tf_op jit(solution)/shard_map/level2_edge/pallas_call | solution.py:383
  34.1 0.3 collective-permute-start.12
  34.4 0.7 %collective-permute-start.14 = (f32[72,768]{1,0:T(8,128)S(1)}, f32[72,768]{1,0:T(8,128)S(1)}, u32[]{:S(2)}, u32[]{:S(2)}) collective-permute-start(f32[72,768]{1,0:T(8,128)S(1)} %get-tuple-element.73), channel_id=1, source_target_pairs={{0,1},{1,0},{2,3},{3,2},{4,5},{5,4},{6,7},{7,6},{8,9},{9,8},{10,11... | collective-permute-start | bytes 663560 | tf_op jit(solution)/shard_map/ppermute | solution.py:403
  35.1 4.5 %level3_inverse.1 = (f32[256,256]{1,0:T(8,128)S(1)}, f32[256,256]{1,0:T(8,128)S(1)}, f32[256,128]{1,0:T(8,128)S(1)}, f32[8,256]{1,0:T(8,128)S(1)}) custom-call(f32[136,256]{1,0:T(8,128)S(1)} %get-tuple-element.53.yi, f32[128,128]{1,0:T(8,128)S(1)} %get-tuple-element.54.yd, f32[136,256]{1,0:T(8,128)S(1)} %collective-permute-done.6.a1, ...), custom_call_target="tpu_custom_call" | custom-call | flops 23000000512 | tf_op jit(solution)/shard_map/level3_inverse/pallas_call | solution.py:383
  39.6 1.1 %collective-permute-done.14.rn = f32[72,768]{1,0:T(8,128)S(1)} collective-permute-done((f32[72,768]{1,0:T(8,128)S(1)}, f32[72,768]{1,0:T(8,128)S(1)}, u32[]{:S(2)}, u32[]{:S(2)}) %collective-permute-start.14) | collective-permute-done | bytes 221216 | tf_op jit(solution)/shard_map/ppermute | solution.py:403
  40.7 1.5 %collective-permute-start.15 = (f32[72,768]{1,0:T(8,128)S(1)}, f32[72,768]{1,0:T(8,128)S(1)}, u32[]{:S(2)}, u32[]{:S(2)}) collective-permute-start(f32[72,768]{1,0:T(8,128)S(1)} %collective-permute-done.14.rn), channel_id=1, source_target_pairs={{0,16},{1,17},{2,18},{3,19},{4,20},{5,21},{6,22},{7,23},{8,24},{9,... | collective-permute-start | bytes 663560 | tf_op jit(solution)/shard_map/ppermute | solution.py:403
  42.2 4.4 %collective-permute-start.13 = (f32[8,256]{1,0:T(8,128)S(1)}, f32[8,256]{1,0:T(8,128)S(1)}, u32[]{:S(2)}, u32[]{:S(2)}) collective-permute-start(f32[8,256]{1,0:T(8,128)S(1)} %get-tuple-element.71), channel_id=1, source_target_pairs={{0,224},{1,225},{2,226},{3,227},{4,228},{5,229},{6,230},{7,231},{8... | collective-permute-start | bytes 24584 | tf_op jit(solution)/shard_map/ppermute | solution.py:403
  46.6 0.0 collective-permute-done.15.rc
  46.6 1.5 %level2_rows.1.rows = f32[192,1152]{1,0:T(8,128)S(1)} custom-call(f32[256,1152]{1,0:T(8,128)S(1)} %get-tuple-element.65.t, f32[768,896]{1,0:T(8,128)S(1)} %get-tuple-element.51.m1, f32[72,768]{1,0:T(8,128)S(1)} %collective-permute-done.14.rn, f32[72,768]{1,0:T(8,128)S(1)} %collective-permute-done.15.rc), custom_call_target="tpu_custom_call" | custom-call | flops 1724999936 | tf_op jit(solution)/shard_map/level2_rows/pallas_call | solution.py:383
  48.1 0.0 collective-permute-done.13
  48.1 0.0 collective-permute-done.12.be
  48.1 0.7 %collective-permute-start.16 = (f32[128,768]{1,0:T(8,128)S(1)}, f32[128,768]{1,0:T(8,128)S(1)}, u32[]{:S(2)}, u32[]{:S(2)}) collective-permute-start(f32[128,768]{1,0:T(8,128)S(1)} %collective-permute-done.12.be), channel_id=1, source_target_pairs={{0,16},{1,17},{2,18},{3,19},{4,20},{5,21},{6,22},{7,23},{8,24},{9,... | collective-permute-start | bytes 1179656 | tf_op jit(solution)/shard_map/ppermute | solution.py:403
  48.8 1.9 %collective-permute-start.18 = (f32[8,256]{1,0:T(8,128)S(1)}, f32[8,256]{1,0:T(8,128)S(1)}, u32[]{:S(2)}, u32[]{:S(2)}) collective-permute-start(f32[8,256]{1,0:T(8,128)S(1)} %collective-permute-done.13), channel_id=1, source_target_pairs={{0,32},{1,33},{2,34},{3,35},{4,36},{5,37},{6,38},{7,39},{8,40},{9,... | collective-permute-start | bytes 24584 | tf_op jit(solution)/shard_map/ppermute | solution.py:403
  50.7 0.8 %collective-permute-start.17 = (f32[8,256]{1,0:T(8,128)S(1)}, f32[8,256]{1,0:T(8,128)S(1)}, u32[]{:S(2)}, u32[]{:S(2)}) collective-permute-start(f32[8,256]{1,0:T(8,128)S(1)} %collective-permute-done.13), channel_id=1, source_target_pairs={{0,1},{1,0},{2,3},{3,2},{4,5},{5,4},{6,7},{7,6},{8,9},{9,8},{10,11... | collective-permute-start | bytes 24584 | tf_op jit(solution)/shard_map/ppermute | solution.py:403
  51.5 2.7 %level3_rows.1 = (f32[192,1536]{1,0:T(8,128)}, f32[192,1536]{1,0:T(8,128)S(1)}, f32[192,128]{1,0:T(8,128)S(1)}) custom-call(f32[256,256]{1,0:T(8,128)S(1)} %get-tuple-element.61.minv, f32[256,256]{1,0:T(8,128)S(1)} %get-tuple-element.62.gii, f32[256,128]{1,0:T(8,128)S(1)} %get-tuple-element.63.th, f32[128,768]{1,0:T(8,128)S(1)} %get-tuple-element.64.ye, ...), custom_call_target="tpu_custom_call" | custom-call | flops 2875000064 | tf_op jit(solution)/shard_map/level3_rows/pallas_call | solution.py:383
  54.2 1.0 %collective-permute-start.20 = (f32[32,256]{1,0:T(8,128)S(1)}, f32[32,256]{1,0:T(8,128)S(1)}, u32[]{:S(2)}, u32[]{:S(2)}) collective-permute-start(f32[32,256]{1,0:T(8,128)S(1)} %constant_dynamic-update-slice_fusion.mine), channel_id=1, source_target_pairs={{0,16},{1,17},{2,18},{3,19},{4,20},{5,21},{6,22},{7,23},{8,24},{9,... | collective-permute-start | bytes 98312 | tf_op jit(solution)/shard_map/ppermute | solution.py:403
  55.2 0.9 %collective-permute-done.20.core = f32[32,256]{1,0:T(8,128)S(1)} collective-permute-done((f32[32,256]{1,0:T(8,128)S(1)}, f32[32,256]{1,0:T(8,128)S(1)}, u32[]{:S(2)}, u32[]{:S(2)}) %collective-permute-start.20) | collective-permute-done | bytes 32800 | tf_op jit(solution)/shard_map/ppermute | solution.py:403
  56.1 0.7 %couple.1 = f32[1,192]{1,0:T(1,128)} custom-call(f32[192,1536]{1,0:T(8,128)S(1)} %get-tuple-element.78.raw, f32[192,128]{1,0:T(8,128)S(1)} %get-tuple-element.81.h3, f32[32,256]{1,0:T(8,128)S(1)} %constant_dynamic-update-slice_fusion.mine, f32[32,256]{1,0:T(8,128)S(1)} %collective-permute-done.20.core), custom_call_target="tpu_custom_call" | custom-call | flops 805000000 | tf_op jit(solution)/shard_map/couple/pallas_call | solution.py:383
  (15 shorter events, 0.0 us)
Async XLA Ops:
  0.6 6.2 %collective-permute-start = (f32[512,512]{1,0:T(8,128)}, f32[512,512]{1,0:T(8,128)S(1)}, u32[]{:S(2)}, u32[]{:S(2)}) collective-permute-start(f32[512,512]{1,0:T(8,128)} %bitcast.6), channel_id=1, source_target_pairs={{0,16},{1,17},{2,18},{3,19},{4,20},{5,21},{6,22},{7,23},{8,24},{9,... | collective-permute-start | bytes 3145736 | tf_op jit(solution)/shard_map/ppermute | solution.py:403
  5.6 1.2 %collective-permute-start.1 = (f32[1,512]{1,0:T(1,128)S(1)}, f32[1,512]{1,0:T(1,128)S(1)}, u32[]{:S(2)}, u32[]{:S(2)}) collective-permute-start(f32[1,512]{1,0:T(1,128)S(1)} %bitcast_multiply_fusion.hown), channel_id=1, source_target_pairs={{0,16},{1,17},{2,18},{3,19},{4,20},{5,21},{6,22},{7,23},{8,24},{9,... | collective-permute-start | bytes 6152 | tf_op jit(solution)/shard_map/ppermute | solution.py:403
  5.6 1.2 %copy-start = (f32[1,1,512,512]{3,2,1,0:T(8,128)S(1)}, f32[1,1,512,512]{3,2,1,0:T(8,128)}, u32[]{:S(2)}) copy-start(f32[1,1,512,512]{3,2,1,0:T(8,128)} %param.4) | copy-start | bytes 3145732
  9.6 4.8 %collective-permute-start.2 = (f32[136,256]{1,0:T(8,128)S(1)}, f32[136,256]{1,0:T(8,128)S(1)}, u32[]{:S(2)}, u32[]{:S(2)}) collective-permute-start(f32[136,256]{1,0:T(8,128)S(1)} %get-tuple-element.45), channel_id=1, source_target_pairs={{0,1},{1,0},{2,3},{3,2},{4,5},{5,4},{6,7},{7,6},{8,9},{9,8},{10,11... | collective-permute-start | bytes 417800 | tf_op jit(solution)/shard_map/ppermute | solution.py:403
  11.9 9.2 %collective-permute-start.4 = (f32[128,512]{1,0:T(8,128)S(1)}, f32[128,512]{1,0:T(8,128)S(1)}, u32[]{:S(2)}, u32[]{:S(2)}) collective-permute-start(f32[128,512]{1,0:T(8,128)S(1)} %get-tuple-element.47), channel_id=1, source_target_pairs={{0,1},{1,0},{2,3},{3,2},{4,5},{5,4},{6,7},{7,6},{8,9},{9,8},{10,11... | collective-permute-start | bytes 786440 | tf_op jit(solution)/shard_map/ppermute | solution.py:403
  14.4 3.0 %collective-permute-start.3 = (f32[136,256]{1,0:T(8,128)S(1)}, f32[136,256]{1,0:T(8,128)S(1)}, u32[]{:S(2)}, u32[]{:S(2)}) collective-permute-start(f32[136,256]{1,0:T(8,128)S(1)} %collective-permute-done.2.xin), channel_id=1, source_target_pairs={{0,16},{1,17},{2,18},{3,19},{4,20},{5,21},{6,22},{7,23},{8,24},{9,... | collective-permute-start | bytes 417800 | tf_op jit(solution)/shard_map/ppermute | solution.py:403
  21.2 1.6 %collective-permute-start.5 = (f32[128,512]{1,0:T(8,128)S(1)}, f32[128,512]{1,0:T(8,128)S(1)}, u32[]{:S(2)}, u32[]{:S(2)}) collective-permute-start(f32[128,512]{1,0:T(8,128)S(1)} %collective-permute-done.4.xen), channel_id=1, source_target_pairs={{0,16},{1,17},{2,18},{3,19},{4,20},{5,21},{6,22},{7,23},{8,24},{9,... | collective-permute-start | bytes 786440 | tf_op jit(solution)/shard_map/ppermute | solution.py:403
  21.6 7.1 %collective-permute-start.10 = (f32[64,768]{1,0:T(8,128)S(1)}, f32[64,768]{1,0:T(8,128)S(1)}, u32[]{:S(2)}, u32[]{:S(2)}) collective-permute-start(f32[64,768]{1,0:T(8,128)S(1)} %get-tuple-element.67), channel_id=1, source_target_pairs={{0,1},{1,0},{2,3},{3,2},{4,5},{5,4},{6,7},{7,6},{8,9},{9,8},{10,11... | collective-permute-start | bytes 589832 | tf_op jit(solution)/shard_map/ppermute | solution.py:403
  23.5 5.1 %collective-permute-start.6 = (f32[136,256]{1,0:T(8,128)S(1)}, f32[136,256]{1,0:T(8,128)S(1)}, u32[]{:S(2)}, u32[]{:S(2)}) collective-permute-start(f32[136,256]{1,0:T(8,128)S(1)} %get-tuple-element.53.yi), channel_id=1, source_target_pairs={{0,1},{1,0},{2,3},{3,2},{4,5},{5,4},{6,7},{7,6},{8,9},{9,8},{10,11... | collective-permute-start | bytes 417800 | tf_op jit(solution)/shard_map/ppermute | solution.py:403
  23.8 4.9 %collective-permute-start.7 = (f32[72,256]{1,0:T(8,128)S(1)}, f32[72,256]{1,0:T(8,128)S(1)}, u32[]{:S(2)}, u32[]{:S(2)}) collective-permute-start(f32[72,256]{1,0:T(8,128)S(1)} %get-tuple-element.55), channel_id=1, source_target_pairs={{0,33},{1,32},{2,35},{3,34},{4,37},{5,36},{6,39},{7,38},{8,41},{9,... | collective-permute-start | bytes 221192 | tf_op jit(solution)/shard_map/ppermute | solution.py:403
  28.7 4.4 %collective-permute-start.11 = (f32[64,768]{1,0:T(8,128)S(1)}, f32[64,768]{1,0:T(8,128)S(1)}, u32[]{:S(2)}, u32[]{:S(2)}) collective-permute-start(f32[64,768]{1,0:T(8,128)S(1)} %collective-permute-done.10.xln), channel_id=1, source_target_pairs={{0,16},{1,17},{2,18},{3,19},{4,20},{5,21},{6,22},{7,23},{8,24},{9,... | collective-permute-start | bytes 589832 | tf_op jit(solution)/shard_map/ppermute | solution.py:403
  32.0 3.1 %collective-permute-start.8 = (f32[136,256]{1,0:T(8,128)S(1)}, f32[136,256]{1,0:T(8,128)S(1)}, u32[]{:S(2)}, u32[]{:S(2)}) collective-permute-start(f32[136,256]{1,0:T(8,128)S(1)} %collective-permute-done.6.a1), channel_id=1, source_target_pairs={{0,16},{1,17},{2,18},{3,19},{4,20},{5,21},{6,22},{7,23},{8,24},{9,... | collective-permute-start | bytes 417800 | tf_op jit(solution)/shard_map/ppermute | solution.py:403
  32.0 3.1 %collective-permute-start.9 = (f32[72,256]{1,0:T(8,128)S(1)}, f32[72,256]{1,0:T(8,128)S(1)}, u32[]{:S(2)}, u32[]{:S(2)}) collective-permute-start(f32[72,256]{1,0:T(8,128)S(1)} %collective-permute-done.7.a2), channel_id=1, source_target_pairs={{0,16},{1,17},{2,18},{3,19},{4,20},{5,21},{6,22},{7,23},{8,24},{9,... | collective-permute-start | bytes 221192 | tf_op jit(solution)/shard_map/ppermute | solution.py:403
  34.1 14.0 %collective-permute-start.12 = (f32[128,768]{1,0:T(8,128)S(1)}, f32[128,768]{1,0:T(8,128)S(1)}, u32[]{:S(2)}, u32[]{:S(2)}) collective-permute-start(f32[128,768]{1,0:T(8,128)S(1)} %get-tuple-element.70), channel_id=1, source_target_pairs={{0,32},{1,33},{2,34},{3,35},{4,36},{5,37},{6,38},{7,39},{8,40},{9,... | collective-permute-start | bytes 1179656 | tf_op jit(solution)/shard_map/ppermute | solution.py:403
  34.4 6.3 %collective-permute-start.14 = (f32[72,768]{1,0:T(8,128)S(1)}, f32[72,768]{1,0:T(8,128)S(1)}, u32[]{:S(2)}, u32[]{:S(2)}) collective-permute-start(f32[72,768]{1,0:T(8,128)S(1)} %get-tuple-element.73), channel_id=1, source_target_pairs={{0,1},{1,0},{2,3},{3,2},{4,5},{5,4},{6,7},{7,6},{8,9},{9,8},{10,11... | collective-permute-start | bytes 663560 | tf_op jit(solution)/shard_map/ppermute | solution.py:403
  40.7 5.9 %collective-permute-start.15 = (f32[72,768]{1,0:T(8,128)S(1)}, f32[72,768]{1,0:T(8,128)S(1)}, u32[]{:S(2)}, u32[]{:S(2)}) collective-permute-start(f32[72,768]{1,0:T(8,128)S(1)} %collective-permute-done.14.rn), channel_id=1, source_target_pairs={{0,16},{1,17},{2,18},{3,19},{4,20},{5,21},{6,22},{7,23},{8,24},{9,... | collective-permute-start | bytes 663560 | tf_op jit(solution)/shard_map/ppermute | solution.py:403
  42.2 5.9 %collective-permute-start.13 = (f32[8,256]{1,0:T(8,128)S(1)}, f32[8,256]{1,0:T(8,128)S(1)}, u32[]{:S(2)}, u32[]{:S(2)}) collective-permute-start(f32[8,256]{1,0:T(8,128)S(1)} %get-tuple-element.71), channel_id=1, source_target_pairs={{0,224},{1,225},{2,226},{3,227},{4,228},{5,229},{6,230},{7,231},{8... | collective-permute-start | bytes 24584 | tf_op jit(solution)/shard_map/ppermute | solution.py:403
  48.1 3.3 %collective-permute-start.16 = (f32[128,768]{1,0:T(8,128)S(1)}, f32[128,768]{1,0:T(8,128)S(1)}, u32[]{:S(2)}, u32[]{:S(2)}) collective-permute-start(f32[128,768]{1,0:T(8,128)S(1)} %collective-permute-done.12.be), channel_id=1, source_target_pairs={{0,16},{1,17},{2,18},{3,19},{4,20},{5,21},{6,22},{7,23},{8,24},{9,... | collective-permute-start | bytes 1179656 | tf_op jit(solution)/shard_map/ppermute | solution.py:403
  48.8 5.4 %collective-permute-start.19 = (f32[8,256]{1,0:T(8,128)S(1)}, f32[8,256]{1,0:T(8,128)S(1)}, u32[]{:S(2)}, u32[]{:S(2)}) collective-permute-start(f32[8,256]{1,0:T(8,128)S(1)} %collective-permute-done.13), channel_id=1, source_target_pairs={{0,33},{1,32},{2,35},{3,34},{4,37},{5,36},{6,39},{7,38},{8,41},{9,... | collective-permute-start | bytes 24584 | tf_op jit(solution)/shard_map/ppermute | solution.py:403
  48.8 5.4 %collective-permute-start.18 = (f32[8,256]{1,0:T(8,128)S(1)}, f32[8,256]{1,0:T(8,128)S(1)}, u32[]{:S(2)}, u32[]{:S(2)}) collective-permute-start(f32[8,256]{1,0:T(8,128)S(1)} %collective-permute-done.13), channel_id=1, source_target_pairs={{0,32},{1,33},{2,34},{3,35},{4,36},{5,37},{6,38},{7,39},{8,40},{9,... | collective-permute-start | bytes 24584 | tf_op jit(solution)/shard_map/ppermute | solution.py:403
  50.7 3.5 %collective-permute-start.17 = (f32[8,256]{1,0:T(8,128)S(1)}, f32[8,256]{1,0:T(8,128)S(1)}, u32[]{:S(2)}, u32[]{:S(2)}) collective-permute-start(f32[8,256]{1,0:T(8,128)S(1)} %collective-permute-done.13), channel_id=1, source_target_pairs={{0,1},{1,0},{2,3},{3,2},{4,5},{5,4},{6,7},{7,6},{8,9},{9,8},{10,11... | collective-permute-start | bytes 24584 | tf_op jit(solution)/shard_map/ppermute | solution.py:403
  54.2 1.9 %collective-permute-start.20 = (f32[32,256]{1,0:T(8,128)S(1)}, f32[32,256]{1,0:T(8,128)S(1)}, u32[]{:S(2)}, u32[]{:S(2)}) collective-permute-start(f32[32,256]{1,0:T(8,128)S(1)} %constant_dynamic-update-slice_fusion.mine), channel_id=1, source_target_pairs={{0,16},{1,17},{2,18},{3,19},{4,20},{5,21},{6,22},{7,23},{8,24},{9,... | collective-permute-start | bytes 98312 | tf_op jit(solution)/shard_map/ppermute | solution.py:403

commit v3 on v2

--- a/solution.py
+++ b/solution.py
@@ -146,7 +146,9 @@
     row = at(2 * (2 - s) + c, S)
     xe[:, : 2 * S] = m1[row, : 2 * S]
     xe[:, 2 * S :] = m1[row, at(2 * (1 + s), 2 * S)]
-    xl[...] = m1[at(2 * (1 - r) + c, S // 2, S // 2), : 6 * S]
+    half = at(2 * (1 - r) + c, S // 2, S // 2)
+    xl[:, :S] = m1[half, at(r, S)]
+    xl[:, S:] = m1[half, 2 * S : 6 * S]
 
 
 def pick(x, s, low, high):
@@ -223,29 +225,21 @@
     rr[H:, S:] = jnp.zeros((8, 5 * S), f32)
 
 
-def level2_edge(t, m1, ye, xln, xlc, be, yx, row):
+def level2_edge(t, m1, ye, xln, be, yx):
     c, s, r = roles()
     o = 1 - s
     H = S // 2
     inner = at(2 * (2 - s), 2 * S)
-    outer = at(2 * (1 + s), 2 * S)
-    row[at(c, H, H), : 6 * S] = xln[...]
-    row[at(1 - c, H, H), : 6 * S] = xlc[...]
-    V = dot3(row[:, outer], m1[inner, : 6 * S])
+    link = pick(xln[:, S:], s, 0, 1)
+    V = dot3(link, m1[inner, : 6 * S])
     D = dot3(pick(V, s, 2, 1), jnp.concatenate([t[:, at(2 * r, 2 * S)], t[:, 4 * S : 8 * S]], 1))
     yx[...] = D
     yx[:, at(s, S)] -= jnp.where(r == 0, V[:, :S], V[:, S : 2 * S])
     yx[:, at(2 + 2 * s, 2 * S)] -= pick(V, s, 1, 2)
-    yx[:, at(o, S)] += row[:, at(r, S)]
-    yx[:, at(2 + 2 * o, 2 * S)] += row[:, inner]
-
-    @pl.when(c == 0)
-    def _():
-        be[...] = ye[...]
-
-    @pl.when(c == 1)
-    def _():
-        be[...] = yx[...]
+    yx[:, at(o, S)] += xln[:, :S]
+    yx[:, at(2 + 2 * o, 2 * S)] += pick(xln[:, S:], s, 1, 0)
+    be[:H] = ye[at(c, H, H), :]
+    be[H:] = yx[...]
 
 
 def level2_rows(t, m1, rn, rc, rows, work):
@@ -333,13 +327,18 @@
     hs[:, S:] = as_rows(h3[2 * S :])
 
 
-def level3_rows(minv, gii, th, ye, yx, be, kb, rows, top, raw, h3, pe, qe):
+def level3_rows(minv, gii, th, ye, yx, yk, be, kb, rows, top, raw, h3, pe, qe):
     c, s, r = roles()
     o = 1 - s
+    d = 1 - c
+    H = S // 2
     pe[at(s, S), :] = ye[...]
-    pe[at(o, S), :] = yx[...]
-    qe[at(s, S), :] = jnp.where(c == 0, be[...], kb[...])
-    qe[at(o, S), :] = jnp.where(c == 0, kb[...], be[...])
+    pe[at(2 * o + c, H, H), :] = yx[...]
+    pe[at(2 * o + d, H, H), :] = yk[...]
+    qe[at(2 * s + c, H, H), :] = be[:H]
+    qe[at(2 * s + d, H, H), :] = kb[:H]
+    qe[at(2 * o + c, H, H), :] = be[H:]
+    qe[at(2 * o + d, H, H), :] = kb[H:]
     A = dot3(gii[...], pe[...])
     B = dot3(minv[...], qe[...])
     R_ei = split(rows[:, at(2 * (1 - r), 2 * S)])
@@ -455,7 +454,7 @@
     )
     xin = over_x(xi)
     m1, xe, xl = call(
-        level1_map, [(6 * S, 7 * S), (S, 4 * S), (H, 6 * S)], [], [leaf, oth, hown, hoth, minv1], 2.0
+        level1_map, [(6 * S, 7 * S), (S, 4 * S), (H, 5 * S)], [], [leaf, oth, hown, hoth, minv1], 2.0
     )
     xen = over_x(xe)
     xic = over_core(after(xin, xe))
@@ -477,10 +476,9 @@
         [after(minv, yd), gii, m1, xin, xic, xen, xec],
         0.01,
     )
-    a1, a2, chip = lax.optimization_barrier((a1, a2, chip))
+    be, yx = call(level2_edge, [(S, 6 * S), (H, 6 * S)], [], [t, m1, ye, xln], 0.01)
+    a1, a2, _, chip = lax.optimization_barrier((a1, a2, be, chip))
     k1, k2 = over_core(a1), over_core(a2)
-    xlc = over_core(after(xln, chip))
-    be, yx = call(level2_edge, [(S, 6 * S)] * 2, [(S, 6 * S)], [t, m1, ye, xln, xlc], 0.01)
     bn = over_z(be)
     rn = over_x(after(rr, be))
     minv3, gii3, th, hs = call(
@@ -492,6 +490,7 @@
     )
     g0 = over_edge(hs)
     rc = over_core(after(rn, minv3))
+    yk = over_core(after(yx, minv3))
     (rows,) = call(level2_rows, [(3 * H, 9 * S)], [(3 * H, 7 * S)], [t, m1, rn, rc], 1.5)
     bn, g0, rows = lax.optimization_barrier((bn, g0, rows))
     kb = over_core(bn)
@@ -500,7 +499,7 @@
         level3_rows,
         [(3 * H, 12 * S), (3 * H, 12 * S), (3 * H, S)],
         [(2 * S, 6 * S)] * 2,
-        [minv3, gii3, th, ye, yx, bn, kb, rows],
+        [minv3, gii3, th, ye, yx, yk, bn, kb, rows],
         2.5,
     )
     g0, gx, gz, gd, h3 = lax.optimization_barrier((g0, gx, gz, gd, h3))

time: 57 us -> 54.5 us (0.956)
  waiting for transfers between devices: 6.72 us -> 5.03 us
  starting transfers between devices: 24.8 us -> 24.1 us
    ppermute x21, waiting for transfers between devices: 6.72 us -> 5.03 us  [send(): return lax.ppermute(value, ('gx', 'gy'), pairs)]
    ppermute x21, starting transfers between devices: 24.8 us -> 24.1 us  [send(): return lax.ppermute(value, ('gx', 'gy'), pairs)]
  transfers between devices with their start and end apart: 21 -> 21, of which waited for: 7 -> 8; matrix products, arithmetic and copies ran while one was open for 3% -> 3% of each run, Pallas kernels for 32% -> 33%
where the time goes in v3:
time: 54.5 us; the launch traced here: 54.4 us
  starting transfers between devices  24.1 us (44%)
  Pallas kernels  21.6 us (40%)
  waiting for transfers between devices  5.03 us (9%)
  other arithmetic  1.44 us (3%)
  local copies, waits for them, and re-layouts  1.39 us (3%)
  between operations  0.77 us (1%)
    ppermute x21, starting transfers between devices, send(): return lax.ppermute(value, ('gx', 'gy'), pairs)  24.1 us
    pallas_call x11, Pallas kernels, call(): pl.pallas_call(body, out_shape=[jax.ShapeDtypeStruct(o, f32) for o in out...  21.6 us
    ppermute x21, waiting for transfers between devices, send(): return lax.ppermute(value, ('gx', 'gy'), pairs)  5.03 us
    unnamed x5, local copies, waits for them, and re-layouts  1.23 us
  transfers between devices with their start and end apart: 21, of which 8 were waited for; matrix products, arithmetic and copies ran while one was open for 3% of the time, Pallas kernels for 33%

profile of v3, /device:TPU:1, one launch (start us, length us, event | category | flops | bytes accessed | tf_op | source)
XLA Modules:
  0.0 54.4 jit_solution(10916110084540519460)
XLA Ops:
  0.6 3.3 %collective-permute-start = (f32[512,512]{1,0:T(8,128)}, f32[512,512]{1,0:T(8,128)S(1)}, u32[]{:S(2)}, u32[]{:S(2)}) collective-permute-start(f32[512,512]{1,0:T(8,128)} %bitcast.6), channel_id=1, source_target_pairs={{0,16},{1,17},{2,18},{3,19},{4,20},{5,21},{6,22},{7,23},{8,24},{9,... | collective-permute-start | bytes 3145736 | tf_op jit(solution)/shard_map/ppermute | solution.py:402
  4.0 0.8 %select_reduce_fusion = f32[16]{0:T(128)S(1)} fusion(f32[8]{0:T(128)} %param.7, s32[16]{0:T(128)} %bitcast.10), kind=kLoop, calls=%fused_computation.4 | loop fusion | flops 368 | bytes 160 | tf_op jit(solution)/shard_map/reduce_sum | solution.py:446
  4.7 0.1 broadcast_in_dim.6
  4.8 0.1 reshape.27
  4.9 0.7 %bitcast_multiply_fusion.hown = f32[1,512]{1,0:T(1,128)S(1)} fusion(f32[1,512]{1,0:T(1,128)S(1)} %reshape.27, f32[1,1,512]{2,1,0:T(1,128)} %param.5), kind=kLoop, calls=%fused_computation.6 | loop fusion | flops 512 | bytes 6144 | tf_op jit(solution)/shard_map/mul | solution.py:449
  5.6 0.0 collective-permute-start.1
  5.6 1.2 %copy-done = f32[1,1,512,512]{3,2,1,0:T(8,128)S(1)} copy-done((f32[1,1,512,512]{3,2,1,0:T(8,128)S(1)}, f32[1,1,512,512]{3,2,1,0:T(8,128)}, u32[]{:S(2)}) %copy-start) | copy-done | bytes 1048600
  6.8 0.0 collective-permute-done.1.hoth
  6.8 2.8 %level1_interface.1 = (f32[128,128]{1,0:T(8,128)S(1)}, f32[256,256]{1,0:T(8,128)S(1)}, f32[136,256]{1,0:T(8,128)S(1)}) custom-call(f32[512,512]{1,0:T(8,128)S(1)} %bitcast.8, f32[512,512]{1,0:T(8,128)S(1)} %collective-permute-done.oth, f32[1,512]{1,0:T(1,128)S(1)} %bitcast_multiply_fusion.hown, f32[1,512]{1,0:T(1,128)S(1)} %collective-permute-done.1.hoth, ...), custom_call_target="tpu_custom_call" | custom-call | flops 2875000064 | tf_op jit(solution)/shard_map/level1_interface/pallas_call | solution.py:382
  9.6 0.1 collective-permute-start.2
  9.7 2.2 %level1_map.1 = (f32[768,896]{1,0:T(8,128)S(1)}, f32[128,512]{1,0:T(8,128)S(1)}, f32[64,640]{1,0:T(8,128)S(1)}) custom-call(f32[512,512]{1,0:T(8,128)S(1)} %bitcast.9, f32[512,512]{1,0:T(8,128)S(1)} %collective-permute-done.oth, f32[1,512]{1,0:T(1,128)S(1)} %bitcast_multiply_fusion.hown, f32[1,512]{1,0:T(1,128)S(1)} %collective-permute-done.1.hoth, ...), custom_call_target="tpu_custom_call" | custom-call | flops 2300000000 | tf_op jit(solution)/shard_map/level1_map/pallas_call | solution.py:382
  11.9 1.5 %collective-permute-start.4 = (f32[128,512]{1,0:T(8,128)S(1)}, f32[128,512]{1,0:T(8,128)S(1)}, u32[]{:S(2)}, u32[]{:S(2)}) collective-permute-start(f32[128,512]{1,0:T(8,128)S(1)} %get-tuple-element.47), channel_id=1, source_target_pairs={{0,1},{1,0},{2,3},{3,2},{4,5},{5,4},{6,7},{7,6},{8,9},{9,8},{10,11... | collective-permute-start | bytes 786440 | tf_op jit(solution)/shard_map/ppermute | solution.py:402
  13.4 1.0 %collective-permute-done.2.xin = f32[136,256]{1,0:T(8,128)S(1)} collective-permute-done((f32[136,256]{1,0:T(8,128)S(1)}, f32[136,256]{1,0:T(8,128)S(1)}, u32[]{:S(2)}, u32[]{:S(2)}) %collective-permute-start.2) | collective-permute-done | bytes 139296 | tf_op jit(solution)/shard_map/ppermute | solution.py:402
  14.4 1.9 %collective-permute-start.3 = (f32[136,256]{1,0:T(8,128)S(1)}, f32[136,256]{1,0:T(8,128)S(1)}, u32[]{:S(2)}, u32[]{:S(2)}) collective-permute-start(f32[136,256]{1,0:T(8,128)S(1)} %collective-permute-done.2.xin), channel_id=1, source_target_pairs={{0,16},{1,17},{2,18},{3,19},{4,20},{5,21},{6,22},{7,23},{8,24},{9,... | collective-permute-start | bytes 417800 | tf_op jit(solution)/shard_map/ppermute | solution.py:402
  16.4 1.0 %collective-permute-done.3.xic = f32[136,256]{1,0:T(8,128)S(1)} collective-permute-done((f32[136,256]{1,0:T(8,128)S(1)}, f32[136,256]{1,0:T(8,128)S(1)}, u32[]{:S(2)}, u32[]{:S(2)}) %collective-permute-start.3) | collective-permute-done | bytes 139296 | tf_op jit(solution)/shard_map/ppermute | solution.py:402
  17.4 3.8 %level2_inverse.1 = (f32[256,256]{1,0:T(8,128)S(1)}, f32[256,256]{1,0:T(8,128)S(1)}) custom-call(f32[256,256]{1,0:T(8,128)S(1)} %get-tuple-element.44.pii, f32[136,256]{1,0:T(8,128)S(1)} %collective-permute-done.2.xin, f32[136,256]{1,0:T(8,128)S(1)} %collective-permute-done.3.xic), custom_call_target="tpu_custom_call" | custom-call | flops 575000000 | tf_op jit(solution)/shard_map/level2_inverse/pallas_call | solution.py:382
  21.1 0.5 collective-permute-start.5
  21.6 0.6 %collective-permute-start.8 = (f32[64,640]{1,0:T(8,128)S(1)}, f32[64,640]{1,0:T(8,128)S(1)}, u32[]{:S(2)}, u32[]{:S(2)}) collective-permute-start(f32[64,640]{1,0:T(8,128)S(1)} %get-tuple-element.60), channel_id=1, source_target_pairs={{0,1},{1,0},{2,3},{3,2},{4,5},{5,4},{6,7},{7,6},{8,9},{9,8},{10,11... | collective-permute-start | bytes 491528 | tf_op jit(solution)/shard_map/ppermute | solution.py:402
  22.2 0.6 %collective-permute-done.5.xec = f32[128,512]{1,0:T(8,128)S(1)} collective-permute-done((f32[128,512]{1,0:T(8,128)S(1)}, f32[128,512]{1,0:T(8,128)S(1)}, u32[]{:S(2)}, u32[]{:S(2)}) %collective-permute-start.5) | collective-permute-done | bytes 262176 | tf_op jit(solution)/shard_map/ppermute | solution.py:402
  22.8 0.8 %level2_interface.1 = (f32[136,256]{1,0:T(8,128)S(1)}, f32[72,256]{1,0:T(8,128)S(1)}, f32[128,128]{1,0:T(8,128)S(1)}) custom-call(f32[256,256]{1,0:T(8,128)S(1)} %get-tuple-element.56.minv, f32[256,256]{1,0:T(8,128)S(1)} %get-tuple-element.50.gii, f32[768,896]{1,0:T(8,128)S(1)} %get-tuple-element.51.m1, f32[136,256]{1,0:T(8,128)S(1)} %collective-permute-done.2.xin, ...), custom_call_target="tpu_custom_call" | custom-call | flops 1150000000 | tf_op jit(solution)/shard_map/level2_interface/pallas_call | solution.py:382
  23.5 0.3 collective-permute-start.6
  23.8 1.5 %collective-permute-start.7 = (f32[72,256]{1,0:T(8,128)S(1)}, f32[72,256]{1,0:T(8,128)S(1)}, u32[]{:S(2)}, u32[]{:S(2)}) collective-permute-start(f32[72,256]{1,0:T(8,128)S(1)} %get-tuple-element.55), channel_id=1, source_target_pairs={{0,33},{1,32},{2,35},{3,34},{4,37},{5,36},{6,39},{7,38},{8,41},{9,... | collective-permute-start | bytes 221192 | tf_op jit(solution)/shard_map/ppermute | solution.py:402
  25.3 1.8 %level2_rest.1 = (f32[256,1152]{1,0:T(8,128)S(1)}, f32[128,768]{1,0:T(8,128)S(1)}, f32[384,384]{1,0:T(8,128)S(1)}, f32[72,768]{1,0:T(8,128)S(1)}) custom-call(f32[256,256]{1,0:T(8,128)S(1)} %get-tuple-element.56.minv, f32[256,256]{1,0:T(8,128)S(1)} %get-tuple-element.50.gii, f32[768,896]{1,0:T(8,128)S(1)} %get-tuple-element.51.m1, ...), custom_call_target="tpu_custom_call" | custom-call | flops 11500000 | tf_op jit(solution)/shard_map/level2_rest/pallas_call | solution.py:382
  27.1 0.1 collective-permute-done.8.xln
  27.3 0.9 %level2_edge.1 = (f32[128,768]{1,0:T(8,128)S(1)}, f32[64,768]{1,0:T(8,128)S(1)}) custom-call(f32[256,1152]{1,0:T(8,128)S(1)} %get-tuple-element.57.t, f32[768,896]{1,0:T(8,128)S(1)} %get-tuple-element.51.m1, f32[128,768]{1,0:T(8,128)S(1)} %get-tuple-element.58.ye, f32[64,640]{1,0:T(8,128)S(1)} %collective-permute-done.8.xln), custom_call_target="tpu_custom_call" | custom-call | flops 11500000 | tf_op jit(solution)/shard_map/level2_edge/pallas_call | solution.py:382
  28.2 0.5 collective-permute-done.7.a2
  28.7 2.6 %collective-permute-start.9 = (f32[136,256]{1,0:T(8,128)S(1)}, f32[136,256]{1,0:T(8,128)S(1)}, u32[]{:S(2)}, u32[]{:S(2)}) collective-permute-start(f32[136,256]{1,0:T(8,128)S(1)} %collective-permute-done.6.a1), channel_id=1, source_target_pairs={{0,16},{1,17},{2,18},{3,19},{4,20},{5,21},{6,22},{7,23},{8,24},{9,... | collective-permute-start | bytes 417800 | tf_op jit(solution)/shard_map/ppermute | solution.py:402
  31.3 0.0 collective-permute-start.10
  31.3 0.2 collective-permute-start.12
  31.5 0.7 %collective-permute-start.14 = (f32[72,768]{1,0:T(8,128)S(1)}, f32[72,768]{1,0:T(8,128)S(1)}, u32[]{:S(2)}, u32[]{:S(2)}) collective-permute-start(f32[72,768]{1,0:T(8,128)S(1)} %get-tuple-element.73), channel_id=1, source_target_pairs={{0,1},{1,0},{2,3},{3,2},{4,5},{5,4},{6,7},{7,6},{8,9},{9,8},{10,11... | collective-permute-start | bytes 663560 | tf_op jit(solution)/shard_map/ppermute | solution.py:402
  32.2 0.3 collective-permute-done.10.k2
  32.6 0.0 collective-permute-done.9.k1
  32.6 4.5 %level3_inverse.1 = (f32[256,256]{1,0:T(8,128)S(1)}, f32[256,256]{1,0:T(8,128)S(1)}, f32[256,128]{1,0:T(8,128)S(1)}, f32[8,256]{1,0:T(8,128)S(1)}) custom-call(f32[136,256]{1,0:T(8,128)S(1)} %get-tuple-element.53.yi, f32[128,128]{1,0:T(8,128)S(1)} %get-tuple-element.54.yd, f32[136,256]{1,0:T(8,128)S(1)} %collective-permute-done.6.a1, ...), custom_call_target="tpu_custom_call" | custom-call | flops 23000000512 | tf_op jit(solution)/shard_map/level3_inverse/pallas_call | solution.py:382
  37.1 0.6 %collective-permute-done.14.rn = f32[72,768]{1,0:T(8,128)S(1)} collective-permute-done((f32[72,768]{1,0:T(8,128)S(1)}, f32[72,768]{1,0:T(8,128)S(1)}, u32[]{:S(2)}, u32[]{:S(2)}) %collective-permute-start.14) | collective-permute-done | bytes 221216 | tf_op jit(solution)/shard_map/ppermute | solution.py:402
  37.7 1.7 %collective-permute-start.15 = (f32[72,768]{1,0:T(8,128)S(1)}, f32[72,768]{1,0:T(8,128)S(1)}, u32[]{:S(2)}, u32[]{:S(2)}) collective-permute-start(f32[72,768]{1,0:T(8,128)S(1)} %collective-permute-done.14.rn), channel_id=1, source_target_pairs={{0,16},{1,17},{2,18},{3,19},{4,20},{5,21},{6,22},{7,23},{8,24},{9,... | collective-permute-start | bytes 663560 | tf_op jit(solution)/shard_map/ppermute | solution.py:402
  39.4 4.4 %collective-permute-start.13 = (f32[8,256]{1,0:T(8,128)S(1)}, f32[8,256]{1,0:T(8,128)S(1)}, u32[]{:S(2)}, u32[]{:S(2)}) collective-permute-start(f32[8,256]{1,0:T(8,128)S(1)} %get-tuple-element.71), channel_id=1, source_target_pairs={{0,224},{1,225},{2,226},{3,227},{4,228},{5,229},{6,230},{7,231},{8... | collective-permute-start | bytes 24584 | tf_op jit(solution)/shard_map/ppermute | solution.py:402
  43.8 0.0 collective-permute-done.15.rc
  43.8 1.5 %level2_rows.1.rows = f32[192,1152]{1,0:T(8,128)S(1)} custom-call(f32[256,1152]{1,0:T(8,128)S(1)} %get-tuple-element.57.t, f32[768,896]{1,0:T(8,128)S(1)} %get-tuple-element.51.m1, f32[72,768]{1,0:T(8,128)S(1)} %collective-permute-done.14.rn, f32[72,768]{1,0:T(8,128)S(1)} %collective-permute-done.15.rc), custom_call_target="tpu_custom_call" | custom-call | flops 1724999936 | tf_op jit(solution)/shard_map/level2_rows/pallas_call | solution.py:382
  45.3 0.0 collective-permute-done.12.be
  45.3 0.7 %collective-permute-start.16 = (f32[128,768]{1,0:T(8,128)S(1)}, f32[128,768]{1,0:T(8,128)S(1)}, u32[]{:S(2)}, u32[]{:S(2)}) collective-permute-start(f32[128,768]{1,0:T(8,128)S(1)} %collective-permute-done.12.be), channel_id=1, source_target_pairs={{0,16},{1,17},{2,18},{3,19},{4,20},{5,21},{6,22},{7,23},{8,24},{9,... | collective-permute-start | bytes 1179656 | tf_op jit(solution)/shard_map/ppermute | solution.py:402
  45.9 0.1 collective-permute-start.11
  46.0 0.7 %collective-permute-start.17 = (f32[8,256]{1,0:T(8,128)S(1)}, f32[8,256]{1,0:T(8,128)S(1)}, u32[]{:S(2)}, u32[]{:S(2)}) collective-permute-start(f32[8,256]{1,0:T(8,128)S(1)} %collective-permute-done.13), channel_id=1, source_target_pairs={{0,1},{1,0},{2,3},{3,2},{4,5},{5,4},{6,7},{7,6},{8,9},{9,8},{10,11... | collective-permute-start | bytes 24584 | tf_op jit(solution)/shard_map/ppermute | solution.py:402
  46.7 0.2 collective-permute-start.18
  46.9 1.7 %collective-permute-start.19 = (f32[8,256]{1,0:T(8,128)S(1)}, f32[8,256]{1,0:T(8,128)S(1)}, u32[]{:S(2)}, u32[]{:S(2)}) collective-permute-start(f32[8,256]{1,0:T(8,128)S(1)} %collective-permute-done.13), channel_id=1, source_target_pairs={{0,33},{1,32},{2,35},{3,34},{4,37},{5,36},{6,39},{7,38},{8,41},{9,... | collective-permute-start | bytes 24584 | tf_op jit(solution)/shard_map/ppermute | solution.py:402
  48.7 2.7 %level3_rows.1 = (f32[192,1536]{1,0:T(8,128)}, f32[192,1536]{1,0:T(8,128)S(1)}, f32[192,128]{1,0:T(8,128)S(1)}) custom-call(f32[256,256]{1,0:T(8,128)S(1)} %get-tuple-element.66.minv, f32[256,256]{1,0:T(8,128)S(1)} %get-tuple-element.67.gii, f32[256,128]{1,0:T(8,128)S(1)} %get-tuple-element.68.th, f32[128,768]{1,0:T(8,128)S(1)} %get-tuple-element.58.ye, ...), custom_call_target="tpu_custom_call" | custom-call | flops 2875000064 | tf_op jit(solution)/shard_map/level3_rows/pallas_call | solution.py:382
  51.4 1.4 %collective-permute-start.20 = (f32[32,256]{1,0:T(8,128)S(1)}, f32[32,256]{1,0:T(8,128)S(1)}, u32[]{:S(2)}, u32[]{:S(2)}) collective-permute-start(f32[32,256]{1,0:T(8,128)S(1)} %constant_dynamic-update-slice_fusion.mine), channel_id=1, source_target_pairs={{0,16},{1,17},{2,18},{3,19},{4,20},{5,21},{6,22},{7,23},{8,24},{9,... | collective-permute-start | bytes 98312 | tf_op jit(solution)/shard_map/ppermute | solution.py:402
  52.7 0.9 %collective-permute-done.20.core = f32[32,256]{1,0:T(8,128)S(1)} collective-permute-done((f32[32,256]{1,0:T(8,128)S(1)}, f32[32,256]{1,0:T(8,128)S(1)}, u32[]{:S(2)}, u32[]{:S(2)}) %collective-permute-start.20) | collective-permute-done | bytes 32800 | tf_op jit(solution)/shard_map/ppermute | solution.py:402
  53.6 0.7 %couple.1 = f32[1,192]{1,0:T(1,128)} custom-call(f32[192,1536]{1,0:T(8,128)S(1)} %get-tuple-element.78.raw, f32[192,128]{1,0:T(8,128)S(1)} %get-tuple-element.81.h3, f32[32,256]{1,0:T(8,128)S(1)} %constant_dynamic-update-slice_fusion.mine, f32[32,256]{1,0:T(8,128)S(1)} %collective-permute-done.20.core), custom_call_target="tpu_custom_call" | custom-call | flops 805000000 | tf_op jit(solution)/shard_map/couple/pallas_call | solution.py:382
  (15 shorter events, 0.0 us)
Async XLA Ops:
  0.6 6.2 %collective-permute-start = (f32[512,512]{1,0:T(8,128)}, f32[512,512]{1,0:T(8,128)S(1)}, u32[]{:S(2)}, u32[]{:S(2)}) collective-permute-start(f32[512,512]{1,0:T(8,128)} %bitcast.6), channel_id=1, source_target_pairs={{0,16},{1,17},{2,18},{3,19},{4,20},{5,21},{6,22},{7,23},{8,24},{9,... | collective-permute-start | bytes 3145736 | tf_op jit(solution)/shard_map/ppermute | solution.py:402
  5.6 1.2 %collective-permute-start.1 = (f32[1,512]{1,0:T(1,128)S(1)}, f32[1,512]{1,0:T(1,128)S(1)}, u32[]{:S(2)}, u32[]{:S(2)}) collective-permute-start(f32[1,512]{1,0:T(1,128)S(1)} %bitcast_multiply_fusion.hown), channel_id=1, source_target_pairs={{0,16},{1,17},{2,18},{3,19},{4,20},{5,21},{6,22},{7,23},{8,24},{9,... | collective-permute-start | bytes 6152 | tf_op jit(solution)/shard_map/ppermute | solution.py:402
  5.6 1.2 %copy-start = (f32[1,1,512,512]{3,2,1,0:T(8,128)S(1)}, f32[1,1,512,512]{3,2,1,0:T(8,128)}, u32[]{:S(2)}) copy-start(f32[1,1,512,512]{3,2,1,0:T(8,128)} %param.4) | copy-start | bytes 3145732
  9.6 4.8 %collective-permute-start.2 = (f32[136,256]{1,0:T(8,128)S(1)}, f32[136,256]{1,0:T(8,128)S(1)}, u32[]{:S(2)}, u32[]{:S(2)}) collective-permute-start(f32[136,256]{1,0:T(8,128)S(1)} %get-tuple-element.45), channel_id=1, source_target_pairs={{0,1},{1,0},{2,3},{3,2},{4,5},{5,4},{6,7},{7,6},{8,9},{9,8},{10,11... | collective-permute-start | bytes 417800 | tf_op jit(solution)/shard_map/ppermute | solution.py:402
  11.9 9.2 %collective-permute-start.4 = (f32[128,512]{1,0:T(8,128)S(1)}, f32[128,512]{1,0:T(8,128)S(1)}, u32[]{:S(2)}, u32[]{:S(2)}) collective-permute-start(f32[128,512]{1,0:T(8,128)S(1)} %get-tuple-element.47), channel_id=1, source_target_pairs={{0,1},{1,0},{2,3},{3,2},{4,5},{5,4},{6,7},{7,6},{8,9},{9,8},{10,11... | collective-permute-start | bytes 786440 | tf_op jit(solution)/shard_map/ppermute | solution.py:402
  14.4 2.9 %collective-permute-start.3 = (f32[136,256]{1,0:T(8,128)S(1)}, f32[136,256]{1,0:T(8,128)S(1)}, u32[]{:S(2)}, u32[]{:S(2)}) collective-permute-start(f32[136,256]{1,0:T(8,128)S(1)} %collective-permute-done.2.xin), channel_id=1, source_target_pairs={{0,16},{1,17},{2,18},{3,19},{4,20},{5,21},{6,22},{7,23},{8,24},{9,... | collective-permute-start | bytes 417800 | tf_op jit(solution)/shard_map/ppermute | solution.py:402
  21.1 1.6 %collective-permute-start.5 = (f32[128,512]{1,0:T(8,128)S(1)}, f32[128,512]{1,0:T(8,128)S(1)}, u32[]{:S(2)}, u32[]{:S(2)}) collective-permute-start(f32[128,512]{1,0:T(8,128)S(1)} %collective-permute-done.4.xen), channel_id=1, source_target_pairs={{0,16},{1,17},{2,18},{3,19},{4,20},{5,21},{6,22},{7,23},{8,24},{9,... | collective-permute-start | bytes 786440 | tf_op jit(solution)/shard_map/ppermute | solution.py:402
  21.6 5.6 %collective-permute-start.8 = (f32[64,640]{1,0:T(8,128)S(1)}, f32[64,640]{1,0:T(8,128)S(1)}, u32[]{:S(2)}, u32[]{:S(2)}) collective-permute-start(f32[64,640]{1,0:T(8,128)S(1)} %get-tuple-element.60), channel_id=1, source_target_pairs={{0,1},{1,0},{2,3},{3,2},{4,5},{5,4},{6,7},{7,6},{8,9},{9,8},{10,11... | collective-permute-start | bytes 491528 | tf_op jit(solution)/shard_map/ppermute | solution.py:402
  23.5 5.1 %collective-permute-start.6 = (f32[136,256]{1,0:T(8,128)S(1)}, f32[136,256]{1,0:T(8,128)S(1)}, u32[]{:S(2)}, u32[]{:S(2)}) collective-permute-start(f32[136,256]{1,0:T(8,128)S(1)} %get-tuple-element.53.yi), channel_id=1, source_target_pairs={{0,1},{1,0},{2,3},{3,2},{4,5},{5,4},{6,7},{7,6},{8,9},{9,8},{10,11... | collective-permute-start | bytes 417800 | tf_op jit(solution)/shard_map/ppermute | solution.py:402
  23.8 4.9 %collective-permute-start.7 = (f32[72,256]{1,0:T(8,128)S(1)}, f32[72,256]{1,0:T(8,128)S(1)}, u32[]{:S(2)}, u32[]{:S(2)}) collective-permute-start(f32[72,256]{1,0:T(8,128)S(1)} %get-tuple-element.55), channel_id=1, source_target_pairs={{0,33},{1,32},{2,35},{3,34},{4,37},{5,36},{6,39},{7,38},{8,41},{9,... | collective-permute-start | bytes 221192 | tf_op jit(solution)/shard_map/ppermute | solution.py:402
  28.7 3.9 %collective-permute-start.9 = (f32[136,256]{1,0:T(8,128)S(1)}, f32[136,256]{1,0:T(8,128)S(1)}, u32[]{:S(2)}, u32[]{:S(2)}) collective-permute-start(f32[136,256]{1,0:T(8,128)S(1)} %collective-permute-done.6.a1), channel_id=1, source_target_pairs={{0,16},{1,17},{2,18},{3,19},{4,20},{5,21},{6,22},{7,23},{8,24},{9,... | collective-permute-start | bytes 417800 | tf_op jit(solution)/shard_map/ppermute | solution.py:402
  31.3 1.3 %collective-permute-start.10 = (f32[72,256]{1,0:T(8,128)S(1)}, f32[72,256]{1,0:T(8,128)S(1)}, u32[]{:S(2)}, u32[]{:S(2)}) collective-permute-start(f32[72,256]{1,0:T(8,128)S(1)} %collective-permute-done.7.a2), channel_id=1, source_target_pairs={{0,16},{1,17},{2,18},{3,19},{4,20},{5,21},{6,22},{7,23},{8,24},{9,... | collective-permute-start | bytes 221192 | tf_op jit(solution)/shard_map/ppermute | solution.py:402
  31.3 14.0 %collective-permute-start.12 = (f32[128,768]{1,0:T(8,128)S(1)}, f32[128,768]{1,0:T(8,128)S(1)}, u32[]{:S(2)}, u32[]{:S(2)}) collective-permute-start(f32[128,768]{1,0:T(8,128)S(1)} %get-tuple-element.61), channel_id=1, source_target_pairs={{0,32},{1,33},{2,34},{3,35},{4,36},{5,37},{6,38},{7,39},{8,40},{9,... | collective-permute-start | bytes 1179656 | tf_op jit(solution)/shard_map/ppermute | solution.py:402
  31.5 6.2 %collective-permute-start.14 = (f32[72,768]{1,0:T(8,128)S(1)}, f32[72,768]{1,0:T(8,128)S(1)}, u32[]{:S(2)}, u32[]{:S(2)}) collective-permute-start(f32[72,768]{1,0:T(8,128)S(1)} %get-tuple-element.73), channel_id=1, source_target_pairs={{0,1},{1,0},{2,3},{3,2},{4,5},{5,4},{6,7},{7,6},{8,9},{9,8},{10,11... | collective-permute-start | bytes 663560 | tf_op jit(solution)/shard_map/ppermute | solution.py:402
  37.7 6.1 %collective-permute-start.15 = (f32[72,768]{1,0:T(8,128)S(1)}, f32[72,768]{1,0:T(8,128)S(1)}, u32[]{:S(2)}, u32[]{:S(2)}) collective-permute-start(f32[72,768]{1,0:T(8,128)S(1)} %collective-permute-done.14.rn), channel_id=1, source_target_pairs={{0,16},{1,17},{2,18},{3,19},{4,20},{5,21},{6,22},{7,23},{8,24},{9,... | collective-permute-start | bytes 663560 | tf_op jit(solution)/shard_map/ppermute | solution.py:402
  39.4 5.9 %collective-permute-start.13 = (f32[8,256]{1,0:T(8,128)S(1)}, f32[8,256]{1,0:T(8,128)S(1)}, u32[]{:S(2)}, u32[]{:S(2)}) collective-permute-start(f32[8,256]{1,0:T(8,128)S(1)} %get-tuple-element.71), channel_id=1, source_target_pairs={{0,224},{1,225},{2,226},{3,227},{4,228},{5,229},{6,230},{7,231},{8... | collective-permute-start | bytes 24584 | tf_op jit(solution)/shard_map/ppermute | solution.py:402
  45.3 3.4 %collective-permute-start.16 = (f32[128,768]{1,0:T(8,128)S(1)}, f32[128,768]{1,0:T(8,128)S(1)}, u32[]{:S(2)}, u32[]{:S(2)}) collective-permute-start(f32[128,768]{1,0:T(8,128)S(1)} %collective-permute-done.12.be), channel_id=1, source_target_pairs={{0,16},{1,17},{2,18},{3,19},{4,20},{5,21},{6,22},{7,23},{8,24},{9,... | collective-permute-start | bytes 1179656 | tf_op jit(solution)/shard_map/ppermute | solution.py:402
  45.9 2.7 %collective-permute-start.11 = (f32[64,768]{1,0:T(8,128)S(1)}, f32[64,768]{1,0:T(8,128)S(1)}, u32[]{:S(2)}, u32[]{:S(2)}) collective-permute-start(f32[64,768]{1,0:T(8,128)S(1)} %get-tuple-element.70.yx), channel_id=1, source_target_pairs={{0,16},{1,17},{2,18},{3,19},{4,20},{5,21},{6,22},{7,23},{8,24},{9,... | collective-permute-start | bytes 589832 | tf_op jit(solution)/shard_map/ppermute | solution.py:402
  46.0 5.3 %collective-permute-start.17 = (f32[8,256]{1,0:T(8,128)S(1)}, f32[8,256]{1,0:T(8,128)S(1)}, u32[]{:S(2)}, u32[]{:S(2)}) collective-permute-start(f32[8,256]{1,0:T(8,128)S(1)} %collective-permute-done.13), channel_id=1, source_target_pairs={{0,1},{1,0},{2,3},{3,2},{4,5},{5,4},{6,7},{7,6},{8,9},{9,8},{10,11... | collective-permute-start | bytes 24584 | tf_op jit(solution)/shard_map/ppermute | solution.py:402
  46.7 4.6 %collective-permute-start.18 = (f32[8,256]{1,0:T(8,128)S(1)}, f32[8,256]{1,0:T(8,128)S(1)}, u32[]{:S(2)}, u32[]{:S(2)}) collective-permute-start(f32[8,256]{1,0:T(8,128)S(1)} %collective-permute-done.13), channel_id=1, source_target_pairs={{0,32},{1,33},{2,34},{3,35},{4,36},{5,37},{6,38},{7,39},{8,40},{9,... | collective-permute-start | bytes 24584 | tf_op jit(solution)/shard_map/ppermute | solution.py:402
  46.9 4.4 %collective-permute-start.19 = (f32[8,256]{1,0:T(8,128)S(1)}, f32[8,256]{1,0:T(8,128)S(1)}, u32[]{:S(2)}, u32[]{:S(2)}) collective-permute-start(f32[8,256]{1,0:T(8,128)S(1)} %collective-permute-done.13), channel_id=1, source_target_pairs={{0,33},{1,32},{2,35},{3,34},{4,37},{5,36},{6,39},{7,38},{8,41},{9,... | collective-permute-start | bytes 24584 | tf_op jit(solution)/shard_map/ppermute | solution.py:402
  51.4 2.2 %collective-permute-start.20 = (f32[32,256]{1,0:T(8,128)S(1)}, f32[32,256]{1,0:T(8,128)S(1)}, u32[]{:S(2)}, u32[]{:S(2)}) collective-permute-start(f32[32,256]{1,0:T(8,128)S(1)} %constant_dynamic-update-slice_fusion.mine), channel_id=1, source_target_pairs={{0,16},{1,17},{2,18},{3,19},{4,20},{5,21},{6,22},{7,23},{8,24},{9,... | collective-permute-start | bytes 98312 | tf_op jit(solution)/shard_map/ppermute | solution.py:402

commit v4 on v3

--- a/solution.py
+++ b/solution.py
@@ -486,7 +486,7 @@
         [(2 * S, 2 * S), (2 * S, 2 * S), (2 * S, S), (8, 2 * S)],
         [(2 * S, 2 * S)] * 3,
         [yi, yd, a1, k1, a2, k2, chip],
-        20.0,
+        0.3,
     )
     g0 = over_edge(hs)
     rc = over_core(after(rn, minv3))

time: 54.5 us -> 52.3 us (0.960)
  starting transfers between devices: 24.1 us -> 21.9 us
    ppermute x21, starting transfers between devices: 24.1 us -> 21.9 us  [send(): return lax.ppermute(value, ('gx', 'gy'), pairs)]
  transfers between devices with their start and end apart: 21 -> 21, of which waited for: 8 -> 7; matrix products, arithmetic and copies ran while one was open for 3% -> 3% of each run, Pallas kernels for 33% -> 35%
where the time goes in v4:
time: 52.3 us; the launch traced here: 52.1 us
  starting transfers between devices  21.9 us (42%)
  Pallas kernels  21.6 us (41%)
  waiting for transfers between devices  5.05 us (10%)
  other arithmetic  1.44 us (3%)
  local copies, waits for them, and re-layouts  1.39 us (3%)
  between operations  0.76 us (1%)
    ppermute x21, starting transfers between devices, send(): return lax.ppermute(value, ('gx', 'gy'), pairs)  21.9 us
    pallas_call x11, Pallas kernels, call(): pl.pallas_call(body, out_shape=[jax.ShapeDtypeStruct(o, f32) for o in out...  21.6 us
    ppermute x21, waiting for transfers between devices, send(): return lax.ppermute(value, ('gx', 'gy'), pairs)  5.05 us
    unnamed x5, local copies, waits for them, and re-layouts  1.23 us
  transfers between devices with their start and end apart: 21, of which 7 were waited for; matrix products, arithmetic and copies ran while one was open for 3% of the time, Pallas kernels for 35%

profile of v4, /device:TPU:1, one launch (start us, length us, event | category | flops | bytes accessed | tf_op | source)
XLA Modules:
  0.0 52.1 jit_solution(1041001426386628856)
XLA Ops:
  0.6 3.3 %collective-permute-start = (f32[512,512]{1,0:T(8,128)}, f32[512,512]{1,0:T(8,128)S(1)}, u32[]{:S(2)}, u32[]{:S(2)}) collective-permute-start(f32[512,512]{1,0:T(8,128)} %bitcast.6), channel_id=1, source_target_pairs={{0,16},{1,17},{2,18},{3,19},{4,20},{5,21},{6,22},{7,23},{8,24},{9,... | collective-permute-start | bytes 3145736 | tf_op jit(solution)/shard_map/ppermute | solution.py:402
  4.0 0.8 %select_reduce_fusion = f32[16]{0:T(128)S(1)} fusion(f32[8]{0:T(128)} %param.7, s32[16]{0:T(128)} %bitcast.10), kind=kLoop, calls=%fused_computation.4 | loop fusion | flops 368 | bytes 160 | tf_op jit(solution)/shard_map/reduce_sum | solution.py:446
  4.7 0.1 broadcast_in_dim.6
  4.8 0.1 reshape.27
  4.9 0.7 %bitcast_multiply_fusion.hown = f32[1,512]{1,0:T(1,128)S(1)} fusion(f32[1,512]{1,0:T(1,128)S(1)} %reshape.27, f32[1,1,512]{2,1,0:T(1,128)} %param.5), kind=kLoop, calls=%fused_computation.6 | loop fusion | flops 512 | bytes 6144 | tf_op jit(solution)/shard_map/mul | solution.py:449
  5.6 0.0 collective-permute-start.1
  5.6 1.2 %copy-done = f32[1,1,512,512]{3,2,1,0:T(8,128)S(1)} copy-done((f32[1,1,512,512]{3,2,1,0:T(8,128)S(1)}, f32[1,1,512,512]{3,2,1,0:T(8,128)}, u32[]{:S(2)}) %copy-start) | copy-done | bytes 1048600
  6.8 2.8 %level1_interface.1 = (f32[128,128]{1,0:T(8,128)S(1)}, f32[256,256]{1,0:T(8,128)S(1)}, f32[136,256]{1,0:T(8,128)S(1)}) custom-call(f32[512,512]{1,0:T(8,128)S(1)} %bitcast.8, f32[512,512]{1,0:T(8,128)S(1)} %collective-permute-done.oth, f32[1,512]{1,0:T(1,128)S(1)} %bitcast_multiply_fusion.hown, f32[1,512]{1,0:T(1,128)S(1)} %collective-permute-done.1.hoth, ...), custom_call_target="tpu_custom_call" | custom-call | flops 2875000064 | tf_op jit(solution)/shard_map/level1_interface/pallas_call | solution.py:382
  9.6 0.1 collective-permute-start.2
  9.7 2.2 %level1_map.1 = (f32[768,896]{1,0:T(8,128)S(1)}, f32[128,512]{1,0:T(8,128)S(1)}, f32[64,640]{1,0:T(8,128)S(1)}) custom-call(f32[512,512]{1,0:T(8,128)S(1)} %bitcast.9, f32[512,512]{1,0:T(8,128)S(1)} %collective-permute-done.oth, f32[1,512]{1,0:T(1,128)S(1)} %bitcast_multiply_fusion.hown, f32[1,512]{1,0:T(1,128)S(1)} %collective-permute-done.1.hoth, ...), custom_call_target="tpu_custom_call" | custom-call | flops 2300000000 | tf_op jit(solution)/shard_map/level1_map/pallas_call | solution.py:382
  11.9 1.5 %collective-permute-start.4 = (f32[128,512]{1,0:T(8,128)S(1)}, f32[128,512]{1,0:T(8,128)S(1)}, u32[]{:S(2)}, u32[]{:S(2)}) collective-permute-start(f32[128,512]{1,0:T(8,128)S(1)} %get-tuple-element.47), channel_id=1, source_target_pairs={{0,1},{1,0},{2,3},{3,2},{4,5},{5,4},{6,7},{7,6},{8,9},{9,8},{10,11... | collective-permute-start | bytes 786440 | tf_op jit(solution)/shard_map/ppermute | solution.py:402
  13.4 1.0 %collective-permute-done.2.xin = f32[136,256]{1,0:T(8,128)S(1)} collective-permute-done((f32[136,256]{1,0:T(8,128)S(1)}, f32[136,256]{1,0:T(8,128)S(1)}, u32[]{:S(2)}, u32[]{:S(2)}) %collective-permute-start.2) | collective-permute-done | bytes 139296 | tf_op jit(solution)/shard_map/ppermute | solution.py:402
  14.4 1.9 %collective-permute-start.3 = (f32[136,256]{1,0:T(8,128)S(1)}, f32[136,256]{1,0:T(8,128)S(1)}, u32[]{:S(2)}, u32[]{:S(2)}) collective-permute-start(f32[136,256]{1,0:T(8,128)S(1)} %collective-permute-done.2.xin), channel_id=1, source_target_pairs={{0,16},{1,17},{2,18},{3,19},{4,20},{5,21},{6,22},{7,23},{8,24},{9,... | collective-permute-start | bytes 417800 | tf_op jit(solution)/shard_map/ppermute | solution.py:402
  16.4 1.0 %collective-permute-done.3.xic = f32[136,256]{1,0:T(8,128)S(1)} collective-permute-done((f32[136,256]{1,0:T(8,128)S(1)}, f32[136,256]{1,0:T(8,128)S(1)}, u32[]{:S(2)}, u32[]{:S(2)}) %collective-permute-start.3) | collective-permute-done | bytes 139296 | tf_op jit(solution)/shard_map/ppermute | solution.py:402
  17.4 3.8 %level2_inverse.1 = (f32[256,256]{1,0:T(8,128)S(1)}, f32[256,256]{1,0:T(8,128)S(1)}) custom-call(f32[256,256]{1,0:T(8,128)S(1)} %get-tuple-element.44.pii, f32[136,256]{1,0:T(8,128)S(1)} %collective-permute-done.2.xin, f32[136,256]{1,0:T(8,128)S(1)} %collective-permute-done.3.xic), custom_call_target="tpu_custom_call" | custom-call | flops 575000000 | tf_op jit(solution)/shard_map/level2_inverse/pallas_call | solution.py:382
  21.1 0.5 collective-permute-start.5
  21.6 0.6 %collective-permute-start.8 = (f32[64,640]{1,0:T(8,128)S(1)}, f32[64,640]{1,0:T(8,128)S(1)}, u32[]{:S(2)}, u32[]{:S(2)}) collective-permute-start(f32[64,640]{1,0:T(8,128)S(1)} %get-tuple-element.60), channel_id=1, source_target_pairs={{0,1},{1,0},{2,3},{3,2},{4,5},{5,4},{6,7},{7,6},{8,9},{9,8},{10,11... | collective-permute-start | bytes 491528 | tf_op jit(solution)/shard_map/ppermute | solution.py:402
  22.2 0.6 %collective-permute-done.5.xec = f32[128,512]{1,0:T(8,128)S(1)} collective-permute-done((f32[128,512]{1,0:T(8,128)S(1)}, f32[128,512]{1,0:T(8,128)S(1)}, u32[]{:S(2)}, u32[]{:S(2)}) %collective-permute-start.5) | collective-permute-done | bytes 262176 | tf_op jit(solution)/shard_map/ppermute | solution.py:402
  22.8 0.8 %level2_interface.1 = (f32[136,256]{1,0:T(8,128)S(1)}, f32[72,256]{1,0:T(8,128)S(1)}, f32[128,128]{1,0:T(8,128)S(1)}) custom-call(f32[256,256]{1,0:T(8,128)S(1)} %get-tuple-element.56.minv, f32[256,256]{1,0:T(8,128)S(1)} %get-tuple-element.50.gii, f32[768,896]{1,0:T(8,128)S(1)} %get-tuple-element.51.m1, f32[136,256]{1,0:T(8,128)S(1)} %collective-permute-done.2.xin, ...), custom_call_target="tpu_custom_call" | custom-call | flops 1150000000 | tf_op jit(solution)/shard_map/level2_interface/pallas_call | solution.py:382
  23.5 0.3 collective-permute-start.6
  23.8 1.5 %collective-permute-start.7 = (f32[72,256]{1,0:T(8,128)S(1)}, f32[72,256]{1,0:T(8,128)S(1)}, u32[]{:S(2)}, u32[]{:S(2)}) collective-permute-start(f32[72,256]{1,0:T(8,128)S(1)} %get-tuple-element.55), channel_id=1, source_target_pairs={{0,33},{1,32},{2,35},{3,34},{4,37},{5,36},{6,39},{7,38},{8,41},{9,... | collective-permute-start | bytes 221192 | tf_op jit(solution)/shard_map/ppermute | solution.py:402
  25.3 1.8 %level2_rest.1 = (f32[256,1152]{1,0:T(8,128)S(1)}, f32[128,768]{1,0:T(8,128)S(1)}, f32[384,384]{1,0:T(8,128)S(1)}, f32[72,768]{1,0:T(8,128)S(1)}) custom-call(f32[256,256]{1,0:T(8,128)S(1)} %get-tuple-element.56.minv, f32[256,256]{1,0:T(8,128)S(1)} %get-tuple-element.50.gii, f32[768,896]{1,0:T(8,128)S(1)} %get-tuple-element.51.m1, ...), custom_call_target="tpu_custom_call" | custom-call | flops 11500000 | tf_op jit(solution)/shard_map/level2_rest/pallas_call | solution.py:382
  27.1 0.1 collective-permute-done.8.xln
  27.3 0.9 %level2_edge.1 = (f32[128,768]{1,0:T(8,128)S(1)}, f32[64,768]{1,0:T(8,128)S(1)}) custom-call(f32[256,1152]{1,0:T(8,128)S(1)} %get-tuple-element.57.t, f32[768,896]{1,0:T(8,128)S(1)} %get-tuple-element.51.m1, f32[128,768]{1,0:T(8,128)S(1)} %get-tuple-element.58.ye, f32[64,640]{1,0:T(8,128)S(1)} %collective-permute-done.8.xln), custom_call_target="tpu_custom_call" | custom-call | flops 11500000 | tf_op jit(solution)/shard_map/level2_edge/pallas_call | solution.py:382
  28.2 0.9 %collective-permute-start.14 = (f32[72,768]{1,0:T(8,128)S(1)}, f32[72,768]{1,0:T(8,128)S(1)}, u32[]{:S(2)}, u32[]{:S(2)}) collective-permute-start(f32[72,768]{1,0:T(8,128)S(1)} %get-tuple-element.73), channel_id=1, source_target_pairs={{0,1},{1,0},{2,3},{3,2},{4,5},{5,4},{6,7},{7,6},{8,9},{9,8},{10,11... | collective-permute-start | bytes 663560 | tf_op jit(solution)/shard_map/ppermute | solution.py:402
  29.1 0.0 collective-permute-done.7.a2
  29.1 0.0 collective-permute-done.6.a1
  29.1 2.2 %collective-permute-start.9 = (f32[136,256]{1,0:T(8,128)S(1)}, f32[136,256]{1,0:T(8,128)S(1)}, u32[]{:S(2)}, u32[]{:S(2)}) collective-permute-start(f32[136,256]{1,0:T(8,128)S(1)} %collective-permute-done.6.a1), channel_id=1, source_target_pairs={{0,16},{1,17},{2,18},{3,19},{4,20},{5,21},{6,22},{7,23},{8,24},{9,... | collective-permute-start | bytes 417800 | tf_op jit(solution)/shard_map/ppermute | solution.py:402
  31.3 0.0 collective-permute-start.10
  31.3 0.2 collective-permute-start.12
  31.5 1.0 %collective-permute-done.10.k2 = f32[72,256]{1,0:T(8,128)S(1)} collective-permute-done((f32[72,256]{1,0:T(8,128)S(1)}, f32[72,256]{1,0:T(8,128)S(1)}, u32[]{:S(2)}, u32[]{:S(2)}) %collective-permute-start.10) | collective-permute-done | bytes 73760 | tf_op jit(solution)/shard_map/ppermute | solution.py:402
  32.6 4.5 %level3_inverse.1 = (f32[256,256]{1,0:T(8,128)S(1)}, f32[256,256]{1,0:T(8,128)S(1)}, f32[256,128]{1,0:T(8,128)S(1)}, f32[8,256]{1,0:T(8,128)S(1)}) custom-call(f32[136,256]{1,0:T(8,128)S(1)} %get-tuple-element.53.yi, f32[128,128]{1,0:T(8,128)S(1)} %get-tuple-element.54.yd, f32[136,256]{1,0:T(8,128)S(1)} %collective-permute-done.6.a1, ...), custom_call_target="tpu_custom_call" | custom-call | flops 345000000 | tf_op jit(solution)/shard_map/level3_inverse/pallas_call | solution.py:382
  37.1 0.3 collective-permute-start.15
  37.3 4.0 %collective-permute-start.13 = (f32[8,256]{1,0:T(8,128)S(1)}, f32[8,256]{1,0:T(8,128)S(1)}, u32[]{:S(2)}, u32[]{:S(2)}) collective-permute-start(f32[8,256]{1,0:T(8,128)S(1)} %get-tuple-element.71), channel_id=1, source_target_pairs={{0,224},{1,225},{2,226},{3,227},{4,228},{5,229},{6,230},{7,231},{8... | collective-permute-start | bytes 24584 | tf_op jit(solution)/shard_map/ppermute | solution.py:402
  41.3 1.5 %level2_rows.1.rows = f32[192,1152]{1,0:T(8,128)S(1)} custom-call(f32[256,1152]{1,0:T(8,128)S(1)} %get-tuple-element.57.t, f32[768,896]{1,0:T(8,128)S(1)} %get-tuple-element.51.m1, f32[72,768]{1,0:T(8,128)S(1)} %collective-permute-done.14.rn, f32[72,768]{1,0:T(8,128)S(1)} %collective-permute-done.15.rc), custom_call_target="tpu_custom_call" | custom-call | flops 1724999936 | tf_op jit(solution)/shard_map/level2_rows/pallas_call | solution.py:382
  42.8 0.4 collective-permute-done.13
  43.2 0.0 collective-permute-done.12.be
  43.2 0.6 %collective-permute-start.16 = (f32[128,768]{1,0:T(8,128)S(1)}, f32[128,768]{1,0:T(8,128)S(1)}, u32[]{:S(2)}, u32[]{:S(2)}) collective-permute-start(f32[128,768]{1,0:T(8,128)S(1)} %collective-permute-done.12.be), channel_id=1, source_target_pairs={{0,16},{1,17},{2,18},{3,19},{4,20},{5,21},{6,22},{7,23},{8,24},{9,... | collective-permute-start | bytes 1179656 | tf_op jit(solution)/shard_map/ppermute | solution.py:402
  43.7 0.1 collective-permute-start.11
  43.8 0.7 %collective-permute-start.17 = (f32[8,256]{1,0:T(8,128)S(1)}, f32[8,256]{1,0:T(8,128)S(1)}, u32[]{:S(2)}, u32[]{:S(2)}) collective-permute-start(f32[8,256]{1,0:T(8,128)S(1)} %collective-permute-done.13), channel_id=1, source_target_pairs={{0,1},{1,0},{2,3},{3,2},{4,5},{5,4},{6,7},{7,6},{8,9},{9,8},{10,11... | collective-permute-start | bytes 24584 | tf_op jit(solution)/shard_map/ppermute | solution.py:402
  44.5 0.0 collective-permute-start.18
  44.5 1.9 %collective-permute-start.19 = (f32[8,256]{1,0:T(8,128)S(1)}, f32[8,256]{1,0:T(8,128)S(1)}, u32[]{:S(2)}, u32[]{:S(2)}) collective-permute-start(f32[8,256]{1,0:T(8,128)S(1)} %collective-permute-done.13), channel_id=1, source_target_pairs={{0,33},{1,32},{2,35},{3,34},{4,37},{5,36},{6,39},{7,38},{8,41},{9,... | collective-permute-start | bytes 24584 | tf_op jit(solution)/shard_map/ppermute | solution.py:402
  46.4 0.0 collective-permute-done.11.yk
  46.4 0.0 collective-permute-done.16.kb
  46.5 2.7 %level3_rows.1 = (f32[192,1536]{1,0:T(8,128)}, f32[192,1536]{1,0:T(8,128)S(1)}, f32[192,128]{1,0:T(8,128)S(1)}) custom-call(f32[256,256]{1,0:T(8,128)S(1)} %get-tuple-element.66.minv, f32[256,256]{1,0:T(8,128)S(1)} %get-tuple-element.67.gii, f32[256,128]{1,0:T(8,128)S(1)} %get-tuple-element.68.th, f32[128,768]{1,0:T(8,128)S(1)} %get-tuple-element.58.ye, ...), custom_call_target="tpu_custom_call" | custom-call | flops 2875000064 | tf_op jit(solution)/shard_map/level3_rows/pallas_call | solution.py:382
  49.2 1.4 %collective-permute-start.20 = (f32[32,256]{1,0:T(8,128)S(1)}, f32[32,256]{1,0:T(8,128)S(1)}, u32[]{:S(2)}, u32[]{:S(2)}) collective-permute-start(f32[32,256]{1,0:T(8,128)S(1)} %constant_dynamic-update-slice_fusion.mine), channel_id=1, source_target_pairs={{0,16},{1,17},{2,18},{3,19},{4,20},{5,21},{6,22},{7,23},{8,24},{9,... | collective-permute-start | bytes 98312 | tf_op jit(solution)/shard_map/ppermute | solution.py:402
  50.5 0.9 %collective-permute-done.20.core = f32[32,256]{1,0:T(8,128)S(1)} collective-permute-done((f32[32,256]{1,0:T(8,128)S(1)}, f32[32,256]{1,0:T(8,128)S(1)}, u32[]{:S(2)}, u32[]{:S(2)}) %collective-permute-start.20) | collective-permute-done | bytes 32800 | tf_op jit(solution)/shard_map/ppermute | solution.py:402
  51.4 0.8 %couple.1 = f32[1,192]{1,0:T(1,128)} custom-call(f32[192,1536]{1,0:T(8,128)S(1)} %get-tuple-element.78.raw, f32[192,128]{1,0:T(8,128)S(1)} %get-tuple-element.81.h3, f32[32,256]{1,0:T(8,128)S(1)} %constant_dynamic-update-slice_fusion.mine, f32[32,256]{1,0:T(8,128)S(1)} %collective-permute-done.20.core), custom_call_target="tpu_custom_call" | custom-call | flops 805000000 | tf_op jit(solution)/shard_map/couple/pallas_call | solution.py:382
  (15 shorter events, 0.0 us)
Async XLA Ops:
  0.6 6.2 %collective-permute-start = (f32[512,512]{1,0:T(8,128)}, f32[512,512]{1,0:T(8,128)S(1)}, u32[]{:S(2)}, u32[]{:S(2)}) collective-permute-start(f32[512,512]{1,0:T(8,128)} %bitcast.6), channel_id=1, source_target_pairs={{0,16},{1,17},{2,18},{3,19},{4,20},{5,21},{6,22},{7,23},{8,24},{9,... | collective-permute-start | bytes 3145736 | tf_op jit(solution)/shard_map/ppermute | solution.py:402
  5.6 1.2 %collective-permute-start.1 = (f32[1,512]{1,0:T(1,128)S(1)}, f32[1,512]{1,0:T(1,128)S(1)}, u32[]{:S(2)}, u32[]{:S(2)}) collective-permute-start(f32[1,512]{1,0:T(1,128)S(1)} %bitcast_multiply_fusion.hown), channel_id=1, source_target_pairs={{0,16},{1,17},{2,18},{3,19},{4,20},{5,21},{6,22},{7,23},{8,24},{9,... | collective-permute-start | bytes 6152 | tf_op jit(solution)/shard_map/ppermute | solution.py:402
  5.6 1.2 %copy-start = (f32[1,1,512,512]{3,2,1,0:T(8,128)S(1)}, f32[1,1,512,512]{3,2,1,0:T(8,128)}, u32[]{:S(2)}) copy-start(f32[1,1,512,512]{3,2,1,0:T(8,128)} %param.4) | copy-start | bytes 3145732
  9.6 4.8 %collective-permute-start.2 = (f32[136,256]{1,0:T(8,128)S(1)}, f32[136,256]{1,0:T(8,128)S(1)}, u32[]{:S(2)}, u32[]{:S(2)}) collective-permute-start(f32[136,256]{1,0:T(8,128)S(1)} %get-tuple-element.45), channel_id=1, source_target_pairs={{0,1},{1,0},{2,3},{3,2},{4,5},{5,4},{6,7},{7,6},{8,9},{9,8},{10,11... | collective-permute-start | bytes 417800 | tf_op jit(solution)/shard_map/ppermute | solution.py:402
  11.9 9.2 %collective-permute-start.4 = (f32[128,512]{1,0:T(8,128)S(1)}, f32[128,512]{1,0:T(8,128)S(1)}, u32[]{:S(2)}, u32[]{:S(2)}) collective-permute-start(f32[128,512]{1,0:T(8,128)S(1)} %get-tuple-element.47), channel_id=1, source_target_pairs={{0,1},{1,0},{2,3},{3,2},{4,5},{5,4},{6,7},{7,6},{8,9},{9,8},{10,11... | collective-permute-start | bytes 786440 | tf_op jit(solution)/shard_map/ppermute | solution.py:402
  14.4 2.9 %collective-permute-start.3 = (f32[136,256]{1,0:T(8,128)S(1)}, f32[136,256]{1,0:T(8,128)S(1)}, u32[]{:S(2)}, u32[]{:S(2)}) collective-permute-start(f32[136,256]{1,0:T(8,128)S(1)} %collective-permute-done.2.xin), channel_id=1, source_target_pairs={{0,16},{1,17},{2,18},{3,19},{4,20},{5,21},{6,22},{7,23},{8,24},{9,... | collective-permute-start | bytes 417800 | tf_op jit(solution)/shard_map/ppermute | solution.py:402
  21.1 1.6 %collective-permute-start.5 = (f32[128,512]{1,0:T(8,128)S(1)}, f32[128,512]{1,0:T(8,128)S(1)}, u32[]{:S(2)}, u32[]{:S(2)}) collective-permute-start(f32[128,512]{1,0:T(8,128)S(1)} %collective-permute-done.4.xen), channel_id=1, source_target_pairs={{0,16},{1,17},{2,18},{3,19},{4,20},{5,21},{6,22},{7,23},{8,24},{9,... | collective-permute-start | bytes 786440 | tf_op jit(solution)/shard_map/ppermute | solution.py:402
  21.6 5.6 %collective-permute-start.8 = (f32[64,640]{1,0:T(8,128)S(1)}, f32[64,640]{1,0:T(8,128)S(1)}, u32[]{:S(2)}, u32[]{:S(2)}) collective-permute-start(f32[64,640]{1,0:T(8,128)S(1)} %get-tuple-element.60), channel_id=1, source_target_pairs={{0,1},{1,0},{2,3},{3,2},{4,5},{5,4},{6,7},{7,6},{8,9},{9,8},{10,11... | collective-permute-start | bytes 491528 | tf_op jit(solution)/shard_map/ppermute | solution.py:402
  23.5 5.6 %collective-permute-start.6 = (f32[136,256]{1,0:T(8,128)S(1)}, f32[136,256]{1,0:T(8,128)S(1)}, u32[]{:S(2)}, u32[]{:S(2)}) collective-permute-start(f32[136,256]{1,0:T(8,128)S(1)} %get-tuple-element.53.yi), channel_id=1, source_target_pairs={{0,1},{1,0},{2,3},{3,2},{4,5},{5,4},{6,7},{7,6},{8,9},{9,8},{10,11... | collective-permute-start | bytes 417800 | tf_op jit(solution)/shard_map/ppermute | solution.py:402
  23.8 5.3 %collective-permute-start.7 = (f32[72,256]{1,0:T(8,128)S(1)}, f32[72,256]{1,0:T(8,128)S(1)}, u32[]{:S(2)}, u32[]{:S(2)}) collective-permute-start(f32[72,256]{1,0:T(8,128)S(1)} %get-tuple-element.55), channel_id=1, source_target_pairs={{0,33},{1,32},{2,35},{3,34},{4,37},{5,36},{6,39},{7,38},{8,41},{9,... | collective-permute-start | bytes 221192 | tf_op jit(solution)/shard_map/ppermute | solution.py:402
  28.2 8.9 %collective-permute-start.14 = (f32[72,768]{1,0:T(8,128)S(1)}, f32[72,768]{1,0:T(8,128)S(1)}, u32[]{:S(2)}, u32[]{:S(2)}) collective-permute-start(f32[72,768]{1,0:T(8,128)S(1)} %get-tuple-element.73), channel_id=1, source_target_pairs={{0,1},{1,0},{2,3},{3,2},{4,5},{5,4},{6,7},{7,6},{8,9},{9,8},{10,11... | collective-permute-start | bytes 663560 | tf_op jit(solution)/shard_map/ppermute | solution.py:402
  29.1 3.5 %collective-permute-start.9 = (f32[136,256]{1,0:T(8,128)S(1)}, f32[136,256]{1,0:T(8,128)S(1)}, u32[]{:S(2)}, u32[]{:S(2)}) collective-permute-start(f32[136,256]{1,0:T(8,128)S(1)} %collective-permute-done.6.a1), channel_id=1, source_target_pairs={{0,16},{1,17},{2,18},{3,19},{4,20},{5,21},{6,22},{7,23},{8,24},{9,... | collective-permute-start | bytes 417800 | tf_op jit(solution)/shard_map/ppermute | solution.py:402
  31.3 1.3 %collective-permute-start.10 = (f32[72,256]{1,0:T(8,128)S(1)}, f32[72,256]{1,0:T(8,128)S(1)}, u32[]{:S(2)}, u32[]{:S(2)}) collective-permute-start(f32[72,256]{1,0:T(8,128)S(1)} %collective-permute-done.7.a2), channel_id=1, source_target_pairs={{0,16},{1,17},{2,18},{3,19},{4,20},{5,21},{6,22},{7,23},{8,24},{9,... | collective-permute-start | bytes 221192 | tf_op jit(solution)/shard_map/ppermute | solution.py:402
  31.3 11.9 %collective-permute-start.12 = (f32[128,768]{1,0:T(8,128)S(1)}, f32[128,768]{1,0:T(8,128)S(1)}, u32[]{:S(2)}, u32[]{:S(2)}) collective-permute-start(f32[128,768]{1,0:T(8,128)S(1)} %get-tuple-element.61), channel_id=1, source_target_pairs={{0,32},{1,33},{2,34},{3,35},{4,36},{5,37},{6,38},{7,39},{8,40},{9,... | collective-permute-start | bytes 1179656 | tf_op jit(solution)/shard_map/ppermute | solution.py:402
  37.1 4.2 %collective-permute-start.15 = (f32[72,768]{1,0:T(8,128)S(1)}, f32[72,768]{1,0:T(8,128)S(1)}, u32[]{:S(2)}, u32[]{:S(2)}) collective-permute-start(f32[72,768]{1,0:T(8,128)S(1)} %collective-permute-done.14.rn), channel_id=1, source_target_pairs={{0,16},{1,17},{2,18},{3,19},{4,20},{5,21},{6,22},{7,23},{8,24},{9,... | collective-permute-start | bytes 663560 | tf_op jit(solution)/shard_map/ppermute | solution.py:402
  37.3 5.8 %collective-permute-start.13 = (f32[8,256]{1,0:T(8,128)S(1)}, f32[8,256]{1,0:T(8,128)S(1)}, u32[]{:S(2)}, u32[]{:S(2)}) collective-permute-start(f32[8,256]{1,0:T(8,128)S(1)} %get-tuple-element.71), channel_id=1, source_target_pairs={{0,224},{1,225},{2,226},{3,227},{4,228},{5,229},{6,230},{7,231},{8... | collective-permute-start | bytes 24584 | tf_op jit(solution)/shard_map/ppermute | solution.py:402
  43.2 3.3 %collective-permute-start.16 = (f32[128,768]{1,0:T(8,128)S(1)}, f32[128,768]{1,0:T(8,128)S(1)}, u32[]{:S(2)}, u32[]{:S(2)}) collective-permute-start(f32[128,768]{1,0:T(8,128)S(1)} %collective-permute-done.12.be), channel_id=1, source_target_pairs={{0,16},{1,17},{2,18},{3,19},{4,20},{5,21},{6,22},{7,23},{8,24},{9,... | collective-permute-start | bytes 1179656 | tf_op jit(solution)/shard_map/ppermute | solution.py:402
  43.7 2.7 %collective-permute-start.11 = (f32[64,768]{1,0:T(8,128)S(1)}, f32[64,768]{1,0:T(8,128)S(1)}, u32[]{:S(2)}, u32[]{:S(2)}) collective-permute-start(f32[64,768]{1,0:T(8,128)S(1)} %get-tuple-element.70.yx), channel_id=1, source_target_pairs={{0,16},{1,17},{2,18},{3,19},{4,20},{5,21},{6,22},{7,23},{8,24},{9,... | collective-permute-start | bytes 589832 | tf_op jit(solution)/shard_map/ppermute | solution.py:402
  43.8 5.3 %collective-permute-start.17 = (f32[8,256]{1,0:T(8,128)S(1)}, f32[8,256]{1,0:T(8,128)S(1)}, u32[]{:S(2)}, u32[]{:S(2)}) collective-permute-start(f32[8,256]{1,0:T(8,128)S(1)} %collective-permute-done.13), channel_id=1, source_target_pairs={{0,1},{1,0},{2,3},{3,2},{4,5},{5,4},{6,7},{7,6},{8,9},{9,8},{10,11... | collective-permute-start | bytes 24584 | tf_op jit(solution)/shard_map/ppermute | solution.py:402
  44.5 4.6 %collective-permute-start.18 = (f32[8,256]{1,0:T(8,128)S(1)}, f32[8,256]{1,0:T(8,128)S(1)}, u32[]{:S(2)}, u32[]{:S(2)}) collective-permute-start(f32[8,256]{1,0:T(8,128)S(1)} %collective-permute-done.13), channel_id=1, source_target_pairs={{0,32},{1,33},{2,34},{3,35},{4,36},{5,37},{6,38},{7,39},{8,40},{9,... | collective-permute-start | bytes 24584 | tf_op jit(solution)/shard_map/ppermute | solution.py:402
  44.5 4.6 %collective-permute-start.19 = (f32[8,256]{1,0:T(8,128)S(1)}, f32[8,256]{1,0:T(8,128)S(1)}, u32[]{:S(2)}, u32[]{:S(2)}) collective-permute-start(f32[8,256]{1,0:T(8,128)S(1)} %collective-permute-done.13), channel_id=1, source_target_pairs={{0,33},{1,32},{2,35},{3,34},{4,37},{5,36},{6,39},{7,38},{8,41},{9,... | collective-permute-start | bytes 24584 | tf_op jit(solution)/shard_map/ppermute | solution.py:402
  49.2 2.2 %collective-permute-start.20 = (f32[32,256]{1,0:T(8,128)S(1)}, f32[32,256]{1,0:T(8,128)S(1)}, u32[]{:S(2)}, u32[]{:S(2)}) collective-permute-start(f32[32,256]{1,0:T(8,128)S(1)} %constant_dynamic-update-slice_fusion.mine), channel_id=1, source_target_pairs={{0,16},{1,17},{2,18},{3,19},{4,20},{5,21},{6,22},{7,23},{8,24},{9,... | collective-permute-start | bytes 98312 | tf_op jit(solution)/shard_map/ppermute | solution.py:402

commit v5 on v4

--- a/solution.py
+++ b/solution.py
@@ -491,7 +491,7 @@
     g0 = over_edge(hs)
     rc = over_core(after(rn, minv3))
     yk = over_core(after(yx, minv3))
-    (rows,) = call(level2_rows, [(3 * H, 9 * S)], [(3 * H, 7 * S)], [t, m1, rn, rc], 1.5)
+    (rows,) = call(level2_rows, [(3 * H, 9 * S)], [(3 * H, 7 * S)], [t, m1, rn, after(rc, yk)], 1.5)
     bn, g0, rows = lax.optimization_barrier((bn, g0, rows))
     kb = over_core(bn)
     gx, gz, gd = over_x(g0), over_z(g0), over_xz(g0)

time: 52.3 us -> 52.1 us (level)
  no operation moved by 1% of the time
where the time goes in v5:
time: 52.1 us; the launch traced here: 52 us
  Pallas kernels  21.6 us (41%)
  starting transfers between devices  21.5 us (41%)
  waiting for transfers between devices  5.25 us (10%)
  other arithmetic  1.44 us (3%)
  local copies, waits for them, and re-layouts  1.39 us (3%)
  between operations  0.76 us (1%)
    pallas_call x11, Pallas kernels, call(): pl.pallas_call(body, out_shape=[jax.ShapeDtypeStruct(o, f32) for o in out...  21.6 us
    ppermute x21, starting transfers between devices, send(): return lax.ppermute(value, ('gx', 'gy'), pairs)  21.5 us
    ppermute x21, waiting for transfers between devices, send(): return lax.ppermute(value, ('gx', 'gy'), pairs)  5.25 us
    unnamed x5, local copies, waits for them, and re-layouts  1.23 us
  transfers between devices with their start and end apart: 21, of which 7 were waited for; matrix products, arithmetic and copies ran while one was open for 3% of the time, Pallas kernels for 35%

profile of v5, /device:TPU:1, one launch (start us, length us, event | category | flops | bytes accessed | tf_op | source)
XLA Modules:
  0.0 52.0 jit_solution(8316835197864366037)
XLA Ops:
  0.6 3.3 %collective-permute-start = (f32[512,512]{1,0:T(8,128)}, f32[512,512]{1,0:T(8,128)S(1)}, u32[]{:S(2)}, u32[]{:S(2)}) collective-permute-start(f32[512,512]{1,0:T(8,128)} %bitcast.6), channel_id=1, source_target_pairs={{0,16},{1,17},{2,18},{3,19},{4,20},{5,21},{6,22},{7,23},{8,24},{9,... | collective-permute-start | bytes 3145736 | tf_op jit(solution)/shard_map/ppermute | solution.py:402
  4.0 0.8 %select_reduce_fusion = f32[16]{0:T(128)S(1)} fusion(f32[8]{0:T(128)} %param.7, s32[16]{0:T(128)} %bitcast.10), kind=kLoop, calls=%fused_computation.4 | loop fusion | flops 368 | bytes 160 | tf_op jit(solution)/shard_map/reduce_sum | solution.py:446
  4.7 0.1 broadcast_in_dim.6
  4.8 0.1 reshape.27
  4.9 0.7 %bitcast_multiply_fusion.hown = f32[1,512]{1,0:T(1,128)S(1)} fusion(f32[1,512]{1,0:T(1,128)S(1)} %reshape.27, f32[1,1,512]{2,1,0:T(1,128)} %param.5), kind=kLoop, calls=%fused_computation.6 | loop fusion | flops 512 | bytes 6144 | tf_op jit(solution)/shard_map/mul | solution.py:449
  5.6 0.0 collective-permute-start.1
  5.6 1.2 %copy-done = f32[1,1,512,512]{3,2,1,0:T(8,128)S(1)} copy-done((f32[1,1,512,512]{3,2,1,0:T(8,128)S(1)}, f32[1,1,512,512]{3,2,1,0:T(8,128)}, u32[]{:S(2)}) %copy-start) | copy-done | bytes 1048600
  6.8 0.0 collective-permute-done.1.hoth
  6.8 2.8 %level1_interface.1 = (f32[128,128]{1,0:T(8,128)S(1)}, f32[256,256]{1,0:T(8,128)S(1)}, f32[136,256]{1,0:T(8,128)S(1)}) custom-call(f32[512,512]{1,0:T(8,128)S(1)} %bitcast.8, f32[512,512]{1,0:T(8,128)S(1)} %collective-permute-done.oth, f32[1,512]{1,0:T(1,128)S(1)} %bitcast_multiply_fusion.hown, f32[1,512]{1,0:T(1,128)S(1)} %collective-permute-done.1.hoth, ...), custom_call_target="tpu_custom_call" | custom-call | flops 2875000064 | tf_op jit(solution)/shard_map/level1_interface/pallas_call | solution.py:382
  9.6 0.1 collective-permute-start.2
  9.7 2.2 %level1_map.1 = (f32[768,896]{1,0:T(8,128)S(1)}, f32[128,512]{1,0:T(8,128)S(1)}, f32[64,640]{1,0:T(8,128)S(1)}) custom-call(f32[512,512]{1,0:T(8,128)S(1)} %bitcast.9, f32[512,512]{1,0:T(8,128)S(1)} %collective-permute-done.oth, f32[1,512]{1,0:T(1,128)S(1)} %bitcast_multiply_fusion.hown, f32[1,512]{1,0:T(1,128)S(1)} %collective-permute-done.1.hoth, ...), custom_call_target="tpu_custom_call" | custom-call | flops 2300000000 | tf_op jit(solution)/shard_map/level1_map/pallas_call | solution.py:382
  11.9 1.5 %collective-permute-start.4 = (f32[128,512]{1,0:T(8,128)S(1)}, f32[128,512]{1,0:T(8,128)S(1)}, u32[]{:S(2)}, u32[]{:S(2)}) collective-permute-start(f32[128,512]{1,0:T(8,128)S(1)} %get-tuple-element.48), channel_id=1, source_target_pairs={{0,1},{1,0},{2,3},{3,2},{4,5},{5,4},{6,7},{7,6},{8,9},{9,8},{10,11... | collective-permute-start | bytes 786440 | tf_op jit(solution)/shard_map/ppermute | solution.py:402
  13.4 1.0 %collective-permute-done.2.xin = f32[136,256]{1,0:T(8,128)S(1)} collective-permute-done((f32[136,256]{1,0:T(8,128)S(1)}, f32[136,256]{1,0:T(8,128)S(1)}, u32[]{:S(2)}, u32[]{:S(2)}) %collective-permute-start.2) | collective-permute-done | bytes 139296 | tf_op jit(solution)/shard_map/ppermute | solution.py:402
  14.4 1.9 %collective-permute-start.3 = (f32[136,256]{1,0:T(8,128)S(1)}, f32[136,256]{1,0:T(8,128)S(1)}, u32[]{:S(2)}, u32[]{:S(2)}) collective-permute-start(f32[136,256]{1,0:T(8,128)S(1)} %collective-permute-done.2.xin), channel_id=1, source_target_pairs={{0,16},{1,17},{2,18},{3,19},{4,20},{5,21},{6,22},{7,23},{8,24},{9,... | collective-permute-start | bytes 417800 | tf_op jit(solution)/shard_map/ppermute | solution.py:402
  16.4 1.0 %collective-permute-done.3.xic = f32[136,256]{1,0:T(8,128)S(1)} collective-permute-done((f32[136,256]{1,0:T(8,128)S(1)}, f32[136,256]{1,0:T(8,128)S(1)}, u32[]{:S(2)}, u32[]{:S(2)}) %collective-permute-start.3) | collective-permute-done | bytes 139296 | tf_op jit(solution)/shard_map/ppermute | solution.py:402
  17.4 3.8 %level2_inverse.1 = (f32[256,256]{1,0:T(8,128)S(1)}, f32[256,256]{1,0:T(8,128)S(1)}) custom-call(f32[256,256]{1,0:T(8,128)S(1)} %get-tuple-element.45.pii, f32[136,256]{1,0:T(8,128)S(1)} %collective-permute-done.2.xin, f32[136,256]{1,0:T(8,128)S(1)} %collective-permute-done.3.xic), custom_call_target="tpu_custom_call" | custom-call | flops 575000000 | tf_op jit(solution)/shard_map/level2_inverse/pallas_call | solution.py:382
  21.1 0.0 collective-permute-done.4.xen
  21.1 0.4 collective-permute-start.5
  21.6 0.6 %collective-permute-start.8 = (f32[64,640]{1,0:T(8,128)S(1)}, f32[64,640]{1,0:T(8,128)S(1)}, u32[]{:S(2)}, u32[]{:S(2)}) collective-permute-start(f32[64,640]{1,0:T(8,128)S(1)} %get-tuple-element.61), channel_id=1, source_target_pairs={{0,1},{1,0},{2,3},{3,2},{4,5},{5,4},{6,7},{7,6},{8,9},{9,8},{10,11... | collective-permute-start | bytes 491528 | tf_op jit(solution)/shard_map/ppermute | solution.py:402
  22.2 0.6 %collective-permute-done.5.xec = f32[128,512]{1,0:T(8,128)S(1)} collective-permute-done((f32[128,512]{1,0:T(8,128)S(1)}, f32[128,512]{1,0:T(8,128)S(1)}, u32[]{:S(2)}, u32[]{:S(2)}) %collective-permute-start.5) | collective-permute-done | bytes 262176 | tf_op jit(solution)/shard_map/ppermute | solution.py:402
  22.8 0.8 %level2_interface.1 = (f32[136,256]{1,0:T(8,128)S(1)}, f32[72,256]{1,0:T(8,128)S(1)}, f32[128,128]{1,0:T(8,128)S(1)}) custom-call(f32[256,256]{1,0:T(8,128)S(1)} %get-tuple-element.57.minv, f32[256,256]{1,0:T(8,128)S(1)} %get-tuple-element.51.gii, f32[768,896]{1,0:T(8,128)S(1)} %get-tuple-element.52.m1, f32[136,256]{1,0:T(8,128)S(1)} %collective-permute-done.2.xin, ...), custom_call_target="tpu_custom_call" | custom-call | flops 1150000000 | tf_op jit(solution)/shard_map/level2_interface/pallas_call | solution.py:382
  23.5 0.3 collective-permute-start.6
  23.8 1.5 %collective-permute-start.7 = (f32[72,256]{1,0:T(8,128)S(1)}, f32[72,256]{1,0:T(8,128)S(1)}, u32[]{:S(2)}, u32[]{:S(2)}) collective-permute-start(f32[72,256]{1,0:T(8,128)S(1)} %get-tuple-element.56), channel_id=1, source_target_pairs={{0,33},{1,32},{2,35},{3,34},{4,37},{5,36},{6,39},{7,38},{8,41},{9,... | collective-permute-start | bytes 221192 | tf_op jit(solution)/shard_map/ppermute | solution.py:402
  25.3 1.8 %level2_rest.1 = (f32[256,1152]{1,0:T(8,128)S(1)}, f32[128,768]{1,0:T(8,128)S(1)}, f32[384,384]{1,0:T(8,128)S(1)}, f32[72,768]{1,0:T(8,128)S(1)}) custom-call(f32[256,256]{1,0:T(8,128)S(1)} %get-tuple-element.57.minv, f32[256,256]{1,0:T(8,128)S(1)} %get-tuple-element.51.gii, f32[768,896]{1,0:T(8,128)S(1)} %get-tuple-element.52.m1, ...), custom_call_target="tpu_custom_call" | custom-call | flops 11500000 | tf_op jit(solution)/shard_map/level2_rest/pallas_call | solution.py:382
  27.1 0.1 collective-permute-done.8.xln
  27.2 0.9 %level2_edge.1 = (f32[128,768]{1,0:T(8,128)S(1)}, f32[64,768]{1,0:T(8,128)S(1)}) custom-call(f32[256,1152]{1,0:T(8,128)S(1)} %get-tuple-element.58.t, f32[768,896]{1,0:T(8,128)S(1)} %get-tuple-element.52.m1, f32[128,768]{1,0:T(8,128)S(1)} %get-tuple-element.59.ye, f32[64,640]{1,0:T(8,128)S(1)} %collective-permute-done.8.xln), custom_call_target="tpu_custom_call" | custom-call | flops 11500000 | tf_op jit(solution)/shard_map/level2_edge/pallas_call | solution.py:382
  28.2 0.9 %collective-permute-start.14 = (f32[72,768]{1,0:T(8,128)S(1)}, f32[72,768]{1,0:T(8,128)S(1)}, u32[]{:S(2)}, u32[]{:S(2)}) collective-permute-start(f32[72,768]{1,0:T(8,128)S(1)} %get-tuple-element.74), channel_id=1, source_target_pairs={{0,1},{1,0},{2,3},{3,2},{4,5},{5,4},{6,7},{7,6},{8,9},{9,8},{10,11... | collective-permute-start | bytes 663560 | tf_op jit(solution)/shard_map/ppermute | solution.py:402
  29.1 0.0 collective-permute-done.7.a2
  29.1 0.0 collective-permute-done.6.a1
  29.1 2.2 %collective-permute-start.9 = (f32[136,256]{1,0:T(8,128)S(1)}, f32[136,256]{1,0:T(8,128)S(1)}, u32[]{:S(2)}, u32[]{:S(2)}) collective-permute-start(f32[136,256]{1,0:T(8,128)S(1)} %collective-permute-done.6.a1), channel_id=1, source_target_pairs={{0,16},{1,17},{2,18},{3,19},{4,20},{5,21},{6,22},{7,23},{8,24},{9,... | collective-permute-start | bytes 417800 | tf_op jit(solution)/shard_map/ppermute | solution.py:402
  31.3 0.0 collective-permute-start.10
  31.3 0.2 collective-permute-start.12
  31.5 1.0 %collective-permute-done.10.k2 = f32[72,256]{1,0:T(8,128)S(1)} collective-permute-done((f32[72,256]{1,0:T(8,128)S(1)}, f32[72,256]{1,0:T(8,128)S(1)}, u32[]{:S(2)}, u32[]{:S(2)}) %collective-permute-start.10) | collective-permute-done | bytes 73760 | tf_op jit(solution)/shard_map/ppermute | solution.py:402
  32.6 4.5 %level3_inverse.1 = (f32[256,256]{1,0:T(8,128)S(1)}, f32[256,256]{1,0:T(8,128)S(1)}, f32[256,128]{1,0:T(8,128)S(1)}, f32[8,256]{1,0:T(8,128)S(1)}) custom-call(f32[136,256]{1,0:T(8,128)S(1)} %get-tuple-element.54.yi, f32[128,128]{1,0:T(8,128)S(1)} %get-tuple-element.55.yd, f32[136,256]{1,0:T(8,128)S(1)} %collective-permute-done.6.a1, ...), custom_call_target="tpu_custom_call" | custom-call | flops 345000000 | tf_op jit(solution)/shard_map/level3_inverse/pallas_call | solution.py:382
  37.1 0.0 collective-permute-done.14.rn
  37.1 0.3 collective-permute-start.15
  37.4 0.3 collective-permute-start.11
  37.7 3.8 %collective-permute-start.13 = (f32[8,256]{1,0:T(8,128)S(1)}, f32[8,256]{1,0:T(8,128)S(1)}, u32[]{:S(2)}, u32[]{:S(2)}) collective-permute-start(f32[8,256]{1,0:T(8,128)S(1)} %get-tuple-element.72), channel_id=1, source_target_pairs={{0,224},{1,225},{2,226},{3,227},{4,228},{5,229},{6,230},{7,231},{8... | collective-permute-start | bytes 24584 | tf_op jit(solution)/shard_map/ppermute | solution.py:402
  41.4 0.0 collective-permute-done.11.yk
  41.4 1.5 %level2_rows.1.rows = f32[192,1152]{1,0:T(8,128)S(1)} custom-call(f32[256,1152]{1,0:T(8,128)S(1)} %get-tuple-element.58.t, f32[768,896]{1,0:T(8,128)S(1)} %get-tuple-element.52.m1, f32[72,768]{1,0:T(8,128)S(1)} %collective-permute-done.14.rn, f32[72,768]{1,0:T(8,128)S(1)} %collective-permute-done.15.rc), custom_call_target="tpu_custom_call" | custom-call | flops 1724999936 | tf_op jit(solution)/shard_map/level2_rows/pallas_call | solution.py:382
  42.9 0.6 %collective-permute-done.13 = f32[8,256]{1,0:T(8,128)S(1)} collective-permute-done((f32[8,256]{1,0:T(8,128)S(1)}, f32[8,256]{1,0:T(8,128)S(1)}, u32[]{:S(2)}, u32[]{:S(2)}) %collective-permute-start.13) | collective-permute-done | bytes 8224 | tf_op jit(solution)/shard_map/ppermute | solution.py:402
  43.5 0.5 collective-permute-start.16
  44.0 1.9 %collective-permute-start.18 = (f32[8,256]{1,0:T(8,128)S(1)}, f32[8,256]{1,0:T(8,128)S(1)}, u32[]{:S(2)}, u32[]{:S(2)}) collective-permute-start(f32[8,256]{1,0:T(8,128)S(1)} %collective-permute-done.13), channel_id=1, source_target_pairs={{0,32},{1,33},{2,34},{3,35},{4,36},{5,37},{6,38},{7,39},{8,40},{9,... | collective-permute-start | bytes 24584 | tf_op jit(solution)/shard_map/ppermute | solution.py:402
  45.9 0.7 %collective-permute-start.17 = (f32[8,256]{1,0:T(8,128)S(1)}, f32[8,256]{1,0:T(8,128)S(1)}, u32[]{:S(2)}, u32[]{:S(2)}) collective-permute-start(f32[8,256]{1,0:T(8,128)S(1)} %collective-permute-done.13), channel_id=1, source_target_pairs={{0,1},{1,0},{2,3},{3,2},{4,5},{5,4},{6,7},{7,6},{8,9},{9,8},{10,11... | collective-permute-start | bytes 24584 | tf_op jit(solution)/shard_map/ppermute | solution.py:402
  46.6 2.7 %level3_rows.1 = (f32[192,1536]{1,0:T(8,128)}, f32[192,1536]{1,0:T(8,128)S(1)}, f32[192,128]{1,0:T(8,128)S(1)}) custom-call(f32[256,256]{1,0:T(8,128)S(1)} %get-tuple-element.67.minv, f32[256,256]{1,0:T(8,128)S(1)} %get-tuple-element.68.gii, f32[256,128]{1,0:T(8,128)S(1)} %get-tuple-element.69.th, f32[128,768]{1,0:T(8,128)S(1)} %get-tuple-element.59.ye, ...), custom_call_target="tpu_custom_call" | custom-call | flops 2875000064 | tf_op jit(solution)/shard_map/level3_rows/pallas_call | solution.py:382
  49.4 1.0 %collective-permute-start.20 = (f32[32,256]{1,0:T(8,128)S(1)}, f32[32,256]{1,0:T(8,128)S(1)}, u32[]{:S(2)}, u32[]{:S(2)}) collective-permute-start(f32[32,256]{1,0:T(8,128)S(1)} %constant_dynamic-update-slice_fusion.mine), channel_id=1, source_target_pairs={{0,16},{1,17},{2,18},{3,19},{4,20},{5,21},{6,22},{7,23},{8,24},{9,... | collective-permute-start | bytes 98312 | tf_op jit(solution)/shard_map/ppermute | solution.py:402
  50.4 0.9 %collective-permute-done.20.core = f32[32,256]{1,0:T(8,128)S(1)} collective-permute-done((f32[32,256]{1,0:T(8,128)S(1)}, f32[32,256]{1,0:T(8,128)S(1)}, u32[]{:S(2)}, u32[]{:S(2)}) %collective-permute-start.20) | collective-permute-done | bytes 32800 | tf_op jit(solution)/shard_map/ppermute | solution.py:402
  51.2 0.7 %couple.1 = f32[1,192]{1,0:T(1,128)} custom-call(f32[192,1536]{1,0:T(8,128)S(1)} %get-tuple-element.80.raw, f32[192,128]{1,0:T(8,128)S(1)} %get-tuple-element.83.h3, f32[32,256]{1,0:T(8,128)S(1)} %constant_dynamic-update-slice_fusion.mine, f32[32,256]{1,0:T(8,128)S(1)} %collective-permute-done.20.core), custom_call_target="tpu_custom_call" | custom-call | flops 805000000 | tf_op jit(solution)/shard_map/couple/pallas_call | solution.py:382
  (15 shorter events, 0.0 us)
Async XLA Ops:
  0.6 6.2 %collective-permute-start = (f32[512,512]{1,0:T(8,128)}, f32[512,512]{1,0:T(8,128)S(1)}, u32[]{:S(2)}, u32[]{:S(2)}) collective-permute-start(f32[512,512]{1,0:T(8,128)} %bitcast.6), channel_id=1, source_target_pairs={{0,16},{1,17},{2,18},{3,19},{4,20},{5,21},{6,22},{7,23},{8,24},{9,... | collective-permute-start | bytes 3145736 | tf_op jit(solution)/shard_map/ppermute | solution.py:402
  5.6 1.2 %collective-permute-start.1 = (f32[1,512]{1,0:T(1,128)S(1)}, f32[1,512]{1,0:T(1,128)S(1)}, u32[]{:S(2)}, u32[]{:S(2)}) collective-permute-start(f32[1,512]{1,0:T(1,128)S(1)} %bitcast_multiply_fusion.hown), channel_id=1, source_target_pairs={{0,16},{1,17},{2,18},{3,19},{4,20},{5,21},{6,22},{7,23},{8,24},{9,... | collective-permute-start | bytes 6152 | tf_op jit(solution)/shard_map/ppermute | solution.py:402
  5.6 1.2 %copy-start = (f32[1,1,512,512]{3,2,1,0:T(8,128)S(1)}, f32[1,1,512,512]{3,2,1,0:T(8,128)}, u32[]{:S(2)}) copy-start(f32[1,1,512,512]{3,2,1,0:T(8,128)} %param.4) | copy-start | bytes 3145732
  9.6 4.8 %collective-permute-start.2 = (f32[136,256]{1,0:T(8,128)S(1)}, f32[136,256]{1,0:T(8,128)S(1)}, u32[]{:S(2)}, u32[]{:S(2)}) collective-permute-start(f32[136,256]{1,0:T(8,128)S(1)} %get-tuple-element.46), channel_id=1, source_target_pairs={{0,1},{1,0},{2,3},{3,2},{4,5},{5,4},{6,7},{7,6},{8,9},{9,8},{10,11... | collective-permute-start | bytes 417800 | tf_op jit(solution)/shard_map/ppermute | solution.py:402
  11.9 9.2 %collective-permute-start.4 = (f32[128,512]{1,0:T(8,128)S(1)}, f32[128,512]{1,0:T(8,128)S(1)}, u32[]{:S(2)}, u32[]{:S(2)}) collective-permute-start(f32[128,512]{1,0:T(8,128)S(1)} %get-tuple-element.48), channel_id=1, source_target_pairs={{0,1},{1,0},{2,3},{3,2},{4,5},{5,4},{6,7},{7,6},{8,9},{9,8},{10,11... | collective-permute-start | bytes 786440 | tf_op jit(solution)/shard_map/ppermute | solution.py:402
  14.4 2.9 %collective-permute-start.3 = (f32[136,256]{1,0:T(8,128)S(1)}, f32[136,256]{1,0:T(8,128)S(1)}, u32[]{:S(2)}, u32[]{:S(2)}) collective-permute-start(f32[136,256]{1,0:T(8,128)S(1)} %collective-permute-done.2.xin), channel_id=1, source_target_pairs={{0,16},{1,17},{2,18},{3,19},{4,20},{5,21},{6,22},{7,23},{8,24},{9,... | collective-permute-start | bytes 417800 | tf_op jit(solution)/shard_map/ppermute | solution.py:402
  21.1 1.6 %collective-permute-start.5 = (f32[128,512]{1,0:T(8,128)S(1)}, f32[128,512]{1,0:T(8,128)S(1)}, u32[]{:S(2)}, u32[]{:S(2)}) collective-permute-start(f32[128,512]{1,0:T(8,128)S(1)} %collective-permute-done.4.xen), channel_id=1, source_target_pairs={{0,16},{1,17},{2,18},{3,19},{4,20},{5,21},{6,22},{7,23},{8,24},{9,... | collective-permute-start | bytes 786440 | tf_op jit(solution)/shard_map/ppermute | solution.py:402
  21.6 5.6 %collective-permute-start.8 = (f32[64,640]{1,0:T(8,128)S(1)}, f32[64,640]{1,0:T(8,128)S(1)}, u32[]{:S(2)}, u32[]{:S(2)}) collective-permute-start(f32[64,640]{1,0:T(8,128)S(1)} %get-tuple-element.61), channel_id=1, source_target_pairs={{0,1},{1,0},{2,3},{3,2},{4,5},{5,4},{6,7},{7,6},{8,9},{9,8},{10,11... | collective-permute-start | bytes 491528 | tf_op jit(solution)/shard_map/ppermute | solution.py:402
  23.5 5.6 %collective-permute-start.6 = (f32[136,256]{1,0:T(8,128)S(1)}, f32[136,256]{1,0:T(8,128)S(1)}, u32[]{:S(2)}, u32[]{:S(2)}) collective-permute-start(f32[136,256]{1,0:T(8,128)S(1)} %get-tuple-element.54.yi), channel_id=1, source_target_pairs={{0,1},{1,0},{2,3},{3,2},{4,5},{5,4},{6,7},{7,6},{8,9},{9,8},{10,11... | collective-permute-start | bytes 417800 | tf_op jit(solution)/shard_map/ppermute | solution.py:402
  23.8 5.3 %collective-permute-start.7 = (f32[72,256]{1,0:T(8,128)S(1)}, f32[72,256]{1,0:T(8,128)S(1)}, u32[]{:S(2)}, u32[]{:S(2)}) collective-permute-start(f32[72,256]{1,0:T(8,128)S(1)} %get-tuple-element.56), channel_id=1, source_target_pairs={{0,33},{1,32},{2,35},{3,34},{4,37},{5,36},{6,39},{7,38},{8,41},{9,... | collective-permute-start | bytes 221192 | tf_op jit(solution)/shard_map/ppermute | solution.py:402
  28.2 8.9 %collective-permute-start.14 = (f32[72,768]{1,0:T(8,128)S(1)}, f32[72,768]{1,0:T(8,128)S(1)}, u32[]{:S(2)}, u32[]{:S(2)}) collective-permute-start(f32[72,768]{1,0:T(8,128)S(1)} %get-tuple-element.74), channel_id=1, source_target_pairs={{0,1},{1,0},{2,3},{3,2},{4,5},{5,4},{6,7},{7,6},{8,9},{9,8},{10,11... | collective-permute-start | bytes 663560 | tf_op jit(solution)/shard_map/ppermute | solution.py:402
  29.1 3.4 %collective-permute-start.9 = (f32[136,256]{1,0:T(8,128)S(1)}, f32[136,256]{1,0:T(8,128)S(1)}, u32[]{:S(2)}, u32[]{:S(2)}) collective-permute-start(f32[136,256]{1,0:T(8,128)S(1)} %collective-permute-done.6.a1), channel_id=1, source_target_pairs={{0,16},{1,17},{2,18},{3,19},{4,20},{5,21},{6,22},{7,23},{8,24},{9,... | collective-permute-start | bytes 417800 | tf_op jit(solution)/shard_map/ppermute | solution.py:402
  31.3 1.3 %collective-permute-start.10 = (f32[72,256]{1,0:T(8,128)S(1)}, f32[72,256]{1,0:T(8,128)S(1)}, u32[]{:S(2)}, u32[]{:S(2)}) collective-permute-start(f32[72,256]{1,0:T(8,128)S(1)} %collective-permute-done.7.a2), channel_id=1, source_target_pairs={{0,16},{1,17},{2,18},{3,19},{4,20},{5,21},{6,22},{7,23},{8,24},{9,... | collective-permute-start | bytes 221192 | tf_op jit(solution)/shard_map/ppermute | solution.py:402
  31.3 12.2 %collective-permute-start.12 = (f32[128,768]{1,0:T(8,128)S(1)}, f32[128,768]{1,0:T(8,128)S(1)}, u32[]{:S(2)}, u32[]{:S(2)}) collective-permute-start(f32[128,768]{1,0:T(8,128)S(1)} %get-tuple-element.62), channel_id=1, source_target_pairs={{0,32},{1,33},{2,34},{3,35},{4,36},{5,37},{6,38},{7,39},{8,40},{9,... | collective-permute-start | bytes 1179656 | tf_op jit(solution)/shard_map/ppermute | solution.py:402
  37.1 4.3 %collective-permute-start.15 = (f32[72,768]{1,0:T(8,128)S(1)}, f32[72,768]{1,0:T(8,128)S(1)}, u32[]{:S(2)}, u32[]{:S(2)}) collective-permute-start(f32[72,768]{1,0:T(8,128)S(1)} %collective-permute-done.14.rn), channel_id=1, source_target_pairs={{0,16},{1,17},{2,18},{3,19},{4,20},{5,21},{6,22},{7,23},{8,24},{9,... | collective-permute-start | bytes 663560 | tf_op jit(solution)/shard_map/ppermute | solution.py:402
  37.4 4.1 %collective-permute-start.11 = (f32[64,768]{1,0:T(8,128)S(1)}, f32[64,768]{1,0:T(8,128)S(1)}, u32[]{:S(2)}, u32[]{:S(2)}) collective-permute-start(f32[64,768]{1,0:T(8,128)S(1)} %get-tuple-element.71.yx), channel_id=1, source_target_pairs={{0,16},{1,17},{2,18},{3,19},{4,20},{5,21},{6,22},{7,23},{8,24},{9,... | collective-permute-start | bytes 589832 | tf_op jit(solution)/shard_map/ppermute | solution.py:402
  37.7 5.8 %collective-permute-start.13 = (f32[8,256]{1,0:T(8,128)S(1)}, f32[8,256]{1,0:T(8,128)S(1)}, u32[]{:S(2)}, u32[]{:S(2)}) collective-permute-start(f32[8,256]{1,0:T(8,128)S(1)} %get-tuple-element.72), channel_id=1, source_target_pairs={{0,224},{1,225},{2,226},{3,227},{4,228},{5,229},{6,230},{7,231},{8... | collective-permute-start | bytes 24584 | tf_op jit(solution)/shard_map/ppermute | solution.py:402
  43.5 3.2 %collective-permute-start.16 = (f32[128,768]{1,0:T(8,128)S(1)}, f32[128,768]{1,0:T(8,128)S(1)}, u32[]{:S(2)}, u32[]{:S(2)}) collective-permute-start(f32[128,768]{1,0:T(8,128)S(1)} %collective-permute-done.12.be), channel_id=1, source_target_pairs={{0,16},{1,17},{2,18},{3,19},{4,20},{5,21},{6,22},{7,23},{8,24},{9,... | collective-permute-start | bytes 1179656 | tf_op jit(solution)/shard_map/ppermute | solution.py:402
  44.0 5.3 %collective-permute-start.19 = (f32[8,256]{1,0:T(8,128)S(1)}, f32[8,256]{1,0:T(8,128)S(1)}, u32[]{:S(2)}, u32[]{:S(2)}) collective-permute-start(f32[8,256]{1,0:T(8,128)S(1)} %collective-permute-done.13), channel_id=1, source_target_pairs={{0,33},{1,32},{2,35},{3,34},{4,37},{5,36},{6,39},{7,38},{8,41},{9,... | collective-permute-start | bytes 24584 | tf_op jit(solution)/shard_map/ppermute | solution.py:402
  44.0 5.3 %collective-permute-start.18 = (f32[8,256]{1,0:T(8,128)S(1)}, f32[8,256]{1,0:T(8,128)S(1)}, u32[]{:S(2)}, u32[]{:S(2)}) collective-permute-start(f32[8,256]{1,0:T(8,128)S(1)} %collective-permute-done.13), channel_id=1, source_target_pairs={{0,32},{1,33},{2,34},{3,35},{4,36},{5,37},{6,38},{7,39},{8,40},{9,... | collective-permute-start | bytes 24584 | tf_op jit(solution)/shard_map/ppermute | solution.py:402
  45.9 3.4 %collective-permute-start.17 = (f32[8,256]{1,0:T(8,128)S(1)}, f32[8,256]{1,0:T(8,128)S(1)}, u32[]{:S(2)}, u32[]{:S(2)}) collective-permute-start(f32[8,256]{1,0:T(8,128)S(1)} %collective-permute-done.13), channel_id=1, source_target_pairs={{0,1},{1,0},{2,3},{3,2},{4,5},{5,4},{6,7},{7,6},{8,9},{9,8},{10,11... | collective-permute-start | bytes 24584 | tf_op jit(solution)/shard_map/ppermute | solution.py:402
  49.4 1.9 %collective-permute-start.20 = (f32[32,256]{1,0:T(8,128)S(1)}, f32[32,256]{1,0:T(8,128)S(1)}, u32[]{:S(2)}, u32[]{:S(2)}) collective-permute-start(f32[32,256]{1,0:T(8,128)S(1)} %constant_dynamic-update-slice_fusion.mine), channel_id=1, source_target_pairs={{0,16},{1,17},{2,18},{3,19},{4,20},{5,21},{6,22},{7,23},{8,24},{9,... | collective-permute-start | bytes 98312 | tf_op jit(solution)/shard_map/ppermute | solution.py:402

commit v6 on v5

--- a/solution.py
+++ b/solution.py
@@ -480,7 +480,7 @@
     a1, a2, _, chip = lax.optimization_barrier((a1, a2, be, chip))
     k1, k2 = over_core(a1), over_core(a2)
     bn = over_z(be)
-    rn = over_x(after(rr, be))
+    rn = over_x(after(rr, xln))
     minv3, gii3, th, hs = call(
         level3_inverse,
         [(2 * S, 2 * S), (2 * S, 2 * S), (2 * S, S), (8, 2 * S)],

time: 52.1 us -> 52.9 us (1.015)
  transfers between devices with their start and end apart: 21 -> 21, of which waited for: 7 -> 7; matrix products, arithmetic and copies ran while one was open for 3% -> 3% of each run, Pallas kernels for 35% -> 34%
where the time goes in v6:
time: 52.9 us; the launch traced here: 52.8 us
  starting transfers between devices  21.9 us (41%)
  Pallas kernels  21.6 us (41%)
  waiting for transfers between devices  5.62 us (11%)
  other arithmetic  1.44 us (3%)
  local copies, waits for them, and re-layouts  1.39 us (3%)
  between operations  0.77 us (1%)
    ppermute x21, starting transfers between devices, send(): return lax.ppermute(value, ('gx', 'gy'), pairs)  21.9 us
    pallas_call x11, Pallas kernels, call(): pl.pallas_call(body, out_shape=[jax.ShapeDtypeStruct(o, f32) for o in out...  21.6 us
    ppermute x21, waiting for transfers between devices, send(): return lax.ppermute(value, ('gx', 'gy'), pairs)  5.62 us
    unnamed x5, local copies, waits for them, and re-layouts  1.23 us
  transfers between devices with their start and end apart: 21, of which 7 were waited for; matrix products, arithmetic and copies ran while one was open for 3% of the time, Pallas kernels for 34%

profile of v6, /device:TPU:1, one launch (start us, length us, event | category | flops | bytes accessed | tf_op | source)
XLA Modules:
  0.0 52.8 jit_solution(8383329505517999979)
XLA Ops:
  0.6 3.3 %collective-permute-start = (f32[512,512]{1,0:T(8,128)}, f32[512,512]{1,0:T(8,128)S(1)}, u32[]{:S(2)}, u32[]{:S(2)}) collective-permute-start(f32[512,512]{1,0:T(8,128)} %bitcast.6), channel_id=1, source_target_pairs={{0,16},{1,17},{2,18},{3,19},{4,20},{5,21},{6,22},{7,23},{8,24},{9,... | collective-permute-start | bytes 3145736 | tf_op jit(solution)/shard_map/ppermute | solution.py:402
  4.0 0.8 %select_reduce_fusion = f32[16]{0:T(128)S(1)} fusion(f32[8]{0:T(128)} %param.7, s32[16]{0:T(128)} %bitcast.10), kind=kLoop, calls=%fused_computation.4 | loop fusion | flops 368 | bytes 160 | tf_op jit(solution)/shard_map/reduce_sum | solution.py:446
  4.7 0.1 broadcast_in_dim.6
  4.8 0.1 reshape.27
  4.9 0.7 %bitcast_multiply_fusion.hown = f32[1,512]{1,0:T(1,128)S(1)} fusion(f32[1,512]{1,0:T(1,128)S(1)} %reshape.27, f32[1,1,512]{2,1,0:T(1,128)} %param.5), kind=kLoop, calls=%fused_computation.6 | loop fusion | flops 512 | bytes 6144 | tf_op jit(solution)/shard_map/mul | solution.py:449
  5.6 0.0 collective-permute-start.1
  5.6 1.2 %copy-done = f32[1,1,512,512]{3,2,1,0:T(8,128)S(1)} copy-done((f32[1,1,512,512]{3,2,1,0:T(8,128)S(1)}, f32[1,1,512,512]{3,2,1,0:T(8,128)}, u32[]{:S(2)}) %copy-start) | copy-done | bytes 1048600
  6.8 0.0 collective-permute-done.1.hoth
  6.8 0.0 collective-permute-done.oth
  6.8 2.8 %level1_interface.1 = (f32[128,128]{1,0:T(8,128)S(1)}, f32[256,256]{1,0:T(8,128)S(1)}, f32[136,256]{1,0:T(8,128)S(1)}) custom-call(f32[512,512]{1,0:T(8,128)S(1)} %bitcast.8, f32[512,512]{1,0:T(8,128)S(1)} %collective-permute-done.oth, f32[1,512]{1,0:T(1,128)S(1)} %bitcast_multiply_fusion.hown, f32[1,512]{1,0:T(1,128)S(1)} %collective-permute-done.1.hoth, ...), custom_call_target="tpu_custom_call" | custom-call | flops 2875000064 | tf_op jit(solution)/shard_map/level1_interface/pallas_call | solution.py:382
  9.6 0.1 collective-permute-start.2
  9.7 2.2 %level1_map.1 = (f32[768,896]{1,0:T(8,128)S(1)}, f32[128,512]{1,0:T(8,128)S(1)}, f32[64,640]{1,0:T(8,128)S(1)}) custom-call(f32[512,512]{1,0:T(8,128)S(1)} %bitcast.9, f32[512,512]{1,0:T(8,128)S(1)} %collective-permute-done.oth, f32[1,512]{1,0:T(1,128)S(1)} %bitcast_multiply_fusion.hown, f32[1,512]{1,0:T(1,128)S(1)} %collective-permute-done.1.hoth, ...), custom_call_target="tpu_custom_call" | custom-call | flops 2300000000 | tf_op jit(solution)/shard_map/level1_map/pallas_call | solution.py:382
  11.9 1.5 %collective-permute-start.4 = (f32[128,512]{1,0:T(8,128)S(1)}, f32[128,512]{1,0:T(8,128)S(1)}, u32[]{:S(2)}, u32[]{:S(2)}) collective-permute-start(f32[128,512]{1,0:T(8,128)S(1)} %get-tuple-element.48), channel_id=1, source_target_pairs={{0,1},{1,0},{2,3},{3,2},{4,5},{5,4},{6,7},{7,6},{8,9},{9,8},{10,11... | collective-permute-start | bytes 786440 | tf_op jit(solution)/shard_map/ppermute | solution.py:402
  13.4 1.0 %collective-permute-done.2.xin = f32[136,256]{1,0:T(8,128)S(1)} collective-permute-done((f32[136,256]{1,0:T(8,128)S(1)}, f32[136,256]{1,0:T(8,128)S(1)}, u32[]{:S(2)}, u32[]{:S(2)}) %collective-permute-start.2) | collective-permute-done | bytes 139296 | tf_op jit(solution)/shard_map/ppermute | solution.py:402
  14.4 1.9 %collective-permute-start.3 = (f32[136,256]{1,0:T(8,128)S(1)}, f32[136,256]{1,0:T(8,128)S(1)}, u32[]{:S(2)}, u32[]{:S(2)}) collective-permute-start(f32[136,256]{1,0:T(8,128)S(1)} %collective-permute-done.2.xin), channel_id=1, source_target_pairs={{0,16},{1,17},{2,18},{3,19},{4,20},{5,21},{6,22},{7,23},{8,24},{9,... | collective-permute-start | bytes 417800 | tf_op jit(solution)/shard_map/ppermute | solution.py:402
  16.4 1.0 %collective-permute-done.3.xic = f32[136,256]{1,0:T(8,128)S(1)} collective-permute-done((f32[136,256]{1,0:T(8,128)S(1)}, f32[136,256]{1,0:T(8,128)S(1)}, u32[]{:S(2)}, u32[]{:S(2)}) %collective-permute-start.3) | collective-permute-done | bytes 139296 | tf_op jit(solution)/shard_map/ppermute | solution.py:402
  17.4 3.8 %level2_inverse.1 = (f32[256,256]{1,0:T(8,128)S(1)}, f32[256,256]{1,0:T(8,128)S(1)}) custom-call(f32[256,256]{1,0:T(8,128)S(1)} %get-tuple-element.45.pii, f32[136,256]{1,0:T(8,128)S(1)} %collective-permute-done.2.xin, f32[136,256]{1,0:T(8,128)S(1)} %collective-permute-done.3.xic), custom_call_target="tpu_custom_call" | custom-call | flops 575000000 | tf_op jit(solution)/shard_map/level2_inverse/pallas_call | solution.py:382
  21.1 0.4 collective-permute-start.5
  21.6 0.6 %collective-permute-start.8 = (f32[64,640]{1,0:T(8,128)S(1)}, f32[64,640]{1,0:T(8,128)S(1)}, u32[]{:S(2)}, u32[]{:S(2)}) collective-permute-start(f32[64,640]{1,0:T(8,128)S(1)} %get-tuple-element.61), channel_id=1, source_target_pairs={{0,1},{1,0},{2,3},{3,2},{4,5},{5,4},{6,7},{7,6},{8,9},{9,8},{10,11... | collective-permute-start | bytes 491528 | tf_op jit(solution)/shard_map/ppermute | solution.py:402
  22.2 0.6 %collective-permute-done.5.xec = f32[128,512]{1,0:T(8,128)S(1)} collective-permute-done((f32[128,512]{1,0:T(8,128)S(1)}, f32[128,512]{1,0:T(8,128)S(1)}, u32[]{:S(2)}, u32[]{:S(2)}) %collective-permute-start.5) | collective-permute-done | bytes 262176 | tf_op jit(solution)/shard_map/ppermute | solution.py:402
  22.8 0.8 %level2_interface.1 = (f32[136,256]{1,0:T(8,128)S(1)}, f32[72,256]{1,0:T(8,128)S(1)}, f32[128,128]{1,0:T(8,128)S(1)}) custom-call(f32[256,256]{1,0:T(8,128)S(1)} %get-tuple-element.57.minv, f32[256,256]{1,0:T(8,128)S(1)} %get-tuple-element.51.gii, f32[768,896]{1,0:T(8,128)S(1)} %get-tuple-element.52.m1, f32[136,256]{1,0:T(8,128)S(1)} %collective-permute-done.2.xin, ...), custom_call_target="tpu_custom_call" | custom-call | flops 1150000000 | tf_op jit(solution)/shard_map/level2_interface/pallas_call | solution.py:382
  23.5 0.3 collective-permute-start.6
  23.8 1.5 %collective-permute-start.7 = (f32[72,256]{1,0:T(8,128)S(1)}, f32[72,256]{1,0:T(8,128)S(1)}, u32[]{:S(2)}, u32[]{:S(2)}) collective-permute-start(f32[72,256]{1,0:T(8,128)S(1)} %get-tuple-element.56), channel_id=1, source_target_pairs={{0,33},{1,32},{2,35},{3,34},{4,37},{5,36},{6,39},{7,38},{8,41},{9,... | collective-permute-start | bytes 221192 | tf_op jit(solution)/shard_map/ppermute | solution.py:402
  25.3 1.8 %level2_rest.1 = (f32[256,1152]{1,0:T(8,128)S(1)}, f32[128,768]{1,0:T(8,128)S(1)}, f32[384,384]{1,0:T(8,128)S(1)}, f32[72,768]{1,0:T(8,128)S(1)}) custom-call(f32[256,256]{1,0:T(8,128)S(1)} %get-tuple-element.57.minv, f32[256,256]{1,0:T(8,128)S(1)} %get-tuple-element.51.gii, f32[768,896]{1,0:T(8,128)S(1)} %get-tuple-element.52.m1, ...), custom_call_target="tpu_custom_call" | custom-call | flops 11500000 | tf_op jit(solution)/shard_map/level2_rest/pallas_call | solution.py:382
  27.1 0.1 collective-permute-done.8.xln
  27.2 0.9 %collective-permute-start.14 = (f32[72,768]{1,0:T(8,128)S(1)}, f32[72,768]{1,0:T(8,128)S(1)}, u32[]{:S(2)}, u32[]{:S(2)}) collective-permute-start(f32[72,768]{1,0:T(8,128)S(1)} %get-tuple-element.74), channel_id=1, source_target_pairs={{0,1},{1,0},{2,3},{3,2},{4,5},{5,4},{6,7},{7,6},{8,9},{9,8},{10,11... | collective-permute-start | bytes 663560 | tf_op jit(solution)/shard_map/ppermute | solution.py:402
  28.1 0.9 %level2_edge.1 = (f32[128,768]{1,0:T(8,128)S(1)}, f32[64,768]{1,0:T(8,128)S(1)}) custom-call(f32[256,1152]{1,0:T(8,128)S(1)} %get-tuple-element.58.t, f32[768,896]{1,0:T(8,128)S(1)} %get-tuple-element.52.m1, f32[128,768]{1,0:T(8,128)S(1)} %get-tuple-element.59.ye, f32[64,640]{1,0:T(8,128)S(1)} %collective-permute-done.8.xln), custom_call_target="tpu_custom_call" | custom-call | flops 11500000 | tf_op jit(solution)/shard_map/level2_edge/pallas_call | solution.py:382
  29.1 0.0 collective-permute-done.6.a1
  29.1 3.0 %collective-permute-start.9 = (f32[136,256]{1,0:T(8,128)S(1)}, f32[136,256]{1,0:T(8,128)S(1)}, u32[]{:S(2)}, u32[]{:S(2)}) collective-permute-start(f32[136,256]{1,0:T(8,128)S(1)} %collective-permute-done.6.a1), channel_id=1, source_target_pairs={{0,16},{1,17},{2,18},{3,19},{4,20},{5,21},{6,22},{7,23},{8,24},{9,... | collective-permute-start | bytes 417800 | tf_op jit(solution)/shard_map/ppermute | solution.py:402
  32.2 0.0 collective-permute-start.10
  32.2 0.0 collective-permute-start.12
  32.2 1.2 %collective-permute-done.10.k2 = f32[72,256]{1,0:T(8,128)S(1)} collective-permute-done((f32[72,256]{1,0:T(8,128)S(1)}, f32[72,256]{1,0:T(8,128)S(1)}, u32[]{:S(2)}, u32[]{:S(2)}) %collective-permute-start.10) | collective-permute-done | bytes 73760 | tf_op jit(solution)/shard_map/ppermute | solution.py:402
  33.4 4.5 %level3_inverse.1 = (f32[256,256]{1,0:T(8,128)S(1)}, f32[256,256]{1,0:T(8,128)S(1)}, f32[256,128]{1,0:T(8,128)S(1)}, f32[8,256]{1,0:T(8,128)S(1)}) custom-call(f32[136,256]{1,0:T(8,128)S(1)} %get-tuple-element.54.yi, f32[128,128]{1,0:T(8,128)S(1)} %get-tuple-element.55.yd, f32[136,256]{1,0:T(8,128)S(1)} %collective-permute-done.6.a1, ...), custom_call_target="tpu_custom_call" | custom-call | flops 345000000 | tf_op jit(solution)/shard_map/level3_inverse/pallas_call | solution.py:382
  37.9 0.3 collective-permute-start.15
  38.2 0.3 collective-permute-start.11
  38.5 3.6 %collective-permute-start.13 = (f32[8,256]{1,0:T(8,128)S(1)}, f32[8,256]{1,0:T(8,128)S(1)}, u32[]{:S(2)}, u32[]{:S(2)}) collective-permute-start(f32[8,256]{1,0:T(8,128)S(1)} %get-tuple-element.72), channel_id=1, source_target_pairs={{0,224},{1,225},{2,226},{3,227},{4,228},{5,229},{6,230},{7,231},{8... | collective-permute-start | bytes 24584 | tf_op jit(solution)/shard_map/ppermute | solution.py:402
  42.1 1.5 %level2_rows.1.rows = f32[192,1152]{1,0:T(8,128)S(1)} custom-call(f32[256,1152]{1,0:T(8,128)S(1)} %get-tuple-element.58.t, f32[768,896]{1,0:T(8,128)S(1)} %get-tuple-element.52.m1, f32[72,768]{1,0:T(8,128)S(1)} %collective-permute-done.14.rn, f32[72,768]{1,0:T(8,128)S(1)} %collective-permute-done.15.rc), custom_call_target="tpu_custom_call" | custom-call | flops 1724999936 | tf_op jit(solution)/shard_map/level2_rows/pallas_call | solution.py:382
  43.6 0.8 %collective-permute-done.13 = f32[8,256]{1,0:T(8,128)S(1)} collective-permute-done((f32[8,256]{1,0:T(8,128)S(1)}, f32[8,256]{1,0:T(8,128)S(1)}, u32[]{:S(2)}, u32[]{:S(2)}) %collective-permute-start.13) | collective-permute-done | bytes 8224 | tf_op jit(solution)/shard_map/ppermute | solution.py:402
  44.3 0.0 collective-permute-done.12.be
  44.4 0.3 collective-permute-start.16
  44.7 0.0 collective-permute-start.19
  44.7 2.0 %collective-permute-start.18 = (f32[8,256]{1,0:T(8,128)S(1)}, f32[8,256]{1,0:T(8,128)S(1)}, u32[]{:S(2)}, u32[]{:S(2)}) collective-permute-start(f32[8,256]{1,0:T(8,128)S(1)} %collective-permute-done.13), channel_id=1, source_target_pairs={{0,32},{1,33},{2,34},{3,35},{4,36},{5,37},{6,38},{7,39},{8,40},{9,... | collective-permute-start | bytes 24584 | tf_op jit(solution)/shard_map/ppermute | solution.py:402
  46.6 0.7 %collective-permute-start.17 = (f32[8,256]{1,0:T(8,128)S(1)}, f32[8,256]{1,0:T(8,128)S(1)}, u32[]{:S(2)}, u32[]{:S(2)}) collective-permute-start(f32[8,256]{1,0:T(8,128)S(1)} %collective-permute-done.13), channel_id=1, source_target_pairs={{0,1},{1,0},{2,3},{3,2},{4,5},{5,4},{6,7},{7,6},{8,9},{9,8},{10,11... | collective-permute-start | bytes 24584 | tf_op jit(solution)/shard_map/ppermute | solution.py:402
  47.3 0.0 collective-permute-done.16.kb
  47.3 2.7 %level3_rows.1 = (f32[192,1536]{1,0:T(8,128)}, f32[192,1536]{1,0:T(8,128)S(1)}, f32[192,128]{1,0:T(8,128)S(1)}) custom-call(f32[256,256]{1,0:T(8,128)S(1)} %get-tuple-element.67.minv, f32[256,256]{1,0:T(8,128)S(1)} %get-tuple-element.68.gii, f32[256,128]{1,0:T(8,128)S(1)} %get-tuple-element.69.th, f32[128,768]{1,0:T(8,128)S(1)} %get-tuple-element.59.ye, ...), custom_call_target="tpu_custom_call" | custom-call | flops 2875000064 | tf_op jit(solution)/shard_map/level3_rows/pallas_call | solution.py:382
  50.0 1.1 %collective-permute-start.20 = (f32[32,256]{1,0:T(8,128)S(1)}, f32[32,256]{1,0:T(8,128)S(1)}, u32[]{:S(2)}, u32[]{:S(2)}) collective-permute-start(f32[32,256]{1,0:T(8,128)S(1)} %constant_dynamic-update-slice_fusion.mine), channel_id=1, source_target_pairs={{0,16},{1,17},{2,18},{3,19},{4,20},{5,21},{6,22},{7,23},{8,24},{9,... | collective-permute-start | bytes 98312 | tf_op jit(solution)/shard_map/ppermute | solution.py:402
  51.2 0.9 %collective-permute-done.20.core = f32[32,256]{1,0:T(8,128)S(1)} collective-permute-done((f32[32,256]{1,0:T(8,128)S(1)}, f32[32,256]{1,0:T(8,128)S(1)}, u32[]{:S(2)}, u32[]{:S(2)}) %collective-permute-start.20) | collective-permute-done | bytes 32800 | tf_op jit(solution)/shard_map/ppermute | solution.py:402
  52.0 0.7 %couple.1 = f32[1,192]{1,0:T(1,128)} custom-call(f32[192,1536]{1,0:T(8,128)S(1)} %get-tuple-element.80.raw, f32[192,128]{1,0:T(8,128)S(1)} %get-tuple-element.83.h3, f32[32,256]{1,0:T(8,128)S(1)} %constant_dynamic-update-slice_fusion.mine, f32[32,256]{1,0:T(8,128)S(1)} %collective-permute-done.20.core), custom_call_target="tpu_custom_call" | custom-call | flops 805000000 | tf_op jit(solution)/shard_map/couple/pallas_call | solution.py:382
  (15 shorter events, 0.0 us)
Async XLA Ops:
  0.6 6.2 %collective-permute-start = (f32[512,512]{1,0:T(8,128)}, f32[512,512]{1,0:T(8,128)S(1)}, u32[]{:S(2)}, u32[]{:S(2)}) collective-permute-start(f32[512,512]{1,0:T(8,128)} %bitcast.6), channel_id=1, source_target_pairs={{0,16},{1,17},{2,18},{3,19},{4,20},{5,21},{6,22},{7,23},{8,24},{9,... | collective-permute-start | bytes 3145736 | tf_op jit(solution)/shard_map/ppermute | solution.py:402
  5.6 1.2 %collective-permute-start.1 = (f32[1,512]{1,0:T(1,128)S(1)}, f32[1,512]{1,0:T(1,128)S(1)}, u32[]{:S(2)}, u32[]{:S(2)}) collective-permute-start(f32[1,512]{1,0:T(1,128)S(1)} %bitcast_multiply_fusion.hown), channel_id=1, source_target_pairs={{0,16},{1,17},{2,18},{3,19},{4,20},{5,21},{6,22},{7,23},{8,24},{9,... | collective-permute-start | bytes 6152 | tf_op jit(solution)/shard_map/ppermute | solution.py:402
  5.6 1.2 %copy-start = (f32[1,1,512,512]{3,2,1,0:T(8,128)S(1)}, f32[1,1,512,512]{3,2,1,0:T(8,128)}, u32[]{:S(2)}) copy-start(f32[1,1,512,512]{3,2,1,0:T(8,128)} %param.4) | copy-start | bytes 3145732
  9.6 4.8 %collective-permute-start.2 = (f32[136,256]{1,0:T(8,128)S(1)}, f32[136,256]{1,0:T(8,128)S(1)}, u32[]{:S(2)}, u32[]{:S(2)}) collective-permute-start(f32[136,256]{1,0:T(8,128)S(1)} %get-tuple-element.46), channel_id=1, source_target_pairs={{0,1},{1,0},{2,3},{3,2},{4,5},{5,4},{6,7},{7,6},{8,9},{9,8},{10,11... | collective-permute-start | bytes 417800 | tf_op jit(solution)/shard_map/ppermute | solution.py:402
  11.9 9.2 %collective-permute-start.4 = (f32[128,512]{1,0:T(8,128)S(1)}, f32[128,512]{1,0:T(8,128)S(1)}, u32[]{:S(2)}, u32[]{:S(2)}) collective-permute-start(f32[128,512]{1,0:T(8,128)S(1)} %get-tuple-element.48), channel_id=1, source_target_pairs={{0,1},{1,0},{2,3},{3,2},{4,5},{5,4},{6,7},{7,6},{8,9},{9,8},{10,11... | collective-permute-start | bytes 786440 | tf_op jit(solution)/shard_map/ppermute | solution.py:402
  14.4 2.9 %collective-permute-start.3 = (f32[136,256]{1,0:T(8,128)S(1)}, f32[136,256]{1,0:T(8,128)S(1)}, u32[]{:S(2)}, u32[]{:S(2)}) collective-permute-start(f32[136,256]{1,0:T(8,128)S(1)} %collective-permute-done.2.xin), channel_id=1, source_target_pairs={{0,16},{1,17},{2,18},{3,19},{4,20},{5,21},{6,22},{7,23},{8,24},{9,... | collective-permute-start | bytes 417800 | tf_op jit(solution)/shard_map/ppermute | solution.py:402
  21.1 1.6 %collective-permute-start.5 = (f32[128,512]{1,0:T(8,128)S(1)}, f32[128,512]{1,0:T(8,128)S(1)}, u32[]{:S(2)}, u32[]{:S(2)}) collective-permute-start(f32[128,512]{1,0:T(8,128)S(1)} %collective-permute-done.4.xen), channel_id=1, source_target_pairs={{0,16},{1,17},{2,18},{3,19},{4,20},{5,21},{6,22},{7,23},{8,24},{9,... | collective-permute-start | bytes 786440 | tf_op jit(solution)/shard_map/ppermute | solution.py:402
  21.6 5.6 %collective-permute-start.8 = (f32[64,640]{1,0:T(8,128)S(1)}, f32[64,640]{1,0:T(8,128)S(1)}, u32[]{:S(2)}, u32[]{:S(2)}) collective-permute-start(f32[64,640]{1,0:T(8,128)S(1)} %get-tuple-element.61), channel_id=1, source_target_pairs={{0,1},{1,0},{2,3},{3,2},{4,5},{5,4},{6,7},{7,6},{8,9},{9,8},{10,11... | collective-permute-start | bytes 491528 | tf_op jit(solution)/shard_map/ppermute | solution.py:402
  23.5 5.6 %collective-permute-start.6 = (f32[136,256]{1,0:T(8,128)S(1)}, f32[136,256]{1,0:T(8,128)S(1)}, u32[]{:S(2)}, u32[]{:S(2)}) collective-permute-start(f32[136,256]{1,0:T(8,128)S(1)} %get-tuple-element.54.yi), channel_id=1, source_target_pairs={{0,1},{1,0},{2,3},{3,2},{4,5},{5,4},{6,7},{7,6},{8,9},{9,8},{10,11... | collective-permute-start | bytes 417800 | tf_op jit(solution)/shard_map/ppermute | solution.py:402
  23.8 5.3 %collective-permute-start.7 = (f32[72,256]{1,0:T(8,128)S(1)}, f32[72,256]{1,0:T(8,128)S(1)}, u32[]{:S(2)}, u32[]{:S(2)}) collective-permute-start(f32[72,256]{1,0:T(8,128)S(1)} %get-tuple-element.56), channel_id=1, source_target_pairs={{0,33},{1,32},{2,35},{3,34},{4,37},{5,36},{6,39},{7,38},{8,41},{9,... | collective-permute-start | bytes 221192 | tf_op jit(solution)/shard_map/ppermute | solution.py:402
  27.2 10.7 %collective-permute-start.14 = (f32[72,768]{1,0:T(8,128)S(1)}, f32[72,768]{1,0:T(8,128)S(1)}, u32[]{:S(2)}, u32[]{:S(2)}) collective-permute-start(f32[72,768]{1,0:T(8,128)S(1)} %get-tuple-element.74), channel_id=1, source_target_pairs={{0,1},{1,0},{2,3},{3,2},{4,5},{5,4},{6,7},{7,6},{8,9},{9,8},{10,11... | collective-permute-start | bytes 663560 | tf_op jit(solution)/shard_map/ppermute | solution.py:402
  29.1 4.3 %collective-permute-start.9 = (f32[136,256]{1,0:T(8,128)S(1)}, f32[136,256]{1,0:T(8,128)S(1)}, u32[]{:S(2)}, u32[]{:S(2)}) collective-permute-start(f32[136,256]{1,0:T(8,128)S(1)} %collective-permute-done.6.a1), channel_id=1, source_target_pairs={{0,16},{1,17},{2,18},{3,19},{4,20},{5,21},{6,22},{7,23},{8,24},{9,... | collective-permute-start | bytes 417800 | tf_op jit(solution)/shard_map/ppermute | solution.py:402
  32.2 1.3 %collective-permute-start.10 = (f32[72,256]{1,0:T(8,128)S(1)}, f32[72,256]{1,0:T(8,128)S(1)}, u32[]{:S(2)}, u32[]{:S(2)}) collective-permute-start(f32[72,256]{1,0:T(8,128)S(1)} %collective-permute-done.7.a2), channel_id=1, source_target_pairs={{0,16},{1,17},{2,18},{3,19},{4,20},{5,21},{6,22},{7,23},{8,24},{9,... | collective-permute-start | bytes 221192 | tf_op jit(solution)/shard_map/ppermute | solution.py:402
  32.2 12.2 %collective-permute-start.12 = (f32[128,768]{1,0:T(8,128)S(1)}, f32[128,768]{1,0:T(8,128)S(1)}, u32[]{:S(2)}, u32[]{:S(2)}) collective-permute-start(f32[128,768]{1,0:T(8,128)S(1)} %get-tuple-element.62), channel_id=1, source_target_pairs={{0,32},{1,33},{2,34},{3,35},{4,36},{5,37},{6,38},{7,39},{8,40},{9,... | collective-permute-start | bytes 1179656 | tf_op jit(solution)/shard_map/ppermute | solution.py:402
  37.9 4.2 %collective-permute-start.15 = (f32[72,768]{1,0:T(8,128)S(1)}, f32[72,768]{1,0:T(8,128)S(1)}, u32[]{:S(2)}, u32[]{:S(2)}) collective-permute-start(f32[72,768]{1,0:T(8,128)S(1)} %collective-permute-done.14.rn), channel_id=1, source_target_pairs={{0,16},{1,17},{2,18},{3,19},{4,20},{5,21},{6,22},{7,23},{8,24},{9,... | collective-permute-start | bytes 663560 | tf_op jit(solution)/shard_map/ppermute | solution.py:402
  38.2 3.9 %collective-permute-start.11 = (f32[64,768]{1,0:T(8,128)S(1)}, f32[64,768]{1,0:T(8,128)S(1)}, u32[]{:S(2)}, u32[]{:S(2)}) collective-permute-start(f32[64,768]{1,0:T(8,128)S(1)} %get-tuple-element.71.yx), channel_id=1, source_target_pairs={{0,16},{1,17},{2,18},{3,19},{4,20},{5,21},{6,22},{7,23},{8,24},{9,... | collective-permute-start | bytes 589832 | tf_op jit(solution)/shard_map/ppermute | solution.py:402
  38.5 5.8 %collective-permute-start.13 = (f32[8,256]{1,0:T(8,128)S(1)}, f32[8,256]{1,0:T(8,128)S(1)}, u32[]{:S(2)}, u32[]{:S(2)}) collective-permute-start(f32[8,256]{1,0:T(8,128)S(1)} %get-tuple-element.72), channel_id=1, source_target_pairs={{0,224},{1,225},{2,226},{3,227},{4,228},{5,229},{6,230},{7,231},{8... | collective-permute-start | bytes 24584 | tf_op jit(solution)/shard_map/ppermute | solution.py:402
  44.4 3.0 %collective-permute-start.16 = (f32[128,768]{1,0:T(8,128)S(1)}, f32[128,768]{1,0:T(8,128)S(1)}, u32[]{:S(2)}, u32[]{:S(2)}) collective-permute-start(f32[128,768]{1,0:T(8,128)S(1)} %collective-permute-done.12.be), channel_id=1, source_target_pairs={{0,16},{1,17},{2,18},{3,19},{4,20},{5,21},{6,22},{7,23},{8,24},{9,... | collective-permute-start | bytes 1179656 | tf_op jit(solution)/shard_map/ppermute | solution.py:402
  44.7 5.3 %collective-permute-start.19 = (f32[8,256]{1,0:T(8,128)S(1)}, f32[8,256]{1,0:T(8,128)S(1)}, u32[]{:S(2)}, u32[]{:S(2)}) collective-permute-start(f32[8,256]{1,0:T(8,128)S(1)} %collective-permute-done.13), channel_id=1, source_target_pairs={{0,33},{1,32},{2,35},{3,34},{4,37},{5,36},{6,39},{7,38},{8,41},{9,... | collective-permute-start | bytes 24584 | tf_op jit(solution)/shard_map/ppermute | solution.py:402
  44.7 5.3 %collective-permute-start.18 = (f32[8,256]{1,0:T(8,128)S(1)}, f32[8,256]{1,0:T(8,128)S(1)}, u32[]{:S(2)}, u32[]{:S(2)}) collective-permute-start(f32[8,256]{1,0:T(8,128)S(1)} %collective-permute-done.13), channel_id=1, source_target_pairs={{0,32},{1,33},{2,34},{3,35},{4,36},{5,37},{6,38},{7,39},{8,40},{9,... | collective-permute-start | bytes 24584 | tf_op jit(solution)/shard_map/ppermute | solution.py:402
  46.6 3.4 %collective-permute-start.17 = (f32[8,256]{1,0:T(8,128)S(1)}, f32[8,256]{1,0:T(8,128)S(1)}, u32[]{:S(2)}, u32[]{:S(2)}) collective-permute-start(f32[8,256]{1,0:T(8,128)S(1)} %collective-permute-done.13), channel_id=1, source_target_pairs={{0,1},{1,0},{2,3},{3,2},{4,5},{5,4},{6,7},{7,6},{8,9},{9,8},{10,11... | collective-permute-start | bytes 24584 | tf_op jit(solution)/shard_map/ppermute | solution.py:402
  50.0 2.0 %collective-permute-start.20 = (f32[32,256]{1,0:T(8,128)S(1)}, f32[32,256]{1,0:T(8,128)S(1)}, u32[]{:S(2)}, u32[]{:S(2)}) collective-permute-start(f32[32,256]{1,0:T(8,128)S(1)} %constant_dynamic-update-slice_fusion.mine), channel_id=1, source_target_pairs={{0,16},{1,17},{2,18},{3,19},{4,20},{5,21},{6,22},{7,23},{8,24},{9,... | collective-permute-start | bytes 98312 | tf_op jit(solution)/shard_map/ppermute | solution.py:402
